TPU v7x, 256 devices: a whole 4x4x8 slice. The times are simulated.
256 devices in a mesh: row: 8 (over z_lo, core), col: 32 (over x, z_hi, y).
Axes of the slice: x: 4, y: 4, z: 8 (z_hi: 2, z_lo: 4; z = z_hi * 4 + z_lo), core: 2. Of those that a mesh axis runs over, the one named last changes fastest.
Arguments:
- embedding: bfloat16 [32768, 256], P(('row', 'col')), may hold values from -1.5 to 1.5
- row_blocks: int32 [6144], P(('row', 'col')), may hold values from 0 to 7
- col_blocks: int32 [6144], P(('row', 'col')), may hold values from 0 to 31
- win_counts: bfloat16 [6144, 128, 128], P(('row', 'col')), may hold values from 0 to 2, as said below
- loss_counts: bfloat16 [6144, 128, 128], P(('row', 'col')), may hold values from 0 to 2, as said below
- live_tiles: int32 [256], P(('row', 'col')), may hold values from 1 to 24, as said below
Outputs:
- fitted: float32 [32768, 256], P(('row', 'col'))
Inputs may be any that keep to these rules, and one draw needn't show every extreme that they name: `win_counts`: whole numbers. `loss_counts`: whole numbers. `live_tiles`: one device has all 24 slots live.
All inputs are finite; a program needn't handle non-finite values.
Results may differ from a plain program's by a relative error of at most 0.003.
Values may be sent and summed in bfloat16 or wider, within the bound.
No kernel may reach another device: no remote copies, remote signals or barrier semaphores. Data moves between devices by JAX's collectives and lax.ppermute only.
A program may use at most 64 MiB of HBM per device.

v0:
```python
import jax
import jax.numpy as jnp
from jax import lax
from jax.sharding import PartitionSpec as P

ITERS = 2


def pick_blocks(panels, blocks, count, tile_size):
    shaped = panels.reshape(count, tile_size, panels.shape[1])
    return jnp.take(shaped, blocks, axis=0)


def spread_terms(selector, flat_terms):
    return jnp.dot(
        selector, flat_terms, preferred_element_type=jnp.float32, precision=lax.Precision.HIGHEST
    )


def per_device(embedding, row_blocks, col_blocks, win_counts, loss_counts, live_tiles):
    tile_size = win_counts.shape[1]
    slot_count = win_counts.shape[0]
    width = embedding.shape[1]
    half_width = width // 2
    row_count = lax.axis_size("row")
    col_count = lax.axis_size("col")
    alive = (jnp.arange(slot_count, dtype=jnp.int32) < live_tiles[0]).astype(jnp.float32)
    first_hot = (row_blocks[None, :] == jnp.arange(row_count, dtype=jnp.int32)[:, None]).astype(
        jnp.float32
    ) * alive[None, :]
    second_hot = (col_blocks[None, :] == jnp.arange(col_count, dtype=jnp.int32)[:, None]).astype(
        jnp.float32
    ) * alive[None, :]
    current = embedding
    result = embedding.astype(jnp.float32)
    for iteration in range(ITERS):
        first_panels = lax.all_gather(current, "row", axis=0, tiled=True)
        second_panels = lax.all_gather(current, "col", axis=0, tiled=True)
        left_rows = pick_blocks(first_panels, row_blocks, row_count, tile_size)
        right_rows = pick_blocks(second_panels, col_blocks, col_count, tile_size)
        blade_one, chest_one = (left_rows[..., :half_width], left_rows[..., half_width:])
        blade_two, chest_two = (right_rows[..., :half_width], right_rows[..., half_width:])
        left_side = jnp.concatenate([blade_one, -chest_one], axis=2)
        right_side = jnp.concatenate([chest_two, blade_two], axis=2)
        score = jnp.einsum(
            "sik,sjk->sij", left_side, right_side, preferred_element_type=jnp.float32
        )
        wins_f = win_counts.astype(jnp.float32)
        losses_f = loss_counts.astype(jnp.float32)
        resid = (wins_f - (wins_f + losses_f) * jax.nn.sigmoid(score)).astype(jnp.bfloat16)
        first_grad = jnp.einsum(
            "sij,sjk->sik",
            resid,
            jnp.concatenate([chest_two, -blade_two], axis=2),
            preferred_element_type=jnp.float32,
        )
        second_grad = jnp.einsum(
            "sij,sik->sjk",
            resid,
            jnp.concatenate([-chest_one, blade_one], axis=2),
            preferred_element_type=jnp.float32,
        )
        first_part = spread_terms(
            first_hot, first_grad.reshape(slot_count, tile_size * width)
        ).reshape(row_count * tile_size, width)
        second_flat = second_grad.reshape(slot_count, tile_size * width)
        second_part = spread_terms(second_hot, second_flat).reshape(col_count * tile_size, width)
        second_share = lax.psum_scatter(second_part, "col", scatter_dimension=0, tiled=True)
        first_share = lax.psum_scatter(first_part, "row", scatter_dimension=0, tiled=True)
        result = current.astype(jnp.float32) + 0.01 * (first_share + second_share)
        current = result.astype(jnp.bfloat16)
    return result


def solution(mesh):
    placed = (
        P(("row", "col"), None),
        P(("row", "col")),
        P(("row", "col")),
        P(("row", "col"), None, None),
        P(("row", "col"), None, None),
        P(("row", "col")),
    )
    return jax.shard_map(
        per_device, mesh=mesh, in_specs=placed, out_specs=P(("row", "col"), None), check_vma=False
    )
```

profile of v0, /device:TPU:8, one launch (start us, length us, event | category | flops | bytes accessed | tf_op | source)
XLA Modules:
  0.0 753.1 jit_solution(14991337416674081205)
XLA Ops:
  6.5 0.0 all-gather.3.cloned.1.call-start
  6.5 0.7 all-gather.3.cloned.1.call-update
  7.3 0.0 reduce-scatter.5.cloned.1.call-start
  7.9 0.7 compare_select_fusion.1
  8.6 16.2 %all_gather.12 = bf16[1024,256]{1,0:T(8,128)(2,1)S(1)} all-gather(bf16[128,256]{1,0:T(8,128)(2,1)} %param.10), channel_id=1, replica_groups=mesh['row'=8,'col'=32] {'row'}, dimensions={0}, use_global_device_ids=true | all-gather | bytes 589824 | tf_op jit(solution)/shard_map/all_gather | solution.py:37
  24.8 0.6 gather_fusion
  25.5 0.2 broadcast_select_fusion.3
  25.8 78.7 %all-gather.3.cloned.1.call-done = bf16[4096,256]{1,0:T(8,128)(2,1)} async-done(((bf16[128,256]{1,0:T(8,128)(2,1)}), bf16[4096,256]{1,0:T(8,128)(2,1)}) %all-gather.3.cloned.1.call-update) | async-done | bytes 2097168 | tf_op jit(solution)/shard_map/all_gather | solution.py:38
  104.4 2.2 gather_fusion.1
  106.7 0.2 broadcast_select_fusion.1
  106.9 0.0 copy-start.8
  106.9 0.0 copy-start.10
  106.9 0.4 slice_negate_fusion.3
  107.3 0.7 copy-done.8
  108.0 0.3 copy-done.10
  108.3 0.7 fusion.4
  109.0 0.6 fusion.3
  109.6 0.3 copy-done
  109.9 1.8 copy.11
  111.7 1.6 fusion.40
  113.3 1.2 reshape.56
  114.6 0.0 reduce-scatter.5.cloned.1.call-update
  114.6 0.0 reduce-scatter.7.cloned.1.call-start
  114.7 1.1 copy-done.1
  115.7 0.6 fusion.11
  116.3 1.8 copy.12
  118.2 4.9 fusion.30
  123.1 4.9 reshape.58
  128.0 0.0 reduce-scatter.7.cloned.1.call-update
  128.0 0.0 all-gather.5.cloned.1.call-start
  128.1 19.4 %reduce-scatter.5.cloned.1.call-done = f32[128,256]{1,0:T(8,128)} async-done(((f32[1024,256]{1,0:T(8,128)}), f32[128,256]{1,0:T(8,128)}) %reduce-scatter.5.cloned.1.call-update) | async-done | bytes 131088 | tf_op jit(solution)/shard_map/reduce_scatter | solution.py:69
  147.4 228.7 %reduce-scatter.7.cloned.1.call-done = f32[128,256]{1,0:T(8,128)} async-done(((f32[4096,256]{1,0:T(8,128)}), f32[128,256]{1,0:T(8,128)}) %reduce-scatter.7.cloned.1.call-update) | async-done | bytes 131088 | tf_op jit(solution)/shard_map/reduce_scatter | solution.py:68
  376.1 1.6 add_convert_fusion
  377.7 0.0 all-gather.5.cloned.1.call-update
  377.7 0.0 reduce-scatter.9.cloned.1.call-start
  377.8 16.7 %all_gather.14 = bf16[1024,256]{1,0:T(8,128)(2,1)S(1)} all-gather(bf16[128,256]{1,0:T(8,128)(2,1)} %add_convert_fusion), channel_id=1, replica_groups=mesh['row'=8,'col'=32] {'row'}, dimensions={0}, use_global_device_ids=true | all-gather | bytes 589824 | tf_op jit(solution)/shard_map/all_gather | solution.py:37
  394.5 0.6 gather_fusion.2
  395.1 0.2 broadcast_select_fusion.2
  395.3 0.2 fusion.58
  395.5 77.9 %all-gather.5.cloned.1.call-done = bf16[4096,256]{1,0:T(8,128)(2,1)} async-done(((bf16[128,256]{1,0:T(8,128)(2,1)}), bf16[4096,256]{1,0:T(8,128)(2,1)}) %all-gather.5.cloned.1.call-update) | async-done | bytes 2097168 | tf_op jit(solution)/shard_map/all_gather | solution.py:38
  473.4 2.2 gather_fusion.3
  475.6 0.2 broadcast_select_fusion
  475.9 0.0 copy-start.9
  475.9 0.0 copy-start.11
  475.9 0.2 slice_negate_fusion.2
  476.1 0.9 copy-done.9
  477.0 0.3 copy-done.11
  477.3 0.7 fusion.5
  478.0 0.6 fusion.1
  478.5 0.3 copy-done.2
  478.9 1.8 copy.13
  480.7 1.6 fusion.38
  482.3 1.2 reshape.62
  483.5 0.0 reduce-scatter.9.cloned.1.call-update
  483.6 0.0 reduce-scatter.11.cloned.1.call-start
  483.6 1.1 copy-done.3
  484.7 0.6 fusion.20
  485.3 1.8 copy.14
  487.1 4.9 fusion.28
  492.1 4.9 reshape.64
  496.9 0.0 reduce-scatter.11.cloned.1.call-update
  497.0 19.3 %reduce-scatter.9.cloned.1.call-done = f32[128,256]{1,0:T(8,128)} async-done(((f32[1024,256]{1,0:T(8,128)}), f32[128,256]{1,0:T(8,128)}) %reduce-scatter.9.cloned.1.call-update) | async-done | bytes 131088 | tf_op jit(solution)/shard_map/reduce_scatter | solution.py:69
  516.3 228.3 %reduce-scatter.11.cloned.1.call-done = f32[128,256]{1,0:T(8,128)} async-done(((f32[4096,256]{1,0:T(8,128)}), f32[128,256]{1,0:T(8,128)}) %reduce-scatter.11.cloned.1.call-update) | async-done | bytes 131088 | tf_op jit(solution)/shard_map/reduce_scatter | solution.py:68
  744.7 1.6 multiply_add_fusion
  (18 shorter events, 0.1 us)
Async XLA Ops:
  6.5 97.9 %all-gather.3.cloned.1.call-start = ((), (), s32[]{:S(2)}) async-start(), calls=%async_computation.4 | async-start | bytes 2162688 | tf_op jit(solution)/shard_map/all_gather | solution.py:38
  7.3 140.2 %reduce-scatter.5.cloned.1.call-start = ((), (), s32[]{:S(2)}) async-start(), calls=%async_computation.5 | async-start | bytes 1179648 | tf_op jit(solution)/shard_map/reduce_scatter | solution.py:69
  24.8 0.7 copy-start.7
  24.8 0.7 copy-start.6
  106.9 1.1 copy-start.8
  106.9 1.4 copy-start.10
  109.0 0.9 copy-start
  114.6 1.1 copy-start.1
  114.6 261.5 %reduce-scatter.7.cloned.1.call-start = ((), (), s32[]{:S(2)}) async-start(), calls=%async_computation.6 | async-start | bytes 4325376 | tf_op jit(solution)/shard_map/reduce_scatter | solution.py:68
  128.0 248.1 %copy-start.5 = (bf16[128,256]{1,0:T(8,128)(2,1)S(1)}, bf16[128,256]{1,0:T(8,128)(2,1)}, u32[]{:S(2)}) copy-start(bf16[128,256]{1,0:T(8,128)(2,1)} %param.10) | copy-start | bytes 196612
  128.0 345.4 %all-gather.5.cloned.1.call-start = ((), (), s32[]{:S(2)}) async-start(), calls=%async_computation.7 | async-start | bytes 2162688 | tf_op jit(solution)/shard_map/all_gather | solution.py:38
  377.7 138.6 %reduce-scatter.9.cloned.1.call-start = ((), (), s32[]{:S(2)}) async-start(), calls=%async_computation.8 | async-start | bytes 1179648 | tf_op jit(solution)/shard_map/reduce_scatter | solution.py:69
  475.9 1.1 copy-start.9
  475.9 1.4 copy-start.11
  478.0 0.9 copy-start.2
  483.5 1.1 copy-start.3
  483.6 261.1 %reduce-scatter.11.cloned.1.call-start = ((), (), s32[]{:S(2)}) async-start(), calls=%async_computation.9 | async-start | bytes 4325376 | tf_op jit(solution)/shard_map/reduce_scatter | solution.py:68
  496.9 247.7 %copy-start.4 = (bf16[128,256]{1,0:T(8,128)(2,1)S(1)}, bf16[128,256]{1,0:T(8,128)(2,1)}, u32[]{:S(2)}) copy-start(bf16[128,256]{1,0:T(8,128)(2,1)} %add_convert_fusion) | copy-start | bytes 196612
Sparse Core Ops, SparseCore 0:
  10.9 93.5 all-gather.2
  114.7 32.6 reduce-scatter.4
  150.0 226.0 reduce-scatter.6
  379.5 93.8 all-gather.4
  483.7 32.5 reduce-scatter.8
  518.7 225.9 reduce-scatter.10
where the time goes:
time: 766 us; the launch traced here: 753 us
  waiting for transfers between devices  653 us (85%)
  blocking collectives  32.8 us (4%)
  local copies, waits for them, and re-layouts  30.2 us (4%)
  matrix products  16.9 us (2%)
  between operations  14.4 us (2%)
    reduce_scatter x2, waiting for transfers between devices, per_device(): lax.psum_scatter(second_part, 'col', scatter_dimension=0, tiled=True)  457 us
    all_gather x2, waiting for transfers between devices, per_device(): second_panels = lax.all_gather(current, 'col', axis=0, tiled=True)  157 us
    reduce_scatter x2, waiting for transfers between devices, per_device(): lax.psum_scatter(first_part, 'row', scatter_dimension=0, tiled=True)  38.7 us
    all_gather x2, blocking collectives, per_device(): first_panels = lax.all_gather(current, 'row', axis=0, tiled=True)  32.8 us
  transfers between devices with their start and end apart: 6, of which 6 were waited for; matrix products, arithmetic and copies ran while one was open for 4% of the time, Pallas kernels for 0%

commit v1 on v0

v1 whole, which is shorter than its diff:
```python
import functools
import itertools

import jax
import jax.numpy as jnp
from jax import lax
from jax.experimental import pallas as pl
from jax.experimental.pallas import tpu as pltpu
from jax.sharding import Mesh
from jax.sharding import PartitionSpec as P

ITERS = 2
RATE = 0.01
GROUP = 4
AXES = ("zl", "core", "x", "zh", "y")
SIZES = (4, 2, 4, 2, 4)


def permutation(move):
    pairs = []
    for source, place in enumerate(itertools.product(*[range(size) for size in SIZES])):
        place = move(dict(zip(AXES, place)))
        target = 0
        for axis, size in zip(AXES, SIZES):
            target = target * size + place[axis] % size
        pairs.append((source, target))
    return pairs


def shift(axis, by):
    def move(place):
        place[axis] += by
        return place

    return permutation(move)


def shift_by_core(axes, by):
    def move(place):
        place[axes[place["core"]]] += by
        return place

    return permutation(move)


def send(values, pairs):
    return lax.ppermute(values, AXES, pairs)


def slot_kernel(
    first_ref, second_ref, live_ref,
    u0, u1, u2, u3, v0, v1, v2, v3, wins, losses,
    near, far, d0, d1, d2, d3,
    left, turned, right, first_sum, second_sum,
):
    half = left.shape[2] // 2
    for index, part in enumerate((u0, u1, u2, u3)):
        for core in range(2):
            block = part[core]
            left[2 * index + core] = block
            turned[2 * index + core, :, :half] = -block[:, half:]
            turned[2 * index + core, :, half:] = block[:, :half]
    for index, part in enumerate((v0, v1, v2, v3)):
        right[pl.ds(8 * index, 8)] = part[...]
    first_sum[...] = jnp.zeros_like(first_sum)
    second_sum[...] = jnp.zeros_like(second_sum)
    live = live_ref[0]

    def step(turn, carry):
        work = []
        for member in range(GROUP):
            slot = turn * GROUP + member
            p, q = first_ref[slot], second_ref[slot]
            score = lax.dot_general(
                turned[p], right[q], (((1,), (1,)), ((), ())), preferred_element_type=jnp.float32
            )
            won = wins[slot].astype(jnp.float32)
            lost = losses[slot].astype(jnp.float32)
            resid = won - (won + lost) * jax.nn.sigmoid(score)
            resid = jnp.where(slot < live, resid, 0.0).astype(jnp.bfloat16)
            work.append((p, q, resid))
        grads = []
        for p, q, resid in work:
            first = jnp.dot(resid, right[q], preferred_element_type=jnp.float32)
            second = lax.dot_general(
                resid, left[p], (((0,), (0,)), ((), ())), preferred_element_type=jnp.float32
            )
            grads.append((p, q, first, second))
        for p, q, first, second in grads:
            first_sum[p] += first
            second_sum[q] += second
        return carry

    lax.fori_loop(0, (live + GROUP - 1) // GROUP, step, 0)
    for index in range(4):
        near[index] = first_sum[2 * index]
        far[index] = first_sum[2 * index + 1].astype(jnp.bfloat16)
    d0[...] = second_sum[pl.ds(0, 8)]
    for index, out in enumerate((d1, d2, d3)):
        out[...] = second_sum[pl.ds(8 * (index + 1), 8)].astype(jnp.bfloat16)


def slot_grads(first_place, second_place, live, left_parts, right_parts, wins, losses):
    tile, width = left_parts[0].shape[1:]
    smem = pl.BlockSpec(memory_space=pltpu.SMEM)
    vmem = pl.BlockSpec(memory_space=pltpu.VMEM)

    def blocks(count, dtype):
        return jax.ShapeDtypeStruct((count, tile, width), dtype)

    return pl.pallas_call(
        slot_kernel,
        out_shape=(
            blocks(4, jnp.float32), blocks(4, jnp.bfloat16),
            blocks(8, jnp.float32), blocks(8, jnp.bfloat16), blocks(8, jnp.bfloat16), blocks(8, jnp.bfloat16),
        ),
        in_specs=[smem] * 3 + [vmem] * 10,
        out_specs=[vmem] * 6,
        scratch_shapes=[
            pltpu.VMEM((8, tile, width), jnp.bfloat16),
            pltpu.VMEM((8, tile, width), jnp.bfloat16),
            pltpu.VMEM((32, tile, width), jnp.bfloat16),
            pltpu.VMEM((8, tile, width), jnp.float32),
            pltpu.VMEM((32, tile, width), jnp.float32),
        ],
        compiler_params=pltpu.CompilerParams(vmem_limit_bytes=40 * 1024 * 1024),
    )(first_place, second_place, live, *left_parts, *right_parts, wins, losses)


def per_device(embedding, row_blocks, col_blocks, win_counts, loss_counts, live_tiles):
    at = {axis: lax.axis_index(axis) for axis in AXES}
    half = embedding.shape[1] // 2
    first_place = ((row_blocks // 2 - at["zl"]) % 4) * 2 + (row_blocks + at["core"]) % 2
    far_x = (col_blocks // 8 - at["x"]) % 4
    far_y = (col_blocks - at["y"]) % 4
    far_z = (col_blocks // 4 + at["zh"]) % 2
    outer = jnp.where(at["core"] == 0, far_y, far_x)
    inner = jnp.where(at["core"] == 0, far_x, far_y)
    second_place = (outer * 4 + inner) * 2 + far_z
    inner_axes, outer_axes = ("x", "y"), ("y", "x")

    current = embedding
    result = embedding.astype(jnp.float32)
    for iteration in range(ITERS):
        pair = jnp.stack([current, send(current, shift("zh", 1))])
        cores = jnp.stack([current, send(current, shift("core", 1))])
        inner_parts = [pair] + [send(pair, shift_by_core(inner_axes, -k)) for k in (1, 2, 3)]
        left_parts = [cores] + [send(cores, shift("zl", -k)) for k in (1, 2, 3)]
        line = jnp.concatenate(inner_parts)
        right_parts = [line] + [send(line, shift_by_core(outer_axes, -k)) for k in (1, 2, 3)]
        near, far, *second = slot_grads(
            first_place, second_place, live_tiles, left_parts, right_parts, win_counts, loss_counts
        )
        came = [send(second[k], shift_by_core(outer_axes, k)) for k in (1, 2, 3)]
        far = send(far, shift("core", 1))
        line_sum = second[0] + sum(part.astype(jnp.float32) for part in came)
        near = near + far.astype(jnp.float32)
        near_out = near.astype(jnp.bfloat16)
        line_out = line_sum.astype(jnp.bfloat16)
        came = [send(line_out[2 * k : 2 * k + 2], shift_by_core(inner_axes, k)) for k in (1, 2, 3)]
        near_came = [send(near_out[k], shift("zl", k)) for k in (1, 2, 3)]
        pair_sum = line_sum[:2] + sum(part.astype(jnp.float32) for part in came)
        partner = send(pair_sum[1].astype(jnp.bfloat16), shift("zh", 1))
        first_share = near[0] + sum(part.astype(jnp.float32) for part in near_came)
        raw = first_share - (pair_sum[0] + partner.astype(jnp.float32))
        grad = jnp.concatenate([raw[:, half:], -raw[:, :half]], axis=1)
        result = current.astype(jnp.float32) + RATE * grad
        current = result.astype(jnp.bfloat16)
    return result


def solution(mesh):
    fine = Mesh(mesh.devices.reshape(SIZES), AXES)
    rows = P(AXES)
    return jax.shard_map(
        per_device, mesh=fine, in_specs=(rows,) * 6, out_specs=rows, check_vma=False
    )
```

time: 766 us -> 160 us (0.21); the launches traced: 753 us -> 159 us
  waiting for transfers between devices: 653 us -> 53.5 us
  starting transfers between devices: 0.21 us -> 95.4 us
  blocking collectives: 32.8 us -> 0 us
  local copies, waits for them, and re-layouts: 30.2 us -> 2.2 us
  matrix products: 16.9 us -> 0 us
  between operations: 14.4 us -> 0.97 us
    reduce_scatter x4 -> x0, waiting for transfers between devices: 496 us -> none  [the longest x2 457 us: per_device(): lax.psum_scatter(second_part, 'col', scatter_dimension=0, tiled=True)]
    all_gather x2 -> x0, waiting for transfers between devices: 157 us -> none  [per_device(): second_panels = lax.all_gather(current, 'col', axis=0, tiled=True)]
    ppermute x0 -> x44, starting transfers between devices: none -> 95.4 us  [send(): return lax.ppermute(values, AXES, pairs)]
    ppermute x0 -> x44, waiting for transfers between devices: none -> 53.5 us  [send(): return lax.ppermute(values, AXES, pairs)]
    all_gather x2 -> x0, blocking collectives: 32.8 us -> none  [per_device(): first_panels = lax.all_gather(current, 'row', axis=0, tiled=True)]
    dot_general x10 -> x0, matrix products: 16.9 us -> none  [the longest x4 13.1 us: spread_terms(): jnp.dot(selector, flat_terms, preferred_element_type=jnp.float32, precisi...]
    reshape x4 -> x0, local copies, waits for them, and re-layouts: 12.2 us -> none  [the longest x2 9.77 us: per_device(): spread_terms(second_hot, second_flat).reshape(col_count * tile_size, width)]
    unnamed x28 -> x19, local copies, waits for them, and re-layouts: 12.2 us -> 2.08 us
  transfers between devices with their start and end apart: 6 -> 44, of which waited for: 6 -> 19; matrix products, arithmetic and copies ran while one was open for 4% -> 1% of each run, Pallas kernels for 0% -> 0%
where the time goes in v1:
time: 160 us; the launch traced here: 159 us
  starting transfers between devices  95.4 us (60%)
  waiting for transfers between devices  53.5 us (33%)
  Pallas kernels  4.8 us (3%)
  local copies, waits for them, and re-layouts  2.2 us (1%)
  other arithmetic  1.8 us (1%)
    ppermute x44, starting transfers between devices, send(): return lax.ppermute(values, AXES, pairs)  95.4 us
    ppermute x44, waiting for transfers between devices, send(): return lax.ppermute(values, AXES, pairs)  53.5 us
    pallas_call x2, Pallas kernels, slot_grads(): pl.pallas_call(slot_kernel, out_shape=(blocks(4, jnp.float32), blocks(4,...  4.8 us
  transfers between devices with their start and end apart: 44, of which 19 were waited for; matrix products, arithmetic and copies ran while one was open for 1% of the time, Pallas kernels for 0%

profile of v1, /device:TPU:8, one launch (start us, length us, event | category | flops | bytes accessed | tf_op | source)
XLA Modules:
  0.0 158.7 jit_solution(15658727399666073140)
XLA Ops:
  0.0 7.2 %collective-permute-start.4 = (bf16[128,256]{1,0:T(8,128)(2,1)}, bf16[128,256]{1,0:T(8,128)(2,1)S(1)}, u32[]{:S(2)}, u32[]{:S(2)}) collective-permute-start(bf16[128,256]{1,0:T(8,128)(2,1)} %param.6), channel_id=1, source_target_pairs={{0,4},{1,5},{2,6},{3,7},{4,0},{5,1},{6,2},{7,3},{8,12},{9,13},{10,... | collective-permute-start | bytes 196616 | tf_op jit(solution)/shard_map/ppermute | solution.py:47
  7.2 0.9 constant_dynamic-update-slice_fusion.4
  8.1 1.8 %collective-permute-done.4 = bf16[128,256]{1,0:T(8,128)(2,1)S(1)} collective-permute-done((bf16[128,256]{1,0:T(8,128)(2,1)}, bf16[128,256]{1,0:T(8,128)(2,1)S(1)}, u32[]{:S(2)}, u32[]{:S(2)}) %collective-permute-start.4) | collective-permute-done | bytes 65568 | tf_op jit(solution)/shard_map/ppermute | solution.py:47
  9.9 1.6 collective-permute-start.7
  11.5 2.7 %collective-permute-start.6 = (bf16[2,128,256]{2,1,0:T(8,128)(2,1)S(1)}, bf16[2,128,256]{2,1,0:T(8,128)(2,1)S(1)}, u32[]{:S(2)}, u32[]{:S(2)}) collective-permute-start(bf16[2,128,256]{2,1,0:T(8,128)(2,1)S(1)} %get-tuple-element.57), channel_id=1, source_target_pairs={{0,16},{1,17},{2,18},{3,19},{4,20},{5,21},{6,22},{7,23},{8,24},{9,... | collective-permute-start | bytes 393224 | tf_op jit(solution)/shard_map/ppermute | solution.py:47
  14.2 1.4 collective-permute-start.5
  15.6 3.5 %collective-permute-done.5 = bf16[2,128,256]{2,1,0:T(8,128)(2,1)S(1)} collective-permute-done((bf16[2,128,256]{2,1,0:T(8,128)(2,1)S(1)}, bf16[2,128,256]{2,1,0:T(8,128)(2,1)S(1)}, u32[]{:S(2)}, u32[]{:S(2)}) %collective-permute-start.5) | collective-permute-done | bytes 131104 | tf_op jit(solution)/shard_map/ppermute | solution.py:47
  19.2 1.7 %collective-permute-start.10 = (bf16[8,128,256]{2,1,0:T(8,128)(2,1)S(1)}, bf16[8,128,256]{2,1,0:T(8,128)(2,1)S(1)}, u32[]{:S(2)}, u32[]{:S(2)}) collective-permute-start(bf16[8,128,256]{2,1,0:T(8,128)(2,1)S(1)} %constant_dynamic-update-slice_fusion.v0), channel_id=1, source_target_pairs={{0,1},{1,2},{2,3},{3,0},{4,5},{5,6},{6,7},{7,4},{8,9},{9,10},{10,1... | collective-permute-start | bytes 1572872 | tf_op jit(solution)/shard_map/ppermute | solution.py:47
  20.9 0.9 collective-permute-start.9
  21.8 2.4 %collective-permute-start.8 = (bf16[8,128,256]{2,1,0:T(8,128)(2,1)S(1)}, bf16[8,128,256]{2,1,0:T(8,128)(2,1)S(1)}, u32[]{:S(2)}, u32[]{:S(2)}) collective-permute-start(bf16[8,128,256]{2,1,0:T(8,128)(2,1)S(1)} %constant_dynamic-update-slice_fusion.v0), channel_id=1, source_target_pairs={{0,3},{1,0},{2,1},{3,2},{4,7},{5,4},{6,5},{7,6},{8,11},{9,8},{10,9... | collective-permute-start | bytes 1572872 | tf_op jit(solution)/shard_map/ppermute | solution.py:47
  24.3 1.9 %collective-permute-start.3 = (bf16[2,128,256]{2,1,0:T(8,128)(2,1)S(1)}, bf16[2,128,256]{2,1,0:T(8,128)(2,1)S(1)}, u32[]{:S(2)}, u32[]{:S(2)}) collective-permute-start(bf16[2,128,256]{2,1,0:T(8,128)(2,1)S(1)} %get-tuple-element.58.u0), channel_id=1, source_target_pairs={{0,64},{1,65},{2,66},{3,67},{4,68},{5,69},{6,70},{7,71},{8,72},{9,... | collective-permute-start | bytes 393224 | tf_op jit(solution)/shard_map/ppermute | solution.py:47
  26.8 1.9 %collective-permute-start.2 = (bf16[2,128,256]{2,1,0:T(8,128)(2,1)S(1)}, bf16[2,128,256]{2,1,0:T(8,128)(2,1)S(1)}, u32[]{:S(2)}, u32[]{:S(2)}) collective-permute-start(bf16[2,128,256]{2,1,0:T(8,128)(2,1)S(1)} %get-tuple-element.58.u0), channel_id=1, source_target_pairs={{0,128},{1,129},{2,130},{3,131},{4,132},{5,133},{6,134},{7,135},{8... | collective-permute-start | bytes 393224 | tf_op jit(solution)/shard_map/ppermute | solution.py:47
  28.7 3.2 %collective-permute-done.3.u3 = bf16[2,128,256]{2,1,0:T(8,128)(2,1)S(1)} collective-permute-done((bf16[2,128,256]{2,1,0:T(8,128)(2,1)S(1)}, bf16[2,128,256]{2,1,0:T(8,128)(2,1)S(1)}, u32[]{:S(2)}, u32[]{:S(2)}) %collective-permute-start.3) | collective-permute-done | bytes 131104 | tf_op jit(solution)/shard_map/ppermute | solution.py:47
  31.9 2.9 %collective-permute-start.1 = (bf16[2,128,256]{2,1,0:T(8,128)(2,1)S(1)}, bf16[2,128,256]{2,1,0:T(8,128)(2,1)S(1)}, u32[]{:S(2)}, u32[]{:S(2)}) collective-permute-start(bf16[2,128,256]{2,1,0:T(8,128)(2,1)S(1)} %get-tuple-element.58.u0), channel_id=1, source_target_pairs={{0,192},{1,193},{2,194},{3,195},{4,196},{5,197},{6,198},{7,199},{8... | collective-permute-start | bytes 393224 | tf_op jit(solution)/shard_map/ppermute | solution.py:47
  34.9 0.9 collective-permute-done.2.u2
  35.8 1.6 %collective-permute-done.1.u1 = bf16[2,128,256]{2,1,0:T(8,128)(2,1)S(1)} collective-permute-done((bf16[2,128,256]{2,1,0:T(8,128)(2,1)S(1)}, bf16[2,128,256]{2,1,0:T(8,128)(2,1)S(1)}, u32[]{:S(2)}, u32[]{:S(2)}) %collective-permute-start.1) | collective-permute-done | bytes 131104 | tf_op jit(solution)/shard_map/ppermute | solution.py:47
  37.4 1.1 copy-done.1
  38.5 2.4 %shard_map.64 = (f32[4,128,256]{2,1,0:T(8,128)S(1)}, bf16[4,128,256]{2,1,0:T(8,128)(2,1)S(1)}, f32[8,128,256]{2,1,0:T(8,128)S(1)}, bf16[8,128,256]{2,1,0:T(8,128...) custom-call(s32[24]{0:T(128)S(1)} %get-tuple-element.59.first_ref, ...), custom_call_target="tpu_custom_call" | custom-call | tf_op jit(solution)/shard_map/pallas_call | solution.py:111
  41.0 1.0 collective-permute-start.15
  42.0 2.6 %collective-permute-start.16 = (bf16[8,128,256]{2,1,0:T(8,128)(2,1)S(1)}, bf16[8,128,256]{2,1,0:T(8,128)(2,1)S(1)}, u32[]{:S(2)}, u32[]{:S(2)}) collective-permute-start(bf16[8,128,256]{2,1,0:T(8,128)(2,1)S(1)} %get-tuple-element.21), channel_id=1, source_target_pairs={{0,2},{1,3},{2,0},{3,1},{4,6},{5,7},{6,4},{7,5},{8,10},{9,11},{10,... | collective-permute-start | bytes 1572872 | tf_op jit(solution)/shard_map/ppermute | solution.py:47
  44.6 0.7 collective-permute-start.17
  45.4 4.9 %collective-permute-done.15 = bf16[8,128,256]{2,1,0:T(8,128)(2,1)S(1)} collective-permute-done((bf16[8,128,256]{2,1,0:T(8,128)(2,1)S(1)}, bf16[8,128,256]{2,1,0:T(8,128)(2,1)S(1)}, u32[]{:S(2)}, u32[]{:S(2)}) %collective-permute-start.15) | collective-permute-done | bytes 524320 | tf_op jit(solution)/shard_map/ppermute | solution.py:47
  50.3 2.5 %collective-permute-done.16 = bf16[8,128,256]{2,1,0:T(8,128)(2,1)S(1)} collective-permute-done((bf16[8,128,256]{2,1,0:T(8,128)(2,1)S(1)}, bf16[8,128,256]{2,1,0:T(8,128)(2,1)S(1)}, u32[]{:S(2)}, u32[]{:S(2)}) %collective-permute-start.16) | collective-permute-done | bytes 524320 | tf_op jit(solution)/shard_map/ppermute | solution.py:47
  52.8 5.5 %collective-permute-done.17 = bf16[8,128,256]{2,1,0:T(8,128)(2,1)S(1)} collective-permute-done((bf16[8,128,256]{2,1,0:T(8,128)(2,1)S(1)}, bf16[8,128,256]{2,1,0:T(8,128)(2,1)S(1)}, u32[]{:S(2)}, u32[]{:S(2)}) %collective-permute-start.17) | collective-permute-done | bytes 524320 | tf_op jit(solution)/shard_map/ppermute | solution.py:47
  58.3 0.3 fusion.25
  58.7 1.0 collective-permute-start.18
  59.7 2.5 %collective-permute-start.20 = (bf16[2,128,256]{2,1,0:T(8,128)(2,1)S(1)}, bf16[2,128,256]{2,1,0:T(8,128)(2,1)S(1)}, u32[]{:S(2)}, u32[]{:S(2)}) collective-permute-start(bf16[2,128,256]{2,1,0:T(8,128)(2,1)S(1)} %get-tuple-element.43), channel_id=1, source_target_pairs={{0,24},{1,25},{2,26},{3,27},{4,28},{5,29},{6,30},{7,31},{8,0},{9,1... | collective-permute-start | bytes 393224 | tf_op jit(solution)/shard_map/ppermute | solution.py:47
  62.2 1.1 collective-permute-start.19
  63.3 1.7 %collective-permute-start.12 = (bf16[128,256]{1,0:T(8,128)(2,1)S(1)}, bf16[128,256]{1,0:T(8,128)(2,1)S(1)}, u32[]{:S(2)}, u32[]{:S(2)}) collective-permute-start(bf16[128,256]{1,0:T(8,128)(2,1)S(1)} %get-tuple-element.48), channel_id=1, source_target_pairs={{0,64},{1,65},{2,66},{3,67},{4,68},{5,69},{6,70},{7,71},{8,72},{9,... | collective-permute-start | bytes 196616 | tf_op jit(solution)/shard_map/ppermute | solution.py:47
  65.0 2.2 %collective-permute-start.14 = (bf16[128,256]{1,0:T(8,128)(2,1)S(1)}, bf16[128,256]{1,0:T(8,128)(2,1)S(1)}, u32[]{:S(2)}, u32[]{:S(2)}) collective-permute-start(bf16[128,256]{1,0:T(8,128)(2,1)S(1)} %get-tuple-element.49), channel_id=1, source_target_pairs={{0,192},{1,193},{2,194},{3,195},{4,196},{5,197},{6,198},{7,199},{8... | collective-permute-start | bytes 196616 | tf_op jit(solution)/shard_map/ppermute | solution.py:47
  67.2 1.5 collective-permute-start.13
  68.9 5.7 %collective-permute-start.21 = (bf16[128,256]{1,0:T(8,128)(2,1)S(1)}, bf16[128,256]{1,0:T(8,128)(2,1)S(1)}, u32[]{:S(2)}, u32[]{:S(2)}) collective-permute-start(bf16[128,256]{1,0:T(8,128)(2,1)S(1)} %fusion.9), channel_id=1, source_target_pairs={{0,4},{1,5},{2,6},{3,7},{4,0},{5,1},{6,2},{7,3},{8,12},{9,13},{10,... | collective-permute-start | bytes 196616 | tf_op jit(solution)/shard_map/ppermute | solution.py:47
  74.6 2.6 %collective-permute-done.21 = bf16[128,256]{1,0:T(8,128)(2,1)S(1)} collective-permute-done((bf16[128,256]{1,0:T(8,128)(2,1)S(1)}, bf16[128,256]{1,0:T(8,128)(2,1)S(1)}, u32[]{:S(2)}, u32[]{:S(2)}) %collective-permute-start.21) | collective-permute-done | bytes 65568 | tf_op jit(solution)/shard_map/ppermute | solution.py:47
  77.3 5.7 %collective-permute-start.26 = (bf16[128,256]{1,0:T(8,128)(2,1)S(1)}, bf16[128,256]{1,0:T(8,128)(2,1)S(1)}, u32[]{:S(2)}, u32[]{:S(2)}) collective-permute-start(bf16[128,256]{1,0:T(8,128)(2,1)S(1)} %get-tuple-element.34), channel_id=1, source_target_pairs={{0,4},{1,5},{2,6},{3,7},{4,0},{5,1},{6,2},{7,3},{8,12},{9,13},{10,... | collective-permute-start | bytes 196616 | tf_op jit(solution)/shard_map/ppermute | solution.py:47
  83.0 2.6 %collective-permute-done.26 = bf16[128,256]{1,0:T(8,128)(2,1)S(1)} collective-permute-done((bf16[128,256]{1,0:T(8,128)(2,1)S(1)}, bf16[128,256]{1,0:T(8,128)(2,1)S(1)}, u32[]{:S(2)}, u32[]{:S(2)}) %collective-permute-start.26) | collective-permute-done | bytes 65568 | tf_op jit(solution)/shard_map/ppermute | solution.py:47
  85.6 1.0 collective-permute-start.29
  86.6 2.3 %collective-permute-start.28 = (bf16[2,128,256]{2,1,0:T(8,128)(2,1)S(1)}, bf16[2,128,256]{2,1,0:T(8,128)(2,1)S(1)}, u32[]{:S(2)}, u32[]{:S(2)}) collective-permute-start(bf16[2,128,256]{2,1,0:T(8,128)(2,1)S(1)} %get-tuple-element.55), channel_id=1, source_target_pairs={{0,16},{1,17},{2,18},{3,19},{4,20},{5,21},{6,22},{7,23},{8,24},{9,... | collective-permute-start | bytes 393224 | tf_op jit(solution)/shard_map/ppermute | solution.py:47
  88.9 2.5 %collective-permute-start.27 = (bf16[2,128,256]{2,1,0:T(8,128)(2,1)S(1)}, bf16[2,128,256]{2,1,0:T(8,128)(2,1)S(1)}, u32[]{:S(2)}, u32[]{:S(2)}) collective-permute-start(bf16[2,128,256]{2,1,0:T(8,128)(2,1)S(1)} %get-tuple-element.55), channel_id=1, source_target_pairs={{0,24},{1,25},{2,26},{3,27},{4,28},{5,29},{6,30},{7,31},{8,0},{9,1... | collective-permute-start | bytes 393224 | tf_op jit(solution)/shard_map/ppermute | solution.py:47
  91.4 2.7 %collective-permute-done.27 = bf16[2,128,256]{2,1,0:T(8,128)(2,1)S(1)} collective-permute-done((bf16[2,128,256]{2,1,0:T(8,128)(2,1)S(1)}, bf16[2,128,256]{2,1,0:T(8,128)(2,1)S(1)}, u32[]{:S(2)}, u32[]{:S(2)}) %collective-permute-start.27) | collective-permute-done | bytes 131104 | tf_op jit(solution)/shard_map/ppermute | solution.py:47
  94.2 1.3 collective-permute-start.32
  95.5 2.1 %collective-permute-start.31 = (bf16[8,128,256]{2,1,0:T(8,128)(2,1)S(1)}, bf16[8,128,256]{2,1,0:T(8,128)(2,1)S(1)}, u32[]{:S(2)}, u32[]{:S(2)}) collective-permute-start(bf16[8,128,256]{2,1,0:T(8,128)(2,1)S(1)} %constant_dynamic-update-slice_fusion.5.v0), channel_id=1, source_target_pairs={{0,2},{1,3},{2,0},{3,1},{4,6},{5,7},{6,4},{7,5},{8,10},{9,11},{10,... | collective-permute-start | bytes 1572872 | tf_op jit(solution)/shard_map/ppermute | solution.py:47
  97.6 2.5 %collective-permute-start.30 = (bf16[8,128,256]{2,1,0:T(8,128)(2,1)S(1)}, bf16[8,128,256]{2,1,0:T(8,128)(2,1)S(1)}, u32[]{:S(2)}, u32[]{:S(2)}) collective-permute-start(bf16[8,128,256]{2,1,0:T(8,128)(2,1)S(1)} %constant_dynamic-update-slice_fusion.5.v0), channel_id=1, source_target_pairs={{0,3},{1,0},{2,1},{3,2},{4,7},{5,4},{6,5},{7,6},{8,11},{9,8},{10,9... | collective-permute-start | bytes 1572872 | tf_op jit(solution)/shard_map/ppermute | solution.py:47
  100.1 1.3 collective-permute-start.25
  101.4 2.7 %collective-permute-start.24 = (bf16[2,128,256]{2,1,0:T(8,128)(2,1)S(1)}, bf16[2,128,256]{2,1,0:T(8,128)(2,1)S(1)}, u32[]{:S(2)}, u32[]{:S(2)}) collective-permute-start(bf16[2,128,256]{2,1,0:T(8,128)(2,1)S(1)} %get-tuple-element.56.u0), channel_id=1, source_target_pairs={{0,128},{1,129},{2,130},{3,131},{4,132},{5,133},{6,134},{7,135},{8... | collective-permute-start | bytes 393224 | tf_op jit(solution)/shard_map/ppermute | solution.py:47
  104.1 3.1 %collective-permute-done.25.u3 = bf16[2,128,256]{2,1,0:T(8,128)(2,1)S(1)} collective-permute-done((bf16[2,128,256]{2,1,0:T(8,128)(2,1)S(1)}, bf16[2,128,256]{2,1,0:T(8,128)(2,1)S(1)}, u32[]{:S(2)}, u32[]{:S(2)}) %collective-permute-start.25) | collective-permute-done | bytes 131104 | tf_op jit(solution)/shard_map/ppermute | solution.py:47
  107.3 2.6 %collective-permute-start.23 = (bf16[2,128,256]{2,1,0:T(8,128)(2,1)S(1)}, bf16[2,128,256]{2,1,0:T(8,128)(2,1)S(1)}, u32[]{:S(2)}, u32[]{:S(2)}) collective-permute-start(bf16[2,128,256]{2,1,0:T(8,128)(2,1)S(1)} %get-tuple-element.56.u0), channel_id=1, source_target_pairs={{0,192},{1,193},{2,194},{3,195},{4,196},{5,197},{6,198},{7,199},{8... | collective-permute-start | bytes 393224 | tf_op jit(solution)/shard_map/ppermute | solution.py:47
  109.8 0.7 collective-permute-done.24.u2
  110.5 1.8 %collective-permute-done.23.u1 = bf16[2,128,256]{2,1,0:T(8,128)(2,1)S(1)} collective-permute-done((bf16[2,128,256]{2,1,0:T(8,128)(2,1)S(1)}, bf16[2,128,256]{2,1,0:T(8,128)(2,1)S(1)}, u32[]{:S(2)}, u32[]{:S(2)}) %collective-permute-start.23) | collective-permute-done | bytes 131104 | tf_op jit(solution)/shard_map/ppermute | solution.py:47
  112.4 2.4 %shard_map.65 = (f32[4,128,256]{2,1,0:T(8,128)S(1)}, bf16[4,128,256]{2,1,0:T(8,128)(2,1)S(1)}, f32[8,128,256]{2,1,0:T(8,128)S(1)}, bf16[8,128,256]{2,1,0:T(8,128...) custom-call(s32[24]{0:T(128)S(1)} %get-tuple-element.59.first_ref, ...), custom_call_target="tpu_custom_call" | custom-call | tf_op jit(solution)/shard_map/pallas_call | solution.py:111
  114.9 0.8 collective-permute-start.37
  115.8 2.3 %collective-permute-start.38 = (bf16[8,128,256]{2,1,0:T(8,128)(2,1)S(1)}, bf16[8,128,256]{2,1,0:T(8,128)(2,1)S(1)}, u32[]{:S(2)}, u32[]{:S(2)}) collective-permute-start(bf16[8,128,256]{2,1,0:T(8,128)(2,1)S(1)} %get-tuple-element.27), channel_id=1, source_target_pairs={{0,2},{1,3},{2,0},{3,1},{4,6},{5,7},{6,4},{7,5},{8,10},{9,11},{10,... | collective-permute-start | bytes 1572872 | tf_op jit(solution)/shard_map/ppermute | solution.py:47
  118.1 1.5 collective-permute-start.39
  119.7 4.5 %collective-permute-done.37 = bf16[8,128,256]{2,1,0:T(8,128)(2,1)S(1)} collective-permute-done((bf16[8,128,256]{2,1,0:T(8,128)(2,1)S(1)}, bf16[8,128,256]{2,1,0:T(8,128)(2,1)S(1)}, u32[]{:S(2)}, u32[]{:S(2)}) %collective-permute-start.37) | collective-permute-done | bytes 524320 | tf_op jit(solution)/shard_map/ppermute | solution.py:47
  124.2 2.4 %collective-permute-done.38 = bf16[8,128,256]{2,1,0:T(8,128)(2,1)S(1)} collective-permute-done((bf16[8,128,256]{2,1,0:T(8,128)(2,1)S(1)}, bf16[8,128,256]{2,1,0:T(8,128)(2,1)S(1)}, u32[]{:S(2)}, u32[]{:S(2)}) %collective-permute-start.38) | collective-permute-done | bytes 524320 | tf_op jit(solution)/shard_map/ppermute | solution.py:47
  126.5 5.5 %collective-permute-done.39 = bf16[8,128,256]{2,1,0:T(8,128)(2,1)S(1)} collective-permute-done((bf16[8,128,256]{2,1,0:T(8,128)(2,1)S(1)}, bf16[8,128,256]{2,1,0:T(8,128)(2,1)S(1)}, u32[]{:S(2)}, u32[]{:S(2)}) %collective-permute-start.39) | collective-permute-done | bytes 524320 | tf_op jit(solution)/shard_map/ppermute | solution.py:47
  132.4 1.1 collective-permute-start.40
  133.5 2.2 %collective-permute-start.42 = (bf16[2,128,256]{2,1,0:T(8,128)(2,1)S(1)}, bf16[2,128,256]{2,1,0:T(8,128)(2,1)S(1)}, u32[]{:S(2)}, u32[]{:S(2)}) collective-permute-start(bf16[2,128,256]{2,1,0:T(8,128)(2,1)S(1)} %get-tuple-element.40), channel_id=1, source_target_pairs={{0,24},{1,25},{2,26},{3,27},{4,28},{5,29},{6,30},{7,31},{8,0},{9,1... | collective-permute-start | bytes 393224 | tf_op jit(solution)/shard_map/ppermute | solution.py:47
  135.7 1.6 collective-permute-start.41
  137.3 2.3 %collective-permute-start.34 = (bf16[128,256]{1,0:T(8,128)(2,1)S(1)}, bf16[128,256]{1,0:T(8,128)(2,1)S(1)}, u32[]{:S(2)}, u32[]{:S(2)}) collective-permute-start(bf16[128,256]{1,0:T(8,128)(2,1)S(1)} %get-tuple-element.45), channel_id=1, source_target_pairs={{0,64},{1,65},{2,66},{3,67},{4,68},{5,69},{6,70},{7,71},{8,72},{9,... | collective-permute-start | bytes 196616 | tf_op jit(solution)/shard_map/ppermute | solution.py:47
  139.6 1.6 collective-permute-start.36
  141.2 0.9 collective-permute-start.35
  142.3 12.1 %collective-permute-start.43 = (bf16[128,256]{1,0:T(8,128)(2,1)S(1)}, bf16[128,256]{1,0:T(8,128)(2,1)S(1)}, u32[]{:S(2)}, u32[]{:S(2)}) collective-permute-start(bf16[128,256]{1,0:T(8,128)(2,1)S(1)} %fusion.10), channel_id=1, source_target_pairs={{0,4},{1,5},{2,6},{3,7},{4,0},{5,1},{6,2},{7,3},{8,12},{9,13},{10,... | collective-permute-start | bytes 196616 | tf_op jit(solution)/shard_map/ppermute | solution.py:47
  154.4 3.5 %collective-permute-done.43 = bf16[128,256]{1,0:T(8,128)(2,1)S(1)} collective-permute-done((bf16[128,256]{1,0:T(8,128)(2,1)S(1)}, bf16[128,256]{1,0:T(8,128)(2,1)S(1)}, u32[]{:S(2)}, u32[]{:S(2)}) %collective-permute-start.43) | collective-permute-done | bytes 65568 | tf_op jit(solution)/shard_map/ppermute | solution.py:47
  158.0 0.7 fusion.8
  (68 shorter events, 1.4 us)
Async XLA Ops:
  0.0 9.9 %copy-start.3 = (bf16[128,256]{1,0:T(8,128)(2,1)S(1)}, bf16[128,256]{1,0:T(8,128)(2,1)}, u32[]{:S(2)}) copy-start(bf16[128,256]{1,0:T(8,128)(2,1)} %param.6) | copy-start | bytes 196612
  0.0 37.4 %copy-start = (bf16[24,128,128]{2,1,0:T(8,128)(2,1)S(1)}, bf16[24,128,128]{2,1,0:T(8,128)(2,1)}, u32[]{:S(2)}) copy-start(bf16[24,128,128]{2,1,0:T(8,128)(2,1)} %wins.3) | copy-start | bytes 2359300
  0.0 9.9 %collective-permute-start.4 = (bf16[128,256]{1,0:T(8,128)(2,1)}, bf16[128,256]{1,0:T(8,128)(2,1)S(1)}, u32[]{:S(2)}, u32[]{:S(2)}) collective-permute-start(bf16[128,256]{1,0:T(8,128)(2,1)} %param.6), channel_id=1, source_target_pairs={{0,4},{1,5},{2,6},{3,7},{4,0},{5,1},{6,2},{7,3},{8,12},{9,13},{10,... | collective-permute-start | bytes 196616 | tf_op jit(solution)/shard_map/ppermute | solution.py:47
  7.2 2.7 %collective-permute-start = (bf16[128,256]{1,0:T(8,128)(2,1)}, bf16[128,256]{1,0:T(8,128)(2,1)S(1)}, u32[]{:S(2)}, u32[]{:S(2)}) collective-permute-start(bf16[128,256]{1,0:T(8,128)(2,1)} %param.6), channel_id=1, source_target_pairs={{0,32},{1,33},{2,34},{3,35},{4,36},{5,37},{6,38},{7,39},{8,40},{9,... | collective-permute-start | bytes 196616 | tf_op jit(solution)/shard_map/ppermute | solution.py:47
  9.9 9.3 %collective-permute-start.7 = (bf16[2,128,256]{2,1,0:T(8,128)(2,1)S(1)}, bf16[2,128,256]{2,1,0:T(8,128)(2,1)S(1)}, u32[]{:S(2)}, u32[]{:S(2)}) collective-permute-start(bf16[2,128,256]{2,1,0:T(8,128)(2,1)S(1)} %get-tuple-element.57), channel_id=1, source_target_pairs={{0,8},{1,9},{2,10},{3,11},{4,12},{5,13},{6,14},{7,15},{8,16},{9,17... | collective-permute-start | bytes 393224 | tf_op jit(solution)/shard_map/ppermute | solution.py:47
  11.5 7.7 %collective-permute-start.6 = (bf16[2,128,256]{2,1,0:T(8,128)(2,1)S(1)}, bf16[2,128,256]{2,1,0:T(8,128)(2,1)S(1)}, u32[]{:S(2)}, u32[]{:S(2)}) collective-permute-start(bf16[2,128,256]{2,1,0:T(8,128)(2,1)S(1)} %get-tuple-element.57), channel_id=1, source_target_pairs={{0,16},{1,17},{2,18},{3,19},{4,20},{5,21},{6,22},{7,23},{8,24},{9,... | collective-permute-start | bytes 393224 | tf_op jit(solution)/shard_map/ppermute | solution.py:47
  14.2 5.0 %collective-permute-start.5 = (bf16[2,128,256]{2,1,0:T(8,128)(2,1)S(1)}, bf16[2,128,256]{2,1,0:T(8,128)(2,1)S(1)}, u32[]{:S(2)}, u32[]{:S(2)}) collective-permute-start(bf16[2,128,256]{2,1,0:T(8,128)(2,1)S(1)} %get-tuple-element.57), channel_id=1, source_target_pairs={{0,24},{1,25},{2,26},{3,27},{4,28},{5,29},{6,30},{7,31},{8,0},{9,1... | collective-permute-start | bytes 393224 | tf_op jit(solution)/shard_map/ppermute | solution.py:47
  19.2 18.1 %collective-permute-start.10 = (bf16[8,128,256]{2,1,0:T(8,128)(2,1)S(1)}, bf16[8,128,256]{2,1,0:T(8,128)(2,1)S(1)}, u32[]{:S(2)}, u32[]{:S(2)}) collective-permute-start(bf16[8,128,256]{2,1,0:T(8,128)(2,1)S(1)} %constant_dynamic-update-slice_fusion.v0), channel_id=1, source_target_pairs={{0,1},{1,2},{2,3},{3,0},{4,5},{5,6},{6,7},{7,4},{8,9},{9,10},{10,1... | collective-permute-start | bytes 1572872 | tf_op jit(solution)/shard_map/ppermute | solution.py:47
  20.9 16.5 %collective-permute-start.9 = (bf16[8,128,256]{2,1,0:T(8,128)(2,1)S(1)}, bf16[8,128,256]{2,1,0:T(8,128)(2,1)S(1)}, u32[]{:S(2)}, u32[]{:S(2)}) collective-permute-start(bf16[8,128,256]{2,1,0:T(8,128)(2,1)S(1)} %constant_dynamic-update-slice_fusion.v0), channel_id=1, source_target_pairs={{0,2},{1,3},{2,0},{3,1},{4,6},{5,7},{6,4},{7,5},{8,10},{9,11},{10,... | collective-permute-start | bytes 1572872 | tf_op jit(solution)/shard_map/ppermute | solution.py:47
  21.8 15.5 %collective-permute-start.8 = (bf16[8,128,256]{2,1,0:T(8,128)(2,1)S(1)}, bf16[8,128,256]{2,1,0:T(8,128)(2,1)S(1)}, u32[]{:S(2)}, u32[]{:S(2)}) collective-permute-start(bf16[8,128,256]{2,1,0:T(8,128)(2,1)S(1)} %constant_dynamic-update-slice_fusion.v0), channel_id=1, source_target_pairs={{0,3},{1,0},{2,1},{3,2},{4,7},{5,4},{6,5},{7,6},{8,11},{9,8},{10,9... | collective-permute-start | bytes 1572872 | tf_op jit(solution)/shard_map/ppermute | solution.py:47
  24.3 7.7 %collective-permute-start.3 = (bf16[2,128,256]{2,1,0:T(8,128)(2,1)S(1)}, bf16[2,128,256]{2,1,0:T(8,128)(2,1)S(1)}, u32[]{:S(2)}, u32[]{:S(2)}) collective-permute-start(bf16[2,128,256]{2,1,0:T(8,128)(2,1)S(1)} %get-tuple-element.58.u0), channel_id=1, source_target_pairs={{0,64},{1,65},{2,66},{3,67},{4,68},{5,69},{6,70},{7,71},{8,72},{9,... | collective-permute-start | bytes 393224 | tf_op jit(solution)/shard_map/ppermute | solution.py:47
  26.8 8.1 %copy-start.4 = (s32[24]{0:T(128)S(1)}, s32[24]{0:T(128)}, u32[]{:S(2)}) copy-start(s32[24]{0:T(128)} %param.7) | copy-start | bytes 292
  26.8 8.1 %copy-start.5 = (s32[24]{0:T(128)S(1)}, s32[24]{0:T(128)}, u32[]{:S(2)}) copy-start(s32[24]{0:T(128)} %param.8) | copy-start | bytes 292
  26.8 9.0 %collective-permute-start.2 = (bf16[2,128,256]{2,1,0:T(8,128)(2,1)S(1)}, bf16[2,128,256]{2,1,0:T(8,128)(2,1)S(1)}, u32[]{:S(2)}, u32[]{:S(2)}) collective-permute-start(bf16[2,128,256]{2,1,0:T(8,128)(2,1)S(1)} %get-tuple-element.58.u0), channel_id=1, source_target_pairs={{0,128},{1,129},{2,130},{3,131},{4,132},{5,133},{6,134},{7,135},{8... | collective-permute-start | bytes 393224 | tf_op jit(solution)/shard_map/ppermute | solution.py:47
  31.9 5.4 %collective-permute-start.1 = (bf16[2,128,256]{2,1,0:T(8,128)(2,1)S(1)}, bf16[2,128,256]{2,1,0:T(8,128)(2,1)S(1)}, u32[]{:S(2)}, u32[]{:S(2)}) collective-permute-start(bf16[2,128,256]{2,1,0:T(8,128)(2,1)S(1)} %get-tuple-element.58.u0), channel_id=1, source_target_pairs={{0,192},{1,193},{2,194},{3,195},{4,196},{5,197},{6,198},{7,199},{8... | collective-permute-start | bytes 393224 | tf_op jit(solution)/shard_map/ppermute | solution.py:47
  37.4 1.1 copy-start.1
  40.9 4.4 %collective-permute-start.11 = (bf16[4,128,256]{2,1,0:T(8,128)(2,1)S(1)}, bf16[4,128,256]{2,1,0:T(8,128)(2,1)S(1)}, u32[]{:S(2)}, u32[]{:S(2)}) collective-permute-start(bf16[4,128,256]{2,1,0:T(8,128)(2,1)S(1)} %get-tuple-element.18), channel_id=1, source_target_pairs={{0,32},{1,33},{2,34},{3,35},{4,36},{5,37},{6,38},{7,39},{8,40},{9,... | collective-permute-start | bytes 786440 | tf_op jit(solution)/shard_map/ppermute | solution.py:47
  41.0 9.3 %collective-permute-start.15 = (bf16[8,128,256]{2,1,0:T(8,128)(2,1)S(1)}, bf16[8,128,256]{2,1,0:T(8,128)(2,1)S(1)}, u32[]{:S(2)}, u32[]{:S(2)}) collective-permute-start(bf16[8,128,256]{2,1,0:T(8,128)(2,1)S(1)} %get-tuple-element.20), channel_id=1, source_target_pairs={{0,1},{1,2},{2,3},{3,0},{4,5},{5,6},{6,7},{7,4},{8,9},{9,10},{10,1... | collective-permute-start | bytes 1572872 | tf_op jit(solution)/shard_map/ppermute | solution.py:47
  42.0 10.8 %collective-permute-start.16 = (bf16[8,128,256]{2,1,0:T(8,128)(2,1)S(1)}, bf16[8,128,256]{2,1,0:T(8,128)(2,1)S(1)}, u32[]{:S(2)}, u32[]{:S(2)}) collective-permute-start(bf16[8,128,256]{2,1,0:T(8,128)(2,1)S(1)} %get-tuple-element.21), channel_id=1, source_target_pairs={{0,2},{1,3},{2,0},{3,1},{4,6},{5,7},{6,4},{7,5},{8,10},{9,11},{10,... | collective-permute-start | bytes 1572872 | tf_op jit(solution)/shard_map/ppermute | solution.py:47
  44.6 13.7 %collective-permute-start.17 = (bf16[8,128,256]{2,1,0:T(8,128)(2,1)S(1)}, bf16[8,128,256]{2,1,0:T(8,128)(2,1)S(1)}, u32[]{:S(2)}, u32[]{:S(2)}) collective-permute-start(bf16[8,128,256]{2,1,0:T(8,128)(2,1)S(1)} %get-tuple-element.22), channel_id=1, source_target_pairs={{0,3},{1,0},{2,1},{3,2},{4,7},{5,4},{6,5},{7,6},{8,11},{9,8},{10,9... | collective-permute-start | bytes 1572872 | tf_op jit(solution)/shard_map/ppermute | solution.py:47
  58.7 8.5 %collective-permute-start.18 = (bf16[2,128,256]{2,1,0:T(8,128)(2,1)S(1)}, bf16[2,128,256]{2,1,0:T(8,128)(2,1)S(1)}, u32[]{:S(2)}, u32[]{:S(2)}) collective-permute-start(bf16[2,128,256]{2,1,0:T(8,128)(2,1)S(1)} %get-tuple-element.42), channel_id=1, source_target_pairs={{0,8},{1,9},{2,10},{3,11},{4,12},{5,13},{6,14},{7,15},{8,16},{9,17... | collective-permute-start | bytes 393224 | tf_op jit(solution)/shard_map/ppermute | solution.py:47
  59.7 9.0 %collective-permute-start.20 = (bf16[2,128,256]{2,1,0:T(8,128)(2,1)S(1)}, bf16[2,128,256]{2,1,0:T(8,128)(2,1)S(1)}, u32[]{:S(2)}, u32[]{:S(2)}) collective-permute-start(bf16[2,128,256]{2,1,0:T(8,128)(2,1)S(1)} %get-tuple-element.43), channel_id=1, source_target_pairs={{0,24},{1,25},{2,26},{3,27},{4,28},{5,29},{6,30},{7,31},{8,0},{9,1... | collective-permute-start | bytes 393224 | tf_op jit(solution)/shard_map/ppermute | solution.py:47
  62.2 6.6 %collective-permute-start.19 = (bf16[2,128,256]{2,1,0:T(8,128)(2,1)S(1)}, bf16[2,128,256]{2,1,0:T(8,128)(2,1)S(1)}, u32[]{:S(2)}, u32[]{:S(2)}) collective-permute-start(bf16[2,128,256]{2,1,0:T(8,128)(2,1)S(1)} %get-tuple-element.44), channel_id=1, source_target_pairs={{0,16},{1,17},{2,18},{3,19},{4,20},{5,21},{6,22},{7,23},{8,24},{9,... | collective-permute-start | bytes 393224 | tf_op jit(solution)/shard_map/ppermute | solution.py:47
  63.3 11.3 %collective-permute-start.12 = (bf16[128,256]{1,0:T(8,128)(2,1)S(1)}, bf16[128,256]{1,0:T(8,128)(2,1)S(1)}, u32[]{:S(2)}, u32[]{:S(2)}) collective-permute-start(bf16[128,256]{1,0:T(8,128)(2,1)S(1)} %get-tuple-element.48), channel_id=1, source_target_pairs={{0,64},{1,65},{2,66},{3,67},{4,68},{5,69},{6,70},{7,71},{8,72},{9,... | collective-permute-start | bytes 196616 | tf_op jit(solution)/shard_map/ppermute | solution.py:47
  65.0 9.6 %collective-permute-start.14 = (bf16[128,256]{1,0:T(8,128)(2,1)S(1)}, bf16[128,256]{1,0:T(8,128)(2,1)S(1)}, u32[]{:S(2)}, u32[]{:S(2)}) collective-permute-start(bf16[128,256]{1,0:T(8,128)(2,1)S(1)} %get-tuple-element.49), channel_id=1, source_target_pairs={{0,192},{1,193},{2,194},{3,195},{4,196},{5,197},{6,198},{7,199},{8... | collective-permute-start | bytes 196616 | tf_op jit(solution)/shard_map/ppermute | solution.py:47
  67.2 7.4 %collective-permute-start.13 = (bf16[128,256]{1,0:T(8,128)(2,1)S(1)}, bf16[128,256]{1,0:T(8,128)(2,1)S(1)}, u32[]{:S(2)}, u32[]{:S(2)}) collective-permute-start(bf16[128,256]{1,0:T(8,128)(2,1)S(1)} %get-tuple-element.50), channel_id=1, source_target_pairs={{0,128},{1,129},{2,130},{3,131},{4,132},{5,133},{6,134},{7,135},{8... | collective-permute-start | bytes 196616 | tf_op jit(solution)/shard_map/ppermute | solution.py:47
  68.9 8.3 %collective-permute-start.21 = (bf16[128,256]{1,0:T(8,128)(2,1)S(1)}, bf16[128,256]{1,0:T(8,128)(2,1)S(1)}, u32[]{:S(2)}, u32[]{:S(2)}) collective-permute-start(bf16[128,256]{1,0:T(8,128)(2,1)S(1)} %fusion.9), channel_id=1, source_target_pairs={{0,4},{1,5},{2,6},{3,7},{4,0},{5,1},{6,2},{7,3},{8,12},{9,13},{10,... | collective-permute-start | bytes 196616 | tf_op jit(solution)/shard_map/ppermute | solution.py:47
  77.2 35.1 %copy-start.2 = (bf16[24,128,128]{2,1,0:T(8,128)(2,1)S(1)}, bf16[24,128,128]{2,1,0:T(8,128)(2,1)}, u32[]{:S(2)}) copy-start(bf16[24,128,128]{2,1,0:T(8,128)(2,1)} %losses.3) | copy-start | bytes 2359300
  77.3 8.3 %collective-permute-start.26 = (bf16[128,256]{1,0:T(8,128)(2,1)S(1)}, bf16[128,256]{1,0:T(8,128)(2,1)S(1)}, u32[]{:S(2)}, u32[]{:S(2)}) collective-permute-start(bf16[128,256]{1,0:T(8,128)(2,1)S(1)} %get-tuple-element.34), channel_id=1, source_target_pairs={{0,4},{1,5},{2,6},{3,7},{4,0},{5,1},{6,2},{7,3},{8,12},{9,13},{10,... | collective-permute-start | bytes 196616 | tf_op jit(solution)/shard_map/ppermute | solution.py:47
  83.0 2.6 %collective-permute-start.22 = (bf16[128,256]{1,0:T(8,128)(2,1)S(1)}, bf16[128,256]{1,0:T(8,128)(2,1)S(1)}, u32[]{:S(2)}, u32[]{:S(2)}) collective-permute-start(bf16[128,256]{1,0:T(8,128)(2,1)S(1)} %get-tuple-element.34), channel_id=1, source_target_pairs={{0,32},{1,33},{2,34},{3,35},{4,36},{5,37},{6,38},{7,39},{8,40},{9,... | collective-permute-start | bytes 196616 | tf_op jit(solution)/shard_map/ppermute | solution.py:47
  85.6 8.6 %collective-permute-start.29 = (bf16[2,128,256]{2,1,0:T(8,128)(2,1)S(1)}, bf16[2,128,256]{2,1,0:T(8,128)(2,1)S(1)}, u32[]{:S(2)}, u32[]{:S(2)}) collective-permute-start(bf16[2,128,256]{2,1,0:T(8,128)(2,1)S(1)} %get-tuple-element.55), channel_id=1, source_target_pairs={{0,8},{1,9},{2,10},{3,11},{4,12},{5,13},{6,14},{7,15},{8,16},{9,17... | collective-permute-start | bytes 393224 | tf_op jit(solution)/shard_map/ppermute | solution.py:47
  86.6 7.5 %collective-permute-start.28 = (bf16[2,128,256]{2,1,0:T(8,128)(2,1)S(1)}, bf16[2,128,256]{2,1,0:T(8,128)(2,1)S(1)}, u32[]{:S(2)}, u32[]{:S(2)}) collective-permute-start(bf16[2,128,256]{2,1,0:T(8,128)(2,1)S(1)} %get-tuple-element.55), channel_id=1, source_target_pairs={{0,16},{1,17},{2,18},{3,19},{4,20},{5,21},{6,22},{7,23},{8,24},{9,... | collective-permute-start | bytes 393224 | tf_op jit(solution)/shard_map/ppermute | solution.py:47
  88.9 5.2 %collective-permute-start.27 = (bf16[2,128,256]{2,1,0:T(8,128)(2,1)S(1)}, bf16[2,128,256]{2,1,0:T(8,128)(2,1)S(1)}, u32[]{:S(2)}, u32[]{:S(2)}) collective-permute-start(bf16[2,128,256]{2,1,0:T(8,128)(2,1)S(1)} %get-tuple-element.55), channel_id=1, source_target_pairs={{0,24},{1,25},{2,26},{3,27},{4,28},{5,29},{6,30},{7,31},{8,0},{9,1... | collective-permute-start | bytes 393224 | tf_op jit(solution)/shard_map/ppermute | solution.py:47
  94.2 18.2 %collective-permute-start.32 = (bf16[8,128,256]{2,1,0:T(8,128)(2,1)S(1)}, bf16[8,128,256]{2,1,0:T(8,128)(2,1)S(1)}, u32[]{:S(2)}, u32[]{:S(2)}) collective-permute-start(bf16[8,128,256]{2,1,0:T(8,128)(2,1)S(1)} %constant_dynamic-update-slice_fusion.5.v0), channel_id=1, source_target_pairs={{0,1},{1,2},{2,3},{3,0},{4,5},{5,6},{6,7},{7,4},{8,9},{9,10},{10,1... | collective-permute-start | bytes 1572872 | tf_op jit(solution)/shard_map/ppermute | solution.py:47
  95.5 16.9 %collective-permute-start.31 = (bf16[8,128,256]{2,1,0:T(8,128)(2,1)S(1)}, bf16[8,128,256]{2,1,0:T(8,128)(2,1)S(1)}, u32[]{:S(2)}, u32[]{:S(2)}) collective-permute-start(bf16[8,128,256]{2,1,0:T(8,128)(2,1)S(1)} %constant_dynamic-update-slice_fusion.5.v0), channel_id=1, source_target_pairs={{0,2},{1,3},{2,0},{3,1},{4,6},{5,7},{6,4},{7,5},{8,10},{9,11},{10,... | collective-permute-start | bytes 1572872 | tf_op jit(solution)/shard_map/ppermute | solution.py:47
  97.6 14.8 %collective-permute-start.30 = (bf16[8,128,256]{2,1,0:T(8,128)(2,1)S(1)}, bf16[8,128,256]{2,1,0:T(8,128)(2,1)S(1)}, u32[]{:S(2)}, u32[]{:S(2)}) collective-permute-start(bf16[8,128,256]{2,1,0:T(8,128)(2,1)S(1)} %constant_dynamic-update-slice_fusion.5.v0), channel_id=1, source_target_pairs={{0,3},{1,0},{2,1},{3,2},{4,7},{5,4},{6,5},{7,6},{8,11},{9,8},{10,9... | collective-permute-start | bytes 1572872 | tf_op jit(solution)/shard_map/ppermute | solution.py:47
  100.1 7.2 %collective-permute-start.25 = (bf16[2,128,256]{2,1,0:T(8,128)(2,1)S(1)}, bf16[2,128,256]{2,1,0:T(8,128)(2,1)S(1)}, u32[]{:S(2)}, u32[]{:S(2)}) collective-permute-start(bf16[2,128,256]{2,1,0:T(8,128)(2,1)S(1)} %get-tuple-element.56.u0), channel_id=1, source_target_pairs={{0,64},{1,65},{2,66},{3,67},{4,68},{5,69},{6,70},{7,71},{8,72},{9,... | collective-permute-start | bytes 393224 | tf_op jit(solution)/shard_map/ppermute | solution.py:47
  101.4 9.2 %collective-permute-start.24 = (bf16[2,128,256]{2,1,0:T(8,128)(2,1)S(1)}, bf16[2,128,256]{2,1,0:T(8,128)(2,1)S(1)}, u32[]{:S(2)}, u32[]{:S(2)}) collective-permute-start(bf16[2,128,256]{2,1,0:T(8,128)(2,1)S(1)} %get-tuple-element.56.u0), channel_id=1, source_target_pairs={{0,128},{1,129},{2,130},{3,131},{4,132},{5,133},{6,134},{7,135},{8... | collective-permute-start | bytes 393224 | tf_op jit(solution)/shard_map/ppermute | solution.py:47
  107.3 5.1 %collective-permute-start.23 = (bf16[2,128,256]{2,1,0:T(8,128)(2,1)S(1)}, bf16[2,128,256]{2,1,0:T(8,128)(2,1)S(1)}, u32[]{:S(2)}, u32[]{:S(2)}) collective-permute-start(bf16[2,128,256]{2,1,0:T(8,128)(2,1)S(1)} %get-tuple-element.56.u0), channel_id=1, source_target_pairs={{0,192},{1,193},{2,194},{3,195},{4,196},{5,197},{6,198},{7,199},{8... | collective-permute-start | bytes 393224 | tf_op jit(solution)/shard_map/ppermute | solution.py:47
  114.8 4.8 %collective-permute-start.33 = (bf16[4,128,256]{2,1,0:T(8,128)(2,1)S(1)}, bf16[4,128,256]{2,1,0:T(8,128)(2,1)S(1)}, u32[]{:S(2)}, u32[]{:S(2)}) collective-permute-start(bf16[4,128,256]{2,1,0:T(8,128)(2,1)S(1)} %get-tuple-element.24), channel_id=1, source_target_pairs={{0,32},{1,33},{2,34},{3,35},{4,36},{5,37},{6,38},{7,39},{8,40},{9,... | collective-permute-start | bytes 786440 | tf_op jit(solution)/shard_map/ppermute | solution.py:47
  114.9 9.3 %collective-permute-start.37 = (bf16[8,128,256]{2,1,0:T(8,128)(2,1)S(1)}, bf16[8,128,256]{2,1,0:T(8,128)(2,1)S(1)}, u32[]{:S(2)}, u32[]{:S(2)}) collective-permute-start(bf16[8,128,256]{2,1,0:T(8,128)(2,1)S(1)} %get-tuple-element.26), channel_id=1, source_target_pairs={{0,1},{1,2},{2,3},{3,0},{4,5},{5,6},{6,7},{7,4},{8,9},{9,10},{10,1... | collective-permute-start | bytes 1572872 | tf_op jit(solution)/shard_map/ppermute | solution.py:47
  115.8 10.8 %collective-permute-start.38 = (bf16[8,128,256]{2,1,0:T(8,128)(2,1)S(1)}, bf16[8,128,256]{2,1,0:T(8,128)(2,1)S(1)}, u32[]{:S(2)}, u32[]{:S(2)}) collective-permute-start(bf16[8,128,256]{2,1,0:T(8,128)(2,1)S(1)} %get-tuple-element.27), channel_id=1, source_target_pairs={{0,2},{1,3},{2,0},{3,1},{4,6},{5,7},{6,4},{7,5},{8,10},{9,11},{10,... | collective-permute-start | bytes 1572872 | tf_op jit(solution)/shard_map/ppermute | solution.py:47
  118.1 14.0 %collective-permute-start.39 = (bf16[8,128,256]{2,1,0:T(8,128)(2,1)S(1)}, bf16[8,128,256]{2,1,0:T(8,128)(2,1)S(1)}, u32[]{:S(2)}, u32[]{:S(2)}) collective-permute-start(bf16[8,128,256]{2,1,0:T(8,128)(2,1)S(1)} %get-tuple-element.28), channel_id=1, source_target_pairs={{0,3},{1,0},{2,1},{3,2},{4,7},{5,4},{6,5},{7,6},{8,11},{9,8},{10,9... | collective-permute-start | bytes 1572872 | tf_op jit(solution)/shard_map/ppermute | solution.py:47
  132.4 8.8 %collective-permute-start.40 = (bf16[2,128,256]{2,1,0:T(8,128)(2,1)S(1)}, bf16[2,128,256]{2,1,0:T(8,128)(2,1)S(1)}, u32[]{:S(2)}, u32[]{:S(2)}) collective-permute-start(bf16[2,128,256]{2,1,0:T(8,128)(2,1)S(1)} %get-tuple-element.39), channel_id=1, source_target_pairs={{0,8},{1,9},{2,10},{3,11},{4,12},{5,13},{6,14},{7,15},{8,16},{9,17... | collective-permute-start | bytes 393224 | tf_op jit(solution)/shard_map/ppermute | solution.py:47
  133.5 8.6 %collective-permute-start.42 = (bf16[2,128,256]{2,1,0:T(8,128)(2,1)S(1)}, bf16[2,128,256]{2,1,0:T(8,128)(2,1)S(1)}, u32[]{:S(2)}, u32[]{:S(2)}) collective-permute-start(bf16[2,128,256]{2,1,0:T(8,128)(2,1)S(1)} %get-tuple-element.40), channel_id=1, source_target_pairs={{0,24},{1,25},{2,26},{3,27},{4,28},{5,29},{6,30},{7,31},{8,0},{9,1... | collective-permute-start | bytes 393224 | tf_op jit(solution)/shard_map/ppermute | solution.py:47
  135.7 6.5 %collective-permute-start.41 = (bf16[2,128,256]{2,1,0:T(8,128)(2,1)S(1)}, bf16[2,128,256]{2,1,0:T(8,128)(2,1)S(1)}, u32[]{:S(2)}, u32[]{:S(2)}) collective-permute-start(bf16[2,128,256]{2,1,0:T(8,128)(2,1)S(1)} %get-tuple-element.41), channel_id=1, source_target_pairs={{0,16},{1,17},{2,18},{3,19},{4,20},{5,21},{6,22},{7,23},{8,24},{9,... | collective-permute-start | bytes 393224 | tf_op jit(solution)/shard_map/ppermute | solution.py:47
  137.3 17.1 %collective-permute-start.34 = (bf16[128,256]{1,0:T(8,128)(2,1)S(1)}, bf16[128,256]{1,0:T(8,128)(2,1)S(1)}, u32[]{:S(2)}, u32[]{:S(2)}) collective-permute-start(bf16[128,256]{1,0:T(8,128)(2,1)S(1)} %get-tuple-element.45), channel_id=1, source_target_pairs={{0,64},{1,65},{2,66},{3,67},{4,68},{5,69},{6,70},{7,71},{8,72},{9,... | collective-permute-start | bytes 196616 | tf_op jit(solution)/shard_map/ppermute | solution.py:47
  139.6 14.8 %collective-permute-start.36 = (bf16[128,256]{1,0:T(8,128)(2,1)S(1)}, bf16[128,256]{1,0:T(8,128)(2,1)S(1)}, u32[]{:S(2)}, u32[]{:S(2)}) collective-permute-start(bf16[128,256]{1,0:T(8,128)(2,1)S(1)} %get-tuple-element.46), channel_id=1, source_target_pairs={{0,192},{1,193},{2,194},{3,195},{4,196},{5,197},{6,198},{7,199},{8... | collective-permute-start | bytes 196616 | tf_op jit(solution)/shard_map/ppermute | solution.py:47
  141.2 13.2 %collective-permute-start.35 = (bf16[128,256]{1,0:T(8,128)(2,1)S(1)}, bf16[128,256]{1,0:T(8,128)(2,1)S(1)}, u32[]{:S(2)}, u32[]{:S(2)}) collective-permute-start(bf16[128,256]{1,0:T(8,128)(2,1)S(1)} %get-tuple-element.47), channel_id=1, source_target_pairs={{0,128},{1,129},{2,130},{3,131},{4,132},{5,133},{6,134},{7,135},{8... | collective-permute-start | bytes 196616 | tf_op jit(solution)/shard_map/ppermute | solution.py:47
  142.3 15.7 %collective-permute-start.43 = (bf16[128,256]{1,0:T(8,128)(2,1)S(1)}, bf16[128,256]{1,0:T(8,128)(2,1)S(1)}, u32[]{:S(2)}, u32[]{:S(2)}) collective-permute-start(bf16[128,256]{1,0:T(8,128)(2,1)S(1)} %fusion.10), channel_id=1, source_target_pairs={{0,4},{1,5},{2,6},{3,7},{4,0},{5,1},{6,2},{7,3},{8,12},{9,13},{10,... | collective-permute-start | bytes 196616 | tf_op jit(solution)/shard_map/ppermute | solution.py:47

commit v2 on v1

--- a/solution.py
+++ b/solution.py
@@ -123,13 +123,21 @@
             pltpu.VMEM((8, tile, width), jnp.float32),
             pltpu.VMEM((32, tile, width), jnp.float32),
         ],
-        compiler_params=pltpu.CompilerParams(vmem_limit_bytes=40 * 1024 * 1024),
+        compiler_params=pltpu.CompilerParams(vmem_limit_bytes=24 * 1024 * 1024),
     )(first_place, second_place, live, *left_parts, *right_parts, wins, losses)
+
+
+def turn_back(raw):
+    half = raw.shape[-1] // 2
+    return jnp.concatenate([raw[..., half:], -raw[..., :half]], axis=-1)
+
+
+def total(first, parts):
+    return first + sum(part.astype(jnp.float32) for part in parts)
 
 
 def per_device(embedding, row_blocks, col_blocks, win_counts, loss_counts, live_tiles):
     at = {axis: lax.axis_index(axis) for axis in AXES}
-    half = embedding.shape[1] // 2
     first_place = ((row_blocks // 2 - at["zl"]) % 4) * 2 + (row_blocks + at["core"]) % 2
     far_x = (col_blocks // 8 - at["x"]) % 4
     far_y = (col_blocks - at["y"]) % 4
@@ -139,34 +147,36 @@
     second_place = (outer * 4 + inner) * 2 + far_z
     inner_axes, outer_axes = ("x", "y"), ("y", "x")
 
-    current = embedding
-    result = embedding.astype(jnp.float32)
+    partner = send(embedding, shift("zh", 1))
+    block, partner = lax.optimization_barrier((embedding, partner))
+    pair = jnp.stack([block, partner])
     for iteration in range(ITERS):
-        pair = jnp.stack([current, send(current, shift("zh", 1))])
-        cores = jnp.stack([current, send(current, shift("core", 1))])
         inner_parts = [pair] + [send(pair, shift_by_core(inner_axes, -k)) for k in (1, 2, 3)]
+        cores = jnp.stack([block, send(block, shift("core", 1))])
+        line = jnp.concatenate(inner_parts)
+        line, cores = lax.optimization_barrier((line, cores))
         left_parts = [cores] + [send(cores, shift("zl", -k)) for k in (1, 2, 3)]
-        line = jnp.concatenate(inner_parts)
         right_parts = [line] + [send(line, shift_by_core(outer_axes, -k)) for k in (1, 2, 3)]
         near, far, *second = slot_grads(
             first_place, second_place, live_tiles, left_parts, right_parts, win_counts, loss_counts
         )
         came = [send(second[k], shift_by_core(outer_axes, k)) for k in (1, 2, 3)]
-        far = send(far, shift("core", 1))
-        line_sum = second[0] + sum(part.astype(jnp.float32) for part in came)
-        near = near + far.astype(jnp.float32)
+        near = near + send(far, shift("core", 1)).astype(jnp.float32)
         near_out = near.astype(jnp.bfloat16)
-        line_out = line_sum.astype(jnp.bfloat16)
+        first_share = total(near[0], [send(near_out[k], shift("zl", k)) for k in (1, 2, 3)])
+        line_sum = total(second[0], came)
+        line_out, first_share = lax.optimization_barrier((line_sum.astype(jnp.bfloat16), first_share))
         came = [send(line_out[2 * k : 2 * k + 2], shift_by_core(inner_axes, k)) for k in (1, 2, 3)]
-        near_came = [send(near_out[k], shift("zl", k)) for k in (1, 2, 3)]
-        pair_sum = line_sum[:2] + sum(part.astype(jnp.float32) for part in came)
-        partner = send(pair_sum[1].astype(jnp.bfloat16), shift("zh", 1))
-        first_share = near[0] + sum(part.astype(jnp.float32) for part in near_came)
-        raw = first_share - (pair_sum[0] + partner.astype(jnp.float32))
-        grad = jnp.concatenate([raw[:, half:], -raw[:, :half]], axis=1)
-        result = current.astype(jnp.float32) + RATE * grad
-        current = result.astype(jnp.bfloat16)
-    return result
+        pair_sum = total(line_sum[:2], came)
+        own, other = first_share - pair_sum[0], -pair_sum[1]
+        if iteration == ITERS - 1:
+            raw = own + send(other.astype(jnp.bfloat16), shift("zh", 1)).astype(jnp.float32)
+            return block.astype(jnp.float32) + RATE * turn_back(raw)
+        pieces = lax.optimization_barrier(jnp.stack([own, other]).astype(jnp.bfloat16))
+        swapped = send(pieces, shift("zh", 1))
+        raw = pieces.astype(jnp.float32) + swapped[::-1].astype(jnp.float32)
+        pair = (pair.astype(jnp.float32) + RATE * turn_back(raw)).astype(jnp.bfloat16)
+        block = pair[0]
 
 
 def solution(mesh):

time: 160 us -> 152 us (0.950)
  starting transfers between devices: 95.4 us -> 83.9 us
  waiting for transfers between devices: 53.5 us -> 55.3 us
    ppermute x44 -> x43, starting transfers between devices: 95.4 us -> 83.9 us  [send(): return lax.ppermute(values, AXES, pairs)]
    ppermute x44 -> x43, waiting for transfers between devices: 53.5 us -> 55.3 us  [send(): return lax.ppermute(values, AXES, pairs)]
  transfers between devices with their start and end apart: 44 -> 43, of which waited for: 19 -> 24; matrix products, arithmetic and copies ran while one was open for 1% -> 1% of each run, Pallas kernels for 0% -> 0%
where the time goes in v2:
time: 152 us; the launch traced here: 149 us
  starting transfers between devices  83.9 us (55%)
  waiting for transfers between devices  55.3 us (36%)
  Pallas kernels  5.02 us (3%)
  local copies, waits for them, and re-layouts  2.13 us (1%)
  other arithmetic  1.95 us (1%)
    ppermute x43, starting transfers between devices, send(): return lax.ppermute(values, AXES, pairs)  83.9 us
    ppermute x43, waiting for transfers between devices, send(): return lax.ppermute(values, AXES, pairs)  55.3 us
    pallas_call x2, Pallas kernels, slot_grads(): pl.pallas_call(slot_kernel, out_shape=(blocks(4, jnp.float32), blocks(4,...  5.02 us
  transfers between devices with their start and end apart: 43, of which 24 were waited for; matrix products, arithmetic and copies ran while one was open for 1% of the time, Pallas kernels for 0%

profile of v2, /device:TPU:8, one launch (start us, length us, event | category | flops | bytes accessed | tf_op | source)
XLA Modules:
  0.0 149.4 jit_solution(16342605071556645996)
XLA Ops:
  0.0 7.2 %collective-permute-start = (bf16[128,256]{1,0:T(8,128)(2,1)}, bf16[128,256]{1,0:T(8,128)(2,1)S(1)}, u32[]{:S(2)}, u32[]{:S(2)}) collective-permute-start(bf16[128,256]{1,0:T(8,128)(2,1)} %param.6), channel_id=1, source_target_pairs={{0,4},{1,5},{2,6},{3,7},{4,0},{5,1},{6,2},{7,3},{8,12},{9,13},{10,... | collective-permute-start | bytes 196616 | tf_op jit(solution)/shard_map/ppermute | solution.py:47
  7.2 2.7 %collective-permute-done = bf16[128,256]{1,0:T(8,128)(2,1)S(1)} collective-permute-done((bf16[128,256]{1,0:T(8,128)(2,1)}, bf16[128,256]{1,0:T(8,128)(2,1)S(1)}, u32[]{:S(2)}, u32[]{:S(2)}) %collective-permute-start) | collective-permute-done | bytes 65568 | tf_op jit(solution)/shard_map/ppermute | solution.py:47
  9.9 0.8 constant_dynamic-update-slice_fusion.4
  11.4 3.1 %collective-permute-start.2 = (bf16[2,128,256]{2,1,0:T(8,128)(2,1)S(1)}, bf16[2,128,256]{2,1,0:T(8,128)(2,1)S(1)}, u32[]{:S(2)}, u32[]{:S(2)}) collective-permute-start(bf16[2,128,256]{2,1,0:T(8,128)(2,1)S(1)} %get-tuple-element.76), channel_id=1, source_target_pairs={{0,16},{1,17},{2,18},{3,19},{4,20},{5,21},{6,22},{7,23},{8,24},{9,... | collective-permute-start | bytes 393224 | tf_op jit(solution)/shard_map/ppermute | solution.py:47
  14.5 1.1 collective-permute-start.1
  15.6 0.9 collective-permute-start.3
  16.5 2.9 %collective-permute-done.1 = bf16[2,128,256]{2,1,0:T(8,128)(2,1)S(1)} collective-permute-done((bf16[2,128,256]{2,1,0:T(8,128)(2,1)S(1)}, bf16[2,128,256]{2,1,0:T(8,128)(2,1)S(1)}, u32[]{:S(2)}, u32[]{:S(2)}) %collective-permute-start.1) | collective-permute-done | bytes 131104 | tf_op jit(solution)/shard_map/ppermute | solution.py:47
  19.5 2.3 %collective-permute-done.3 = bf16[2,128,256]{2,1,0:T(8,128)(2,1)S(1)} collective-permute-done((bf16[2,128,256]{2,1,0:T(8,128)(2,1)S(1)}, bf16[2,128,256]{2,1,0:T(8,128)(2,1)S(1)}, u32[]{:S(2)}, u32[]{:S(2)}) %collective-permute-start.3) | collective-permute-done | bytes 131104 | tf_op jit(solution)/shard_map/ppermute | solution.py:47
  21.8 1.7 %collective-permute-start.10 = (bf16[8,128,256]{2,1,0:T(8,128)(2,1)S(1)}, bf16[8,128,256]{2,1,0:T(8,128)(2,1)S(1)}, u32[]{:S(2)}, u32[]{:S(2)}) collective-permute-start(bf16[8,128,256]{2,1,0:T(8,128)(2,1)S(1)} %constant_dynamic-update-slice_fusion.v0), channel_id=1, source_target_pairs={{0,1},{1,2},{2,3},{3,0},{4,5},{5,6},{6,7},{7,4},{8,9},{9,10},{10,1... | collective-permute-start | bytes 1572872 | tf_op jit(solution)/shard_map/ppermute | solution.py:47
  23.5 0.9 collective-permute-start.9
  24.4 2.4 %collective-permute-start.8 = (bf16[8,128,256]{2,1,0:T(8,128)(2,1)S(1)}, bf16[8,128,256]{2,1,0:T(8,128)(2,1)S(1)}, u32[]{:S(2)}, u32[]{:S(2)}) collective-permute-start(bf16[8,128,256]{2,1,0:T(8,128)(2,1)S(1)} %constant_dynamic-update-slice_fusion.v0), channel_id=1, source_target_pairs={{0,3},{1,0},{2,1},{3,2},{4,7},{5,4},{6,5},{7,6},{8,11},{9,8},{10,9... | collective-permute-start | bytes 1572872 | tf_op jit(solution)/shard_map/ppermute | solution.py:47
  26.8 1.9 %collective-permute-start.7 = (bf16[2,128,256]{2,1,0:T(8,128)(2,1)S(1)}, bf16[2,128,256]{2,1,0:T(8,128)(2,1)S(1)}, u32[]{:S(2)}, u32[]{:S(2)}) collective-permute-start(bf16[2,128,256]{2,1,0:T(8,128)(2,1)S(1)} %get-tuple-element.29.u0), channel_id=1, source_target_pairs={{0,64},{1,65},{2,66},{3,67},{4,68},{5,69},{6,70},{7,71},{8,72},{9,... | collective-permute-start | bytes 393224 | tf_op jit(solution)/shard_map/ppermute | solution.py:47
  29.4 1.9 %collective-permute-start.6 = (bf16[2,128,256]{2,1,0:T(8,128)(2,1)S(1)}, bf16[2,128,256]{2,1,0:T(8,128)(2,1)S(1)}, u32[]{:S(2)}, u32[]{:S(2)}) collective-permute-start(bf16[2,128,256]{2,1,0:T(8,128)(2,1)S(1)} %get-tuple-element.29.u0), channel_id=1, source_target_pairs={{0,128},{1,129},{2,130},{3,131},{4,132},{5,133},{6,134},{7,135},{8... | collective-permute-start | bytes 393224 | tf_op jit(solution)/shard_map/ppermute | solution.py:47
  31.3 3.2 %collective-permute-done.7.u3 = bf16[2,128,256]{2,1,0:T(8,128)(2,1)S(1)} collective-permute-done((bf16[2,128,256]{2,1,0:T(8,128)(2,1)S(1)}, bf16[2,128,256]{2,1,0:T(8,128)(2,1)S(1)}, u32[]{:S(2)}, u32[]{:S(2)}) %collective-permute-start.7) | collective-permute-done | bytes 131104 | tf_op jit(solution)/shard_map/ppermute | solution.py:47
  34.5 1.0 collective-permute-start.5
  35.5 2.5 %collective-permute-done.6.u2 = bf16[2,128,256]{2,1,0:T(8,128)(2,1)S(1)} collective-permute-done((bf16[2,128,256]{2,1,0:T(8,128)(2,1)S(1)}, bf16[2,128,256]{2,1,0:T(8,128)(2,1)S(1)}, u32[]{:S(2)}, u32[]{:S(2)}) %collective-permute-start.6) | collective-permute-done | bytes 131104 | tf_op jit(solution)/shard_map/ppermute | solution.py:47
  38.0 1.5 %collective-permute-done.5.u1 = bf16[2,128,256]{2,1,0:T(8,128)(2,1)S(1)} collective-permute-done((bf16[2,128,256]{2,1,0:T(8,128)(2,1)S(1)}, bf16[2,128,256]{2,1,0:T(8,128)(2,1)S(1)}, u32[]{:S(2)}, u32[]{:S(2)}) %collective-permute-start.5) | collective-permute-done | bytes 131104 | tf_op jit(solution)/shard_map/ppermute | solution.py:47
  39.5 1.1 copy-done.1
  40.7 2.4 %shard_map.64 = (f32[4,128,256]{2,1,0:T(8,128)S(1)}, bf16[4,128,256]{2,1,0:T(8,128)(2,1)S(1)}, f32[8,128,256]{2,1,0:T(8,128)S(1)}, bf16[8,128,256]{2,1,0:T(8,128...) custom-call(s32[24]{0:T(128)S(1)} %get-tuple-element.77.first_ref, ...), custom_call_target="tpu_custom_call" | custom-call | tf_op jit(solution)/shard_map/pallas_call | solution.py:111
  43.2 1.4 collective-permute-start.11
  44.6 2.4 %collective-permute-start.12 = (bf16[8,128,256]{2,1,0:T(8,128)(2,1)S(1)}, bf16[8,128,256]{2,1,0:T(8,128)(2,1)S(1)}, u32[]{:S(2)}, u32[]{:S(2)}) collective-permute-start(bf16[8,128,256]{2,1,0:T(8,128)(2,1)S(1)} %get-tuple-element.33), channel_id=1, source_target_pairs={{0,2},{1,3},{2,0},{3,1},{4,6},{5,7},{6,4},{7,5},{8,10},{9,11},{10,... | collective-permute-start | bytes 1572872 | tf_op jit(solution)/shard_map/ppermute | solution.py:47
  47.3 3.0 %collective-permute-start.15 = (bf16[128,256]{1,0:T(8,128)(2,1)S(1)}, bf16[128,256]{1,0:T(8,128)(2,1)S(1)}, u32[]{:S(2)}, u32[]{:S(2)}) collective-permute-start(bf16[128,256]{1,0:T(8,128)(2,1)S(1)} %get-tuple-element.68), channel_id=1, source_target_pairs={{0,64},{1,65},{2,66},{3,67},{4,68},{5,69},{6,70},{7,71},{8,72},{9,... | collective-permute-start | bytes 196616 | tf_op jit(solution)/shard_map/ppermute | solution.py:47
  50.3 1.1 collective-permute-start.17
  51.3 2.6 %collective-permute-done.15 = bf16[128,256]{1,0:T(8,128)(2,1)S(1)} collective-permute-done((bf16[128,256]{1,0:T(8,128)(2,1)S(1)}, bf16[128,256]{1,0:T(8,128)(2,1)S(1)}, u32[]{:S(2)}, u32[]{:S(2)}) %collective-permute-start.15) | collective-permute-done | bytes 65568 | tf_op jit(solution)/shard_map/ppermute | solution.py:47
  53.9 4.7 %collective-permute-start.16 = (bf16[128,256]{1,0:T(8,128)(2,1)S(1)}, bf16[128,256]{1,0:T(8,128)(2,1)S(1)}, u32[]{:S(2)}, u32[]{:S(2)}) collective-permute-start(bf16[128,256]{1,0:T(8,128)(2,1)S(1)} %get-tuple-element.70), channel_id=1, source_target_pairs={{0,128},{1,129},{2,130},{3,131},{4,132},{5,133},{6,134},{7,135},{8... | collective-permute-start | bytes 196616 | tf_op jit(solution)/shard_map/ppermute | solution.py:47
  58.6 2.9 %collective-permute-done.16 = bf16[128,256]{1,0:T(8,128)(2,1)S(1)} collective-permute-done((bf16[128,256]{1,0:T(8,128)(2,1)S(1)}, bf16[128,256]{1,0:T(8,128)(2,1)S(1)}, u32[]{:S(2)}, u32[]{:S(2)}) %collective-permute-start.16) | collective-permute-done | bytes 65568 | tf_op jit(solution)/shard_map/ppermute | solution.py:47
  62.0 1.2 collective-permute-start.18
  63.2 2.1 %collective-permute-start.20 = (bf16[2,128,256]{2,1,0:T(8,128)(2,1)S(1)}, bf16[2,128,256]{2,1,0:T(8,128)(2,1)S(1)}, u32[]{:S(2)}, u32[]{:S(2)}) collective-permute-start(bf16[2,128,256]{2,1,0:T(8,128)(2,1)S(1)} %get-tuple-element.61), channel_id=1, source_target_pairs={{0,24},{1,25},{2,26},{3,27},{4,28},{5,29},{6,30},{7,31},{8,0},{9,1... | collective-permute-start | bytes 393224 | tf_op jit(solution)/shard_map/ppermute | solution.py:47
  65.3 2.9 %collective-permute-done.18 = bf16[2,128,256]{2,1,0:T(8,128)(2,1)S(1)} collective-permute-done((bf16[2,128,256]{2,1,0:T(8,128)(2,1)S(1)}, bf16[2,128,256]{2,1,0:T(8,128)(2,1)S(1)}, u32[]{:S(2)}, u32[]{:S(2)}) %collective-permute-start.18) | collective-permute-done | bytes 131104 | tf_op jit(solution)/shard_map/ppermute | solution.py:47
  68.3 1.0 collective-permute-done.20
  69.2 2.5 %collective-permute-done.19 = bf16[2,128,256]{2,1,0:T(8,128)(2,1)S(1)} collective-permute-done((bf16[2,128,256]{2,1,0:T(8,128)(2,1)S(1)}, bf16[2,128,256]{2,1,0:T(8,128)(2,1)S(1)}, u32[]{:S(2)}, u32[]{:S(2)}) %collective-permute-start.19) | collective-permute-done | bytes 131104 | tf_op jit(solution)/shard_map/ppermute | solution.py:47
  71.9 5.6 %collective-permute-start.21 = (bf16[2,128,256]{2,1,0:T(8,128)(2,1)S(1)}, bf16[2,128,256]{2,1,0:T(8,128)(2,1)S(1)}, u32[]{:S(2)}, u32[]{:S(2)}) collective-permute-start(bf16[2,128,256]{2,1,0:T(8,128)(2,1)S(1)} %pad_maximum_fusion.3), channel_id=1, source_target_pairs={{0,4},{1,5},{2,6},{3,7},{4,0},{5,1},{6,2},{7,3},{8,12},{9,13},{10,... | collective-permute-start | bytes 393224 | tf_op jit(solution)/shard_map/ppermute | solution.py:47
  77.5 3.4 %collective-permute-done.21 = bf16[2,128,256]{2,1,0:T(8,128)(2,1)S(1)} collective-permute-done((bf16[2,128,256]{2,1,0:T(8,128)(2,1)S(1)}, bf16[2,128,256]{2,1,0:T(8,128)(2,1)S(1)}, u32[]{:S(2)}, u32[]{:S(2)}) %collective-permute-start.21) | collective-permute-done | bytes 131104 | tf_op jit(solution)/shard_map/ppermute | solution.py:47
  81.2 2.6 %collective-permute-start.23 = (bf16[2,128,256]{2,1,0:T(8,128)(2,1)S(1)}, bf16[2,128,256]{2,1,0:T(8,128)(2,1)S(1)}, u32[]{:S(2)}, u32[]{:S(2)}) collective-permute-start(bf16[2,128,256]{2,1,0:T(8,128)(2,1)S(1)} %fusion.1), channel_id=1, source_target_pairs={{0,16},{1,17},{2,18},{3,19},{4,20},{5,21},{6,22},{7,23},{8,24},{9,... | collective-permute-start | bytes 393224 | tf_op jit(solution)/shard_map/ppermute | solution.py:47
  83.8 0.7 collective-permute-start.22
  84.5 4.3 %collective-permute-done.24 = bf16[2,128,256]{2,1,0:T(8,128)(2,1)S(1)} collective-permute-done((bf16[2,128,256]{2,1,0:T(8,128)(2,1)S(1)}, bf16[2,128,256]{2,1,0:T(8,128)(2,1)S(1)}, u32[]{:S(2)}, u32[]{:S(2)}) %collective-permute-start.24) | collective-permute-done | bytes 131104 | tf_op jit(solution)/shard_map/ppermute | solution.py:47
  88.8 0.9 collective-permute-done.22
  89.8 1.0 collective-permute-start.31
  90.8 3.5 %collective-permute-start.30 = (bf16[8,128,256]{2,1,0:T(8,128)(2,1)S(1)}, bf16[8,128,256]{2,1,0:T(8,128)(2,1)S(1)}, u32[]{:S(2)}, u32[]{:S(2)}) collective-permute-start(bf16[8,128,256]{2,1,0:T(8,128)(2,1)S(1)} %pad_maximum_fusion.v0), channel_id=1, source_target_pairs={{0,2},{1,3},{2,0},{3,1},{4,6},{5,7},{6,4},{7,5},{8,10},{9,11},{10,... | collective-permute-start | bytes 1572872 | tf_op jit(solution)/shard_map/ppermute | solution.py:47
  94.3 0.8 collective-permute-start.29
  95.1 3.2 %collective-permute-start.28 = (bf16[2,128,256]{2,1,0:T(8,128)(2,1)S(1)}, bf16[2,128,256]{2,1,0:T(8,128)(2,1)S(1)}, u32[]{:S(2)}, u32[]{:S(2)}) collective-permute-start(bf16[2,128,256]{2,1,0:T(8,128)(2,1)S(1)} %pad_maximum_fusion.4.u0), channel_id=1, source_target_pairs={{0,64},{1,65},{2,66},{3,67},{4,68},{5,69},{6,70},{7,71},{8,72},{9,... | collective-permute-start | bytes 393224 | tf_op jit(solution)/shard_map/ppermute | solution.py:47
  98.2 1.1 collective-permute-start.27
  99.3 2.7 %collective-permute-done.28.u3 = bf16[2,128,256]{2,1,0:T(8,128)(2,1)S(1)} collective-permute-done((bf16[2,128,256]{2,1,0:T(8,128)(2,1)S(1)}, bf16[2,128,256]{2,1,0:T(8,128)(2,1)S(1)}, u32[]{:S(2)}, u32[]{:S(2)}) %collective-permute-start.28) | collective-permute-done | bytes 131104 | tf_op jit(solution)/shard_map/ppermute | solution.py:47
  102.1 3.8 %collective-permute-start.26 = (bf16[2,128,256]{2,1,0:T(8,128)(2,1)S(1)}, bf16[2,128,256]{2,1,0:T(8,128)(2,1)S(1)}, u32[]{:S(2)}, u32[]{:S(2)}) collective-permute-start(bf16[2,128,256]{2,1,0:T(8,128)(2,1)S(1)} %pad_maximum_fusion.4.u0), channel_id=1, source_target_pairs={{0,192},{1,193},{2,194},{3,195},{4,196},{5,197},{6,198},{7,199},{8... | collective-permute-start | bytes 393224 | tf_op jit(solution)/shard_map/ppermute | solution.py:47
  105.9 1.1 collective-permute-done.27.u2
  107.0 1.4 collective-permute-done.26.u1
  108.4 2.6 %shard_map.65 = (f32[4,128,256]{2,1,0:T(8,128)S(1)}, bf16[4,128,256]{2,1,0:T(8,128)(2,1)S(1)}, f32[8,128,256]{2,1,0:T(8,128)S(1)}, bf16[8,128,256]{2,1,0:T(8,128...) custom-call(s32[24]{0:T(128)S(1)} %get-tuple-element.77.first_ref, ...), custom_call_target="tpu_custom_call" | custom-call | tf_op jit(solution)/shard_map/pallas_call | solution.py:111
  111.2 1.1 collective-permute-start.32
  112.3 3.6 %collective-permute-start.33 = (bf16[8,128,256]{2,1,0:T(8,128)(2,1)S(1)}, bf16[8,128,256]{2,1,0:T(8,128)(2,1)S(1)}, u32[]{:S(2)}, u32[]{:S(2)}) collective-permute-start(bf16[8,128,256]{2,1,0:T(8,128)(2,1)S(1)} %get-tuple-element.43), channel_id=1, source_target_pairs={{0,2},{1,3},{2,0},{3,1},{4,6},{5,7},{6,4},{7,5},{8,10},{9,11},{10,... | collective-permute-start | bytes 1572872 | tf_op jit(solution)/shard_map/ppermute | solution.py:47
  115.9 1.3 collective-permute-start.34
  117.3 3.1 %collective-permute-start.36 = (bf16[128,256]{1,0:T(8,128)(2,1)S(1)}, bf16[128,256]{1,0:T(8,128)(2,1)S(1)}, u32[]{:S(2)}, u32[]{:S(2)}) collective-permute-start(bf16[128,256]{1,0:T(8,128)(2,1)S(1)} %get-tuple-element.63), channel_id=1, source_target_pairs={{0,64},{1,65},{2,66},{3,67},{4,68},{5,69},{6,70},{7,71},{8,72},{9,... | collective-permute-start | bytes 196616 | tf_op jit(solution)/shard_map/ppermute | solution.py:47
  120.4 0.8 collective-permute-start.38
  121.2 2.7 %collective-permute-done.36 = bf16[128,256]{1,0:T(8,128)(2,1)S(1)} collective-permute-done((bf16[128,256]{1,0:T(8,128)(2,1)S(1)}, bf16[128,256]{1,0:T(8,128)(2,1)S(1)}, u32[]{:S(2)}, u32[]{:S(2)}) %collective-permute-start.36) | collective-permute-done | bytes 65568 | tf_op jit(solution)/shard_map/ppermute | solution.py:47
  123.9 3.3 %collective-permute-start.37 = (bf16[128,256]{1,0:T(8,128)(2,1)S(1)}, bf16[128,256]{1,0:T(8,128)(2,1)S(1)}, u32[]{:S(2)}, u32[]{:S(2)}) collective-permute-start(bf16[128,256]{1,0:T(8,128)(2,1)S(1)} %get-tuple-element.65), channel_id=1, source_target_pairs={{0,128},{1,129},{2,130},{3,131},{4,132},{5,133},{6,134},{7,135},{8... | collective-permute-start | bytes 196616 | tf_op jit(solution)/shard_map/ppermute | solution.py:47
  127.2 2.9 %collective-permute-done.37 = bf16[128,256]{1,0:T(8,128)(2,1)S(1)} collective-permute-done((bf16[128,256]{1,0:T(8,128)(2,1)S(1)}, bf16[128,256]{1,0:T(8,128)(2,1)S(1)}, u32[]{:S(2)}, u32[]{:S(2)}) %collective-permute-start.37) | collective-permute-done | bytes 65568 | tf_op jit(solution)/shard_map/ppermute | solution.py:47
  130.5 0.8 collective-permute-start.39
  131.3 2.5 %collective-permute-start.41 = (bf16[2,128,256]{2,1,0:T(8,128)(2,1)S(1)}, bf16[2,128,256]{2,1,0:T(8,128)(2,1)S(1)}, u32[]{:S(2)}, u32[]{:S(2)}) collective-permute-start(bf16[2,128,256]{2,1,0:T(8,128)(2,1)S(1)} %get-tuple-element.58), channel_id=1, source_target_pairs={{0,24},{1,25},{2,26},{3,27},{4,28},{5,29},{6,30},{7,31},{8,0},{9,1... | collective-permute-start | bytes 393224 | tf_op jit(solution)/shard_map/ppermute | solution.py:47
  133.8 1.3 collective-permute-start.40
  135.1 1.6 %collective-permute-done.39 = bf16[2,128,256]{2,1,0:T(8,128)(2,1)S(1)} collective-permute-done((bf16[2,128,256]{2,1,0:T(8,128)(2,1)S(1)}, bf16[2,128,256]{2,1,0:T(8,128)(2,1)S(1)}, u32[]{:S(2)}, u32[]{:S(2)}) %collective-permute-start.39) | collective-permute-done | bytes 131104 | tf_op jit(solution)/shard_map/ppermute | solution.py:47
  136.8 1.0 collective-permute-done.41
  137.7 2.5 %collective-permute-done.40 = bf16[2,128,256]{2,1,0:T(8,128)(2,1)S(1)} collective-permute-done((bf16[2,128,256]{2,1,0:T(8,128)(2,1)S(1)}, bf16[2,128,256]{2,1,0:T(8,128)(2,1)S(1)}, u32[]{:S(2)}, u32[]{:S(2)}) %collective-permute-start.40) | collective-permute-done | bytes 131104 | tf_op jit(solution)/shard_map/ppermute | solution.py:47
  140.4 5.3 %collective-permute-start.42 = (bf16[128,256]{1,0:T(8,128)(2,1)S(1)}, bf16[128,256]{1,0:T(8,128)(2,1)S(1)}, u32[]{:S(2)}, u32[]{:S(2)}) collective-permute-start(bf16[128,256]{1,0:T(8,128)(2,1)S(1)} %fusion.12), channel_id=1, source_target_pairs={{0,4},{1,5},{2,6},{3,7},{4,0},{5,1},{6,2},{7,3},{8,12},{9,13},{10,... | collective-permute-start | bytes 196616 | tf_op jit(solution)/shard_map/ppermute | solution.py:47
  145.7 2.9 %collective-permute-done.42 = bf16[128,256]{1,0:T(8,128)(2,1)S(1)} collective-permute-done((bf16[128,256]{1,0:T(8,128)(2,1)S(1)}, bf16[128,256]{1,0:T(8,128)(2,1)S(1)}, u32[]{:S(2)}, u32[]{:S(2)}) %collective-permute-start.42) | collective-permute-done | bytes 65568 | tf_op jit(solution)/shard_map/ppermute | solution.py:47
  148.7 0.7 fusion.10
  (68 shorter events, 2.6 us)
Async XLA Ops:
  0.0 11.3 %copy-start.3 = (bf16[128,256]{1,0:T(8,128)(2,1)S(1)}, bf16[128,256]{1,0:T(8,128)(2,1)}, u32[]{:S(2)}) copy-start(bf16[128,256]{1,0:T(8,128)(2,1)} %param.6) | copy-start | bytes 196612
  0.0 39.5 %copy-start = (bf16[24,128,128]{2,1,0:T(8,128)(2,1)S(1)}, bf16[24,128,128]{2,1,0:T(8,128)(2,1)}, u32[]{:S(2)}) copy-start(bf16[24,128,128]{2,1,0:T(8,128)(2,1)} %wins.3) | copy-start | bytes 2359300
  0.0 9.9 %collective-permute-start = (bf16[128,256]{1,0:T(8,128)(2,1)}, bf16[128,256]{1,0:T(8,128)(2,1)S(1)}, u32[]{:S(2)}, u32[]{:S(2)}) collective-permute-start(bf16[128,256]{1,0:T(8,128)(2,1)} %param.6), channel_id=1, source_target_pairs={{0,4},{1,5},{2,6},{3,7},{4,0},{5,1},{6,2},{7,3},{8,12},{9,13},{10,... | collective-permute-start | bytes 196616 | tf_op jit(solution)/shard_map/ppermute | solution.py:47
  9.9 1.5 collective-permute-start.4
  11.4 8.1 %collective-permute-start.2 = (bf16[2,128,256]{2,1,0:T(8,128)(2,1)S(1)}, bf16[2,128,256]{2,1,0:T(8,128)(2,1)S(1)}, u32[]{:S(2)}, u32[]{:S(2)}) collective-permute-start(bf16[2,128,256]{2,1,0:T(8,128)(2,1)S(1)} %get-tuple-element.76), channel_id=1, source_target_pairs={{0,16},{1,17},{2,18},{3,19},{4,20},{5,21},{6,22},{7,23},{8,24},{9,... | collective-permute-start | bytes 393224 | tf_op jit(solution)/shard_map/ppermute | solution.py:47
  14.5 5.0 %collective-permute-start.1 = (bf16[2,128,256]{2,1,0:T(8,128)(2,1)S(1)}, bf16[2,128,256]{2,1,0:T(8,128)(2,1)S(1)}, u32[]{:S(2)}, u32[]{:S(2)}) collective-permute-start(bf16[2,128,256]{2,1,0:T(8,128)(2,1)S(1)} %get-tuple-element.76), channel_id=1, source_target_pairs={{0,24},{1,25},{2,26},{3,27},{4,28},{5,29},{6,30},{7,31},{8,0},{9,1... | collective-permute-start | bytes 393224 | tf_op jit(solution)/shard_map/ppermute | solution.py:47
  15.6 6.2 %collective-permute-start.3 = (bf16[2,128,256]{2,1,0:T(8,128)(2,1)S(1)}, bf16[2,128,256]{2,1,0:T(8,128)(2,1)S(1)}, u32[]{:S(2)}, u32[]{:S(2)}) collective-permute-start(bf16[2,128,256]{2,1,0:T(8,128)(2,1)S(1)} %get-tuple-element.76), channel_id=1, source_target_pairs={{0,8},{1,9},{2,10},{3,11},{4,12},{5,13},{6,14},{7,15},{8,16},{9,17... | collective-permute-start | bytes 393224 | tf_op jit(solution)/shard_map/ppermute | solution.py:47
  21.8 17.7 %collective-permute-start.10 = (bf16[8,128,256]{2,1,0:T(8,128)(2,1)S(1)}, bf16[8,128,256]{2,1,0:T(8,128)(2,1)S(1)}, u32[]{:S(2)}, u32[]{:S(2)}) collective-permute-start(bf16[8,128,256]{2,1,0:T(8,128)(2,1)S(1)} %constant_dynamic-update-slice_fusion.v0), channel_id=1, source_target_pairs={{0,1},{1,2},{2,3},{3,0},{4,5},{5,6},{6,7},{7,4},{8,9},{9,10},{10,1... | collective-permute-start | bytes 1572872 | tf_op jit(solution)/shard_map/ppermute | solution.py:47
  23.5 16.0 %collective-permute-start.9 = (bf16[8,128,256]{2,1,0:T(8,128)(2,1)S(1)}, bf16[8,128,256]{2,1,0:T(8,128)(2,1)S(1)}, u32[]{:S(2)}, u32[]{:S(2)}) collective-permute-start(bf16[8,128,256]{2,1,0:T(8,128)(2,1)S(1)} %constant_dynamic-update-slice_fusion.v0), channel_id=1, source_target_pairs={{0,2},{1,3},{2,0},{3,1},{4,6},{5,7},{6,4},{7,5},{8,10},{9,11},{10,... | collective-permute-start | bytes 1572872 | tf_op jit(solution)/shard_map/ppermute | solution.py:47
  24.4 15.1 %collective-permute-start.8 = (bf16[8,128,256]{2,1,0:T(8,128)(2,1)S(1)}, bf16[8,128,256]{2,1,0:T(8,128)(2,1)S(1)}, u32[]{:S(2)}, u32[]{:S(2)}) collective-permute-start(bf16[8,128,256]{2,1,0:T(8,128)(2,1)S(1)} %constant_dynamic-update-slice_fusion.v0), channel_id=1, source_target_pairs={{0,3},{1,0},{2,1},{3,2},{4,7},{5,4},{6,5},{7,6},{8,11},{9,8},{10,9... | collective-permute-start | bytes 1572872 | tf_op jit(solution)/shard_map/ppermute | solution.py:47
  26.8 7.7 %collective-permute-start.7 = (bf16[2,128,256]{2,1,0:T(8,128)(2,1)S(1)}, bf16[2,128,256]{2,1,0:T(8,128)(2,1)S(1)}, u32[]{:S(2)}, u32[]{:S(2)}) collective-permute-start(bf16[2,128,256]{2,1,0:T(8,128)(2,1)S(1)} %get-tuple-element.29.u0), channel_id=1, source_target_pairs={{0,64},{1,65},{2,66},{3,67},{4,68},{5,69},{6,70},{7,71},{8,72},{9,... | collective-permute-start | bytes 393224 | tf_op jit(solution)/shard_map/ppermute | solution.py:47
  29.3 6.2 %copy-start.4 = (s32[24]{0:T(128)S(1)}, s32[24]{0:T(128)}, u32[]{:S(2)}) copy-start(s32[24]{0:T(128)} %param.7) | copy-start | bytes 292
  29.3 6.2 %copy-start.5 = (s32[24]{0:T(128)S(1)}, s32[24]{0:T(128)}, u32[]{:S(2)}) copy-start(s32[24]{0:T(128)} %param.8) | copy-start | bytes 292
  29.4 8.6 %collective-permute-start.6 = (bf16[2,128,256]{2,1,0:T(8,128)(2,1)S(1)}, bf16[2,128,256]{2,1,0:T(8,128)(2,1)S(1)}, u32[]{:S(2)}, u32[]{:S(2)}) collective-permute-start(bf16[2,128,256]{2,1,0:T(8,128)(2,1)S(1)} %get-tuple-element.29.u0), channel_id=1, source_target_pairs={{0,128},{1,129},{2,130},{3,131},{4,132},{5,133},{6,134},{7,135},{8... | collective-permute-start | bytes 393224 | tf_op jit(solution)/shard_map/ppermute | solution.py:47
  34.5 5.0 %collective-permute-start.5 = (bf16[2,128,256]{2,1,0:T(8,128)(2,1)S(1)}, bf16[2,128,256]{2,1,0:T(8,128)(2,1)S(1)}, u32[]{:S(2)}, u32[]{:S(2)}) collective-permute-start(bf16[2,128,256]{2,1,0:T(8,128)(2,1)S(1)} %get-tuple-element.29.u0), channel_id=1, source_target_pairs={{0,192},{1,193},{2,194},{3,195},{4,196},{5,197},{6,198},{7,199},{8... | collective-permute-start | bytes 393224 | tf_op jit(solution)/shard_map/ppermute | solution.py:47
  39.5 1.1 copy-start.1
  43.1 4.1 %collective-permute-start.14 = (bf16[4,128,256]{2,1,0:T(8,128)(2,1)S(1)}, bf16[4,128,256]{2,1,0:T(8,128)(2,1)S(1)}, u32[]{:S(2)}, u32[]{:S(2)}) collective-permute-start(bf16[4,128,256]{2,1,0:T(8,128)(2,1)S(1)} %get-tuple-element.36), channel_id=1, source_target_pairs={{0,32},{1,33},{2,34},{3,35},{4,36},{5,37},{6,38},{7,39},{8,40},{9,... | collective-permute-start | bytes 786440 | tf_op jit(solution)/shard_map/ppermute | solution.py:47
  43.2 18.4 %collective-permute-start.11 = (bf16[8,128,256]{2,1,0:T(8,128)(2,1)S(1)}, bf16[8,128,256]{2,1,0:T(8,128)(2,1)S(1)}, u32[]{:S(2)}, u32[]{:S(2)}) collective-permute-start(bf16[8,128,256]{2,1,0:T(8,128)(2,1)S(1)} %get-tuple-element.32), channel_id=1, source_target_pairs={{0,1},{1,2},{2,3},{3,0},{4,5},{5,6},{6,7},{7,4},{8,9},{9,10},{10,1... | collective-permute-start | bytes 1572872 | tf_op jit(solution)/shard_map/ppermute | solution.py:47
  44.6 17.0 %collective-permute-start.12 = (bf16[8,128,256]{2,1,0:T(8,128)(2,1)S(1)}, bf16[8,128,256]{2,1,0:T(8,128)(2,1)S(1)}, u32[]{:S(2)}, u32[]{:S(2)}) collective-permute-start(bf16[8,128,256]{2,1,0:T(8,128)(2,1)S(1)} %get-tuple-element.33), channel_id=1, source_target_pairs={{0,2},{1,3},{2,0},{3,1},{4,6},{5,7},{6,4},{7,5},{8,10},{9,11},{10,... | collective-permute-start | bytes 1572872 | tf_op jit(solution)/shard_map/ppermute | solution.py:47
  47.0 14.6 %collective-permute-start.13 = (bf16[8,128,256]{2,1,0:T(8,128)(2,1)S(1)}, bf16[8,128,256]{2,1,0:T(8,128)(2,1)S(1)}, u32[]{:S(2)}, u32[]{:S(2)}) collective-permute-start(bf16[8,128,256]{2,1,0:T(8,128)(2,1)S(1)} %get-tuple-element.34), channel_id=1, source_target_pairs={{0,3},{1,0},{2,1},{3,2},{4,7},{5,4},{6,5},{7,6},{8,11},{9,8},{10,9... | collective-permute-start | bytes 1572872 | tf_op jit(solution)/shard_map/ppermute | solution.py:47
  47.3 6.7 %collective-permute-start.15 = (bf16[128,256]{1,0:T(8,128)(2,1)S(1)}, bf16[128,256]{1,0:T(8,128)(2,1)S(1)}, u32[]{:S(2)}, u32[]{:S(2)}) collective-permute-start(bf16[128,256]{1,0:T(8,128)(2,1)S(1)} %get-tuple-element.68), channel_id=1, source_target_pairs={{0,64},{1,65},{2,66},{3,67},{4,68},{5,69},{6,70},{7,71},{8,72},{9,... | collective-permute-start | bytes 196616 | tf_op jit(solution)/shard_map/ppermute | solution.py:47
  50.3 8.3 %collective-permute-start.17 = (bf16[128,256]{1,0:T(8,128)(2,1)S(1)}, bf16[128,256]{1,0:T(8,128)(2,1)S(1)}, u32[]{:S(2)}, u32[]{:S(2)}) collective-permute-start(bf16[128,256]{1,0:T(8,128)(2,1)S(1)} %get-tuple-element.69), channel_id=1, source_target_pairs={{0,192},{1,193},{2,194},{3,195},{4,196},{5,197},{6,198},{7,199},{8... | collective-permute-start | bytes 196616 | tf_op jit(solution)/shard_map/ppermute | solution.py:47
  53.9 7.6 %collective-permute-start.16 = (bf16[128,256]{1,0:T(8,128)(2,1)S(1)}, bf16[128,256]{1,0:T(8,128)(2,1)S(1)}, u32[]{:S(2)}, u32[]{:S(2)}) collective-permute-start(bf16[128,256]{1,0:T(8,128)(2,1)S(1)} %get-tuple-element.70), channel_id=1, source_target_pairs={{0,128},{1,129},{2,130},{3,131},{4,132},{5,133},{6,134},{7,135},{8... | collective-permute-start | bytes 196616 | tf_op jit(solution)/shard_map/ppermute | solution.py:47
  62.0 6.3 %collective-permute-start.18 = (bf16[2,128,256]{2,1,0:T(8,128)(2,1)S(1)}, bf16[2,128,256]{2,1,0:T(8,128)(2,1)S(1)}, u32[]{:S(2)}, u32[]{:S(2)}) collective-permute-start(bf16[2,128,256]{2,1,0:T(8,128)(2,1)S(1)} %get-tuple-element.60), channel_id=1, source_target_pairs={{0,8},{1,9},{2,10},{3,11},{4,12},{5,13},{6,14},{7,15},{8,16},{9,17... | collective-permute-start | bytes 393224 | tf_op jit(solution)/shard_map/ppermute | solution.py:47
  63.2 6.1 %collective-permute-start.20 = (bf16[2,128,256]{2,1,0:T(8,128)(2,1)S(1)}, bf16[2,128,256]{2,1,0:T(8,128)(2,1)S(1)}, u32[]{:S(2)}, u32[]{:S(2)}) collective-permute-start(bf16[2,128,256]{2,1,0:T(8,128)(2,1)S(1)} %get-tuple-element.61), channel_id=1, source_target_pairs={{0,24},{1,25},{2,26},{3,27},{4,28},{5,29},{6,30},{7,31},{8,0},{9,1... | collective-permute-start | bytes 393224 | tf_op jit(solution)/shard_map/ppermute | solution.py:47
  65.3 6.5 %collective-permute-start.19 = (bf16[2,128,256]{2,1,0:T(8,128)(2,1)S(1)}, bf16[2,128,256]{2,1,0:T(8,128)(2,1)S(1)}, u32[]{:S(2)}, u32[]{:S(2)}) collective-permute-start(bf16[2,128,256]{2,1,0:T(8,128)(2,1)S(1)} %get-tuple-element.62), channel_id=1, source_target_pairs={{0,16},{1,17},{2,18},{3,19},{4,20},{5,21},{6,22},{7,23},{8,24},{9,... | collective-permute-start | bytes 393224 | tf_op jit(solution)/shard_map/ppermute | solution.py:47
  71.9 9.0 %collective-permute-start.21 = (bf16[2,128,256]{2,1,0:T(8,128)(2,1)S(1)}, bf16[2,128,256]{2,1,0:T(8,128)(2,1)S(1)}, u32[]{:S(2)}, u32[]{:S(2)}) collective-permute-start(bf16[2,128,256]{2,1,0:T(8,128)(2,1)S(1)} %pad_maximum_fusion.3), channel_id=1, source_target_pairs={{0,4},{1,5},{2,6},{3,7},{4,0},{5,1},{6,2},{7,3},{8,12},{9,13},{10,... | collective-permute-start | bytes 393224 | tf_op jit(solution)/shard_map/ppermute | solution.py:47
  81.0 27.4 %copy-start.2 = (bf16[24,128,128]{2,1,0:T(8,128)(2,1)S(1)}, bf16[24,128,128]{2,1,0:T(8,128)(2,1)}, u32[]{:S(2)}) copy-start(bf16[24,128,128]{2,1,0:T(8,128)(2,1)} %losses.3) | copy-start | bytes 2359300
  81.0 3.4 %collective-permute-start.25 = (bf16[128,256]{1,0:T(8,128)(2,1)S(1)}, bf16[128,256]{1,0:T(8,128)(2,1)S(1)}, u32[]{:S(2)}, u32[]{:S(2)}) collective-permute-start(bf16[128,256]{1,0:T(8,128)(2,1)S(1)} %get-tuple-element.74), channel_id=1, source_target_pairs={{0,32},{1,33},{2,34},{3,35},{4,36},{5,37},{6,38},{7,39},{8,40},{9,... | collective-permute-start | bytes 196616 | tf_op jit(solution)/shard_map/ppermute | solution.py:47
  81.1 7.7 %collective-permute-start.24 = (bf16[2,128,256]{2,1,0:T(8,128)(2,1)S(1)}, bf16[2,128,256]{2,1,0:T(8,128)(2,1)S(1)}, u32[]{:S(2)}, u32[]{:S(2)}) collective-permute-start(bf16[2,128,256]{2,1,0:T(8,128)(2,1)S(1)} %fusion.1), channel_id=1, source_target_pairs={{0,8},{1,9},{2,10},{3,11},{4,12},{5,13},{6,14},{7,15},{8,16},{9,17... | collective-permute-start | bytes 393224 | tf_op jit(solution)/shard_map/ppermute | solution.py:47
  81.2 7.6 %collective-permute-start.23 = (bf16[2,128,256]{2,1,0:T(8,128)(2,1)S(1)}, bf16[2,128,256]{2,1,0:T(8,128)(2,1)S(1)}, u32[]{:S(2)}, u32[]{:S(2)}) collective-permute-start(bf16[2,128,256]{2,1,0:T(8,128)(2,1)S(1)} %fusion.1), channel_id=1, source_target_pairs={{0,16},{1,17},{2,18},{3,19},{4,20},{5,21},{6,22},{7,23},{8,24},{9,... | collective-permute-start | bytes 393224 | tf_op jit(solution)/shard_map/ppermute | solution.py:47
  83.8 5.9 %collective-permute-start.22 = (bf16[2,128,256]{2,1,0:T(8,128)(2,1)S(1)}, bf16[2,128,256]{2,1,0:T(8,128)(2,1)S(1)}, u32[]{:S(2)}, u32[]{:S(2)}) collective-permute-start(bf16[2,128,256]{2,1,0:T(8,128)(2,1)S(1)} %fusion.1), channel_id=1, source_target_pairs={{0,24},{1,25},{2,26},{3,27},{4,28},{5,29},{6,30},{7,31},{8,0},{9,1... | collective-permute-start | bytes 393224 | tf_op jit(solution)/shard_map/ppermute | solution.py:47
  89.8 18.7 %collective-permute-start.31 = (bf16[8,128,256]{2,1,0:T(8,128)(2,1)S(1)}, bf16[8,128,256]{2,1,0:T(8,128)(2,1)S(1)}, u32[]{:S(2)}, u32[]{:S(2)}) collective-permute-start(bf16[8,128,256]{2,1,0:T(8,128)(2,1)S(1)} %pad_maximum_fusion.v0), channel_id=1, source_target_pairs={{0,1},{1,2},{2,3},{3,0},{4,5},{5,6},{6,7},{7,4},{8,9},{9,10},{10,1... | collective-permute-start | bytes 1572872 | tf_op jit(solution)/shard_map/ppermute | solution.py:47
  90.8 17.7 %collective-permute-start.30 = (bf16[8,128,256]{2,1,0:T(8,128)(2,1)S(1)}, bf16[8,128,256]{2,1,0:T(8,128)(2,1)S(1)}, u32[]{:S(2)}, u32[]{:S(2)}) collective-permute-start(bf16[8,128,256]{2,1,0:T(8,128)(2,1)S(1)} %pad_maximum_fusion.v0), channel_id=1, source_target_pairs={{0,2},{1,3},{2,0},{3,1},{4,6},{5,7},{6,4},{7,5},{8,10},{9,11},{10,... | collective-permute-start | bytes 1572872 | tf_op jit(solution)/shard_map/ppermute | solution.py:47
  94.3 14.1 %collective-permute-start.29 = (bf16[8,128,256]{2,1,0:T(8,128)(2,1)S(1)}, bf16[8,128,256]{2,1,0:T(8,128)(2,1)S(1)}, u32[]{:S(2)}, u32[]{:S(2)}) collective-permute-start(bf16[8,128,256]{2,1,0:T(8,128)(2,1)S(1)} %pad_maximum_fusion.v0), channel_id=1, source_target_pairs={{0,3},{1,0},{2,1},{3,2},{4,7},{5,4},{6,5},{7,6},{8,11},{9,8},{10,9... | collective-permute-start | bytes 1572872 | tf_op jit(solution)/shard_map/ppermute | solution.py:47
  95.1 7.0 %collective-permute-start.28 = (bf16[2,128,256]{2,1,0:T(8,128)(2,1)S(1)}, bf16[2,128,256]{2,1,0:T(8,128)(2,1)S(1)}, u32[]{:S(2)}, u32[]{:S(2)}) collective-permute-start(bf16[2,128,256]{2,1,0:T(8,128)(2,1)S(1)} %pad_maximum_fusion.4.u0), channel_id=1, source_target_pairs={{0,64},{1,65},{2,66},{3,67},{4,68},{5,69},{6,70},{7,71},{8,72},{9,... | collective-permute-start | bytes 393224 | tf_op jit(solution)/shard_map/ppermute | solution.py:47
  98.2 8.8 %collective-permute-start.27 = (bf16[2,128,256]{2,1,0:T(8,128)(2,1)S(1)}, bf16[2,128,256]{2,1,0:T(8,128)(2,1)S(1)}, u32[]{:S(2)}, u32[]{:S(2)}) collective-permute-start(bf16[2,128,256]{2,1,0:T(8,128)(2,1)S(1)} %pad_maximum_fusion.4.u0), channel_id=1, source_target_pairs={{0,128},{1,129},{2,130},{3,131},{4,132},{5,133},{6,134},{7,135},{8... | collective-permute-start | bytes 393224 | tf_op jit(solution)/shard_map/ppermute | solution.py:47
  102.1 6.4 %collective-permute-start.26 = (bf16[2,128,256]{2,1,0:T(8,128)(2,1)S(1)}, bf16[2,128,256]{2,1,0:T(8,128)(2,1)S(1)}, u32[]{:S(2)}, u32[]{:S(2)}) collective-permute-start(bf16[2,128,256]{2,1,0:T(8,128)(2,1)S(1)} %pad_maximum_fusion.4.u0), channel_id=1, source_target_pairs={{0,192},{1,193},{2,194},{3,195},{4,196},{5,197},{6,198},{7,199},{8... | collective-permute-start | bytes 393224 | tf_op jit(solution)/shard_map/ppermute | solution.py:47
  111.1 6.1 %collective-permute-start.35 = (bf16[4,128,256]{2,1,0:T(8,128)(2,1)S(1)}, bf16[4,128,256]{2,1,0:T(8,128)(2,1)S(1)}, u32[]{:S(2)}, u32[]{:S(2)}) collective-permute-start(bf16[4,128,256]{2,1,0:T(8,128)(2,1)S(1)} %get-tuple-element.46), channel_id=1, source_target_pairs={{0,32},{1,33},{2,34},{3,35},{4,36},{5,37},{6,38},{7,39},{8,40},{9,... | collective-permute-start | bytes 786440 | tf_op jit(solution)/shard_map/ppermute | solution.py:47
  111.2 19.0 %collective-permute-start.32 = (bf16[8,128,256]{2,1,0:T(8,128)(2,1)S(1)}, bf16[8,128,256]{2,1,0:T(8,128)(2,1)S(1)}, u32[]{:S(2)}, u32[]{:S(2)}) collective-permute-start(bf16[8,128,256]{2,1,0:T(8,128)(2,1)S(1)} %get-tuple-element.42), channel_id=1, source_target_pairs={{0,1},{1,2},{2,3},{3,0},{4,5},{5,6},{6,7},{7,4},{8,9},{9,10},{10,1... | collective-permute-start | bytes 1572872 | tf_op jit(solution)/shard_map/ppermute | solution.py:47
  112.3 17.8 %collective-permute-start.33 = (bf16[8,128,256]{2,1,0:T(8,128)(2,1)S(1)}, bf16[8,128,256]{2,1,0:T(8,128)(2,1)S(1)}, u32[]{:S(2)}, u32[]{:S(2)}) collective-permute-start(bf16[8,128,256]{2,1,0:T(8,128)(2,1)S(1)} %get-tuple-element.43), channel_id=1, source_target_pairs={{0,2},{1,3},{2,0},{3,1},{4,6},{5,7},{6,4},{7,5},{8,10},{9,11},{10,... | collective-permute-start | bytes 1572872 | tf_op jit(solution)/shard_map/ppermute | solution.py:47
  115.9 14.3 %collective-permute-start.34 = (bf16[8,128,256]{2,1,0:T(8,128)(2,1)S(1)}, bf16[8,128,256]{2,1,0:T(8,128)(2,1)S(1)}, u32[]{:S(2)}, u32[]{:S(2)}) collective-permute-start(bf16[8,128,256]{2,1,0:T(8,128)(2,1)S(1)} %get-tuple-element.44), channel_id=1, source_target_pairs={{0,3},{1,0},{2,1},{3,2},{4,7},{5,4},{6,5},{7,6},{8,11},{9,8},{10,9... | collective-permute-start | bytes 1572872 | tf_op jit(solution)/shard_map/ppermute | solution.py:47
  117.3 6.6 %collective-permute-start.36 = (bf16[128,256]{1,0:T(8,128)(2,1)S(1)}, bf16[128,256]{1,0:T(8,128)(2,1)S(1)}, u32[]{:S(2)}, u32[]{:S(2)}) collective-permute-start(bf16[128,256]{1,0:T(8,128)(2,1)S(1)} %get-tuple-element.63), channel_id=1, source_target_pairs={{0,64},{1,65},{2,66},{3,67},{4,68},{5,69},{6,70},{7,71},{8,72},{9,... | collective-permute-start | bytes 196616 | tf_op jit(solution)/shard_map/ppermute | solution.py:47
  120.4 6.8 %collective-permute-start.38 = (bf16[128,256]{1,0:T(8,128)(2,1)S(1)}, bf16[128,256]{1,0:T(8,128)(2,1)S(1)}, u32[]{:S(2)}, u32[]{:S(2)}) collective-permute-start(bf16[128,256]{1,0:T(8,128)(2,1)S(1)} %get-tuple-element.64), channel_id=1, source_target_pairs={{0,192},{1,193},{2,194},{3,195},{4,196},{5,197},{6,198},{7,199},{8... | collective-permute-start | bytes 196616 | tf_op jit(solution)/shard_map/ppermute | solution.py:47
  123.9 6.2 %collective-permute-start.37 = (bf16[128,256]{1,0:T(8,128)(2,1)S(1)}, bf16[128,256]{1,0:T(8,128)(2,1)S(1)}, u32[]{:S(2)}, u32[]{:S(2)}) collective-permute-start(bf16[128,256]{1,0:T(8,128)(2,1)S(1)} %get-tuple-element.65), channel_id=1, source_target_pairs={{0,128},{1,129},{2,130},{3,131},{4,132},{5,133},{6,134},{7,135},{8... | collective-permute-start | bytes 196616 | tf_op jit(solution)/shard_map/ppermute | solution.py:47
  130.5 6.3 %collective-permute-start.39 = (bf16[2,128,256]{2,1,0:T(8,128)(2,1)S(1)}, bf16[2,128,256]{2,1,0:T(8,128)(2,1)S(1)}, u32[]{:S(2)}, u32[]{:S(2)}) collective-permute-start(bf16[2,128,256]{2,1,0:T(8,128)(2,1)S(1)} %get-tuple-element.57), channel_id=1, source_target_pairs={{0,8},{1,9},{2,10},{3,11},{4,12},{5,13},{6,14},{7,15},{8,16},{9,17... | collective-permute-start | bytes 393224 | tf_op jit(solution)/shard_map/ppermute | solution.py:47
  131.3 6.4 %collective-permute-start.41 = (bf16[2,128,256]{2,1,0:T(8,128)(2,1)S(1)}, bf16[2,128,256]{2,1,0:T(8,128)(2,1)S(1)}, u32[]{:S(2)}, u32[]{:S(2)}) collective-permute-start(bf16[2,128,256]{2,1,0:T(8,128)(2,1)S(1)} %get-tuple-element.58), channel_id=1, source_target_pairs={{0,24},{1,25},{2,26},{3,27},{4,28},{5,29},{6,30},{7,31},{8,0},{9,1... | collective-permute-start | bytes 393224 | tf_op jit(solution)/shard_map/ppermute | solution.py:47
  133.8 6.5 %collective-permute-start.40 = (bf16[2,128,256]{2,1,0:T(8,128)(2,1)S(1)}, bf16[2,128,256]{2,1,0:T(8,128)(2,1)S(1)}, u32[]{:S(2)}, u32[]{:S(2)}) collective-permute-start(bf16[2,128,256]{2,1,0:T(8,128)(2,1)S(1)} %get-tuple-element.59), channel_id=1, source_target_pairs={{0,16},{1,17},{2,18},{3,19},{4,20},{5,21},{6,22},{7,23},{8,24},{9,... | collective-permute-start | bytes 393224 | tf_op jit(solution)/shard_map/ppermute | solution.py:47
  140.4 8.3 %collective-permute-start.42 = (bf16[128,256]{1,0:T(8,128)(2,1)S(1)}, bf16[128,256]{1,0:T(8,128)(2,1)S(1)}, u32[]{:S(2)}, u32[]{:S(2)}) collective-permute-start(bf16[128,256]{1,0:T(8,128)(2,1)S(1)} %fusion.12), channel_id=1, source_target_pairs={{0,4},{1,5},{2,6},{3,7},{4,0},{5,1},{6,2},{7,3},{8,12},{9,13},{10,... | collective-permute-start | bytes 196616 | tf_op jit(solution)/shard_map/ppermute | solution.py:47

commit v3 on v2

v3 whole, which is shorter than its diff:
```python
import functools
import itertools

import jax
import jax.numpy as jnp
from jax import lax
from jax.experimental import pallas as pl
from jax.experimental.pallas import tpu as pltpu
from jax.sharding import Mesh
from jax.sharding import PartitionSpec as P

ITERS = 2
RATE = 0.01
GROUP = 4
AXES = ("zl", "core", "x", "zh", "y")
SIZES = (4, 2, 4, 2, 4)


def permutation(move):
    pairs = []
    for source, place in enumerate(itertools.product(*[range(size) for size in SIZES])):
        place = move(dict(zip(AXES, place)))
        target = 0
        for axis, size in zip(AXES, SIZES):
            target = target * size + place[axis] % size
        pairs.append((source, target))
    return pairs


def shift(axis, by):
    def move(place):
        place[axis] += by
        return place

    return permutation(move)


def shift_by_core(axes, by):
    def move(place):
        place[axes[place["core"]]] += by
        return place

    return permutation(move)


def send(values, pairs):
    return lax.ppermute(values, AXES, pairs)


def list_slots(second_ref, live, slots, begin, end, slot_count):
    count = jnp.int32(0)
    for slot in range(slot_count):
        slots[count] = slot
        here = (second_ref[slot] >= begin) & (second_ref[slot] < end) & (slot < live)
        count = count + here.astype(jnp.int32)
    for extra in range(GROUP):
        slots[count + extra] = 0
    return count


def visit_slots(
    first_ref, second_ref, live_ref, slots, begin, end, left, turned, right, wins, losses, first_sum, second_sum
):
    count = list_slots(second_ref, live_ref[0], slots, begin, end, wins.shape[0])

    def step(turn, carry):
        work = []
        for member in range(GROUP):
            place = turn * GROUP + member
            slot = slots[place]
            p = first_ref[slot]
            q = jnp.clip(second_ref[slot] - begin, 0, end - begin - 1)
            score = lax.dot_general(
                turned[p], right[q], (((1,), (1,)), ((), ())), preferred_element_type=jnp.float32
            )
            won = wins[slot].astype(jnp.float32)
            lost = losses[slot].astype(jnp.float32)
            resid = won - (won + lost) * jax.nn.sigmoid(score)
            resid = jnp.where(place < count, resid, 0.0).astype(jnp.bfloat16)
            work.append((p, q, resid))
        grads = []
        for p, q, resid in work:
            first = jnp.dot(resid, right[q], preferred_element_type=jnp.float32)
            second = lax.dot_general(
                resid, left[p], (((0,), (0,)), ((), ())), preferred_element_type=jnp.float32
            )
            grads.append((p, q, first, second))
        for p, q, first, second in grads:
            first_sum[p] += first
            second_sum[q] += second
        return carry

    lax.fori_loop(0, (count + GROUP - 1) // GROUP, step, 0)


def own_kernel(
    first_ref, second_ref, live_ref, u0, u1, u2, u3, right, wins, losses,
    left, turned, first_sum, second_sum, slots,
):
    half = left.shape[2] // 2
    for place, part in zip((0, 1, 4, 5), (u0, u1, u2, u3)):
        here = pl.ds(place, part.shape[0])
        left[here] = part[...]
        turned[here, :, :half] = -part[:, :, half:]
        turned[here, :, half:] = part[:, :, :half]
    first_sum[...] = jnp.zeros_like(first_sum)
    second_sum[...] = jnp.zeros_like(second_sum)
    visit_slots(
        first_ref, second_ref, live_ref, slots, 0, 8, left, turned, right, wins, losses, first_sum, second_sum
    )


def rest_kernel(
    first_ref, second_ref, live_ref, left, turned, first_in, v1, v2, v3, wins, losses,
    near, far, d1, d2, d3, slots, right, first_sum, second_sum,
):
    for index, part in enumerate((v1, v2, v3)):
        right[pl.ds(8 * index, 8)] = part[...]
    first_sum[...] = first_in[...]
    second_sum[...] = jnp.zeros_like(second_sum)
    visit_slots(
        first_ref, second_ref, live_ref, slots, 8, 32, left, turned, right, wins, losses, first_sum, second_sum
    )
    for index, out in enumerate((d1, d2, d3)):
        out[...] = second_sum[pl.ds(8 * index, 8)].astype(jnp.bfloat16)
    near[...] = first_sum[:4]
    far[...] = first_sum[4:].astype(jnp.bfloat16)


def call(kernel, places, operands, outs, scratch, tile, width):
    smem = pl.BlockSpec(memory_space=pltpu.SMEM)
    vmem = pl.BlockSpec(memory_space=pltpu.VMEM)
    slot_count = operands[-1].shape[0]
    return pl.pallas_call(
        kernel,
        out_shape=[jax.ShapeDtypeStruct((count, tile, width), dtype) for count, dtype in outs],
        in_specs=[smem] * 3 + [vmem] * len(operands),
        out_specs=[vmem] * len(outs),
        scratch_shapes=[pltpu.SMEM((slot_count + GROUP,), jnp.int32)]
        + [pltpu.VMEM((count, tile, width), dtype) for count, dtype in scratch],
        compiler_params=pltpu.CompilerParams(vmem_limit_bytes=16 * 1024 * 1024),
    )(*places, *operands)


def turn_back(raw):
    half = raw.shape[-1] // 2
    return jnp.concatenate([raw[..., half:], -raw[..., :half]], axis=-1)


def total(first, parts):
    return first + sum(part.astype(jnp.float32) for part in parts)


def per_device(embedding, row_blocks, col_blocks, win_counts, loss_counts, live_tiles):
    at = {axis: lax.axis_index(axis) for axis in AXES}
    first_place = (row_blocks // 2 - at["zl"]) % 4 + (row_blocks + at["core"]) % 2 * 4
    far_x = (col_blocks // 8 - at["x"]) % 4
    far_y = (col_blocks - at["y"]) % 4
    far_z = (col_blocks // 4 + at["zh"]) % 2
    outer = jnp.where(at["core"] == 0, far_y, far_x)
    inner = jnp.where(at["core"] == 0, far_x, far_y)
    second_place = (outer * 4 + inner) * 2 + far_z
    inner_axes, outer_axes = ("x", "y"), ("y", "x")

    block = embedding
    partner = send(block, shift("zh", 1))
    pair = jnp.stack([block, partner])
    block, partner = lax.optimization_barrier((block, partner))
    for iteration in range(ITERS):
        inner_parts = {k: send(pair, shift_by_core(inner_axes, -k)) for k in (1, 3, 2)}
        inner_parts = [pair] + [inner_parts[k] for k in (1, 2, 3)]
        other = send(block, shift("core", 1))
        line = jnp.concatenate(inner_parts)
        line, block, other = lax.optimization_barrier((line, block, other))
        mine = jnp.stack([send(block, shift("zl", -k)) for k in (1, 2, 3)])
        theirs = send(mine, shift("core", 1))
        left_parts = (block[None], mine, other[None], theirs)
        right_parts = {k: send(line, shift_by_core(outer_axes, -k)) for k in (1, 3, 2)}
        right_parts = [line] + [right_parts[k] for k in (1, 2, 3)]
        places = (first_place, second_place, live_tiles)
        tile, width = block.shape
        left, turned, first_sum, line_sum = call(
            own_kernel,
            places,
            (*left_parts, right_parts[0], win_counts, loss_counts),
            [(8, jnp.bfloat16), (8, jnp.bfloat16), (8, jnp.float32), (8, jnp.float32)],
            [],
            tile,
            width,
        )
        near, far, *second = call(
            rest_kernel,
            places,
            (left, turned, first_sum, *right_parts[1:], win_counts, loss_counts),
            [(4, jnp.float32), (4, jnp.bfloat16)] + [(8, jnp.bfloat16)] * 3,
            [(24, jnp.bfloat16), (8, jnp.float32), (24, jnp.float32)],
            tile,
            width,
        )
        second = [line_sum] + second
        came = [send(second[k], shift_by_core(outer_axes, k)) for k in (2, 1, 3)]
        near = near + send(far, shift("core", 1)).astype(jnp.float32)
        near_out = near.astype(jnp.bfloat16)
        first_share = total(near[0], [send(near_out[k], shift("zl", k)) for k in (1, 2, 3)])
        line_sum = total(second[0], came)
        line_out, first_share = lax.optimization_barrier((line_sum.astype(jnp.bfloat16), first_share))
        came = [send(line_out[2 * k : 2 * k + 2], shift_by_core(inner_axes, k)) for k in (2, 1, 3)]
        pair_sum = total(line_sum[:2], came)
        own, other = first_share - pair_sum[0], -pair_sum[1]
        if iteration == ITERS - 1:
            raw = own + send(other.astype(jnp.bfloat16), shift("zh", 1)).astype(jnp.float32)
            return block.astype(jnp.float32) + RATE * turn_back(raw)
        pieces = lax.optimization_barrier(jnp.stack([other, own]).astype(jnp.bfloat16))
        raw = jnp.stack([own, other]) + send(pieces, shift("zh", 1)).astype(jnp.float32)
        pair = (pair.astype(jnp.float32) + RATE * turn_back(raw)).astype(jnp.bfloat16)
        block = pair[0]


def solution(mesh):
    fine = Mesh(mesh.devices.reshape(SIZES), AXES)
    rows = P(AXES)
    return jax.shard_map(
        per_device, mesh=fine, in_specs=(rows,) * 6, out_specs=rows, check_vma=False
    )
```

time: 152 us -> 144 us (0.947); the launches traced: 149 us -> 144 us
  starting transfers between devices: 83.9 us -> 69.6 us
  waiting for transfers between devices: 55.3 us -> 61.4 us
  Pallas kernels: 5.02 us -> 8.56 us
    ppermute x43 -> x45, starting transfers between devices: 83.9 us -> 69.6 us  [send(): return lax.ppermute(values, AXES, pairs)]
    ppermute x43 -> x45, waiting for transfers between devices: 55.3 us -> 61.4 us  [send(): return lax.ppermute(values, AXES, pairs)]
    pallas_call x2 -> x4, Pallas kernels: 5.02 us -> 8.56 us  [call(): pl.pallas_call(kernel, out_shape=[jax.ShapeDtypeStruct((count, tile, widt...]
  transfers between devices with their start and end apart: 43 -> 45, of which waited for: 24 -> 24; matrix products, arithmetic and copies ran while one was open for 1% -> 1% of each run, Pallas kernels for 0% -> 2%
where the time goes in v3:
time: 144 us
  starting transfers between devices  69.6 us (48%)
  waiting for transfers between devices  61.4 us (43%)
  Pallas kernels  8.56 us (6%)
  other arithmetic  1.96 us (1%)
  local copies, waits for them, and re-layouts  1.56 us (1%)
    ppermute x45, starting transfers between devices, send(): return lax.ppermute(values, AXES, pairs)  69.6 us
    ppermute x45, waiting for transfers between devices, send(): return lax.ppermute(values, AXES, pairs)  61.4 us
    pallas_call x4, Pallas kernels, call(): pl.pallas_call(kernel, out_shape=[jax.ShapeDtypeStruct((count, tile, widt...  8.56 us
  transfers between devices with their start and end apart: 45, of which 24 were waited for; matrix products, arithmetic and copies ran while one was open for 1% of the time, Pallas kernels for 2%

profile of v3, /device:TPU:8, one launch (start us, length us, event | category | flops | bytes accessed | tf_op | source)
XLA Modules:
  0.0 144.2 jit_solution(2619525059654084991)
XLA Ops:
  0.0 7.2 %collective-permute-start = (bf16[128,256]{1,0:T(8,128)(2,1)}, bf16[128,256]{1,0:T(8,128)(2,1)S(1)}, u32[]{:S(2)}, u32[]{:S(2)}) collective-permute-start(bf16[128,256]{1,0:T(8,128)(2,1)} %param.6), channel_id=1, source_target_pairs={{0,4},{1,5},{2,6},{3,7},{4,0},{5,1},{6,2},{7,3},{8,12},{9,13},{10,... | collective-permute-start | bytes 196616 | tf_op jit(solution)/shard_map/ppermute | solution.py:47
  7.2 0.9 constant_dynamic-update-slice_fusion.4
  8.1 1.8 %collective-permute-done = bf16[128,256]{1,0:T(8,128)(2,1)S(1)} collective-permute-done((bf16[128,256]{1,0:T(8,128)(2,1)}, bf16[128,256]{1,0:T(8,128)(2,1)S(1)}, u32[]{:S(2)}, u32[]{:S(2)}) %collective-permute-start) | collective-permute-done | bytes 65568 | tf_op jit(solution)/shard_map/ppermute | solution.py:47
  9.9 3.1 %collective-permute-start.2 = (bf16[2,128,256]{2,1,0:T(8,128)(2,1)S(1)}, bf16[2,128,256]{2,1,0:T(8,128)(2,1)S(1)}, u32[]{:S(2)}, u32[]{:S(2)}) collective-permute-start(bf16[2,128,256]{2,1,0:T(8,128)(2,1)S(1)} %pad_maximum_fusion.3), channel_id=1, source_target_pairs={{0,16},{1,17},{2,18},{3,19},{4,20},{5,21},{6,22},{7,23},{8,24},{9,... | collective-permute-start | bytes 393224 | tf_op jit(solution)/shard_map/ppermute | solution.py:47
  13.0 1.1 collective-permute-start.1
  14.1 0.9 collective-permute-start.3
  15.0 2.9 %collective-permute-done.1 = bf16[2,128,256]{2,1,0:T(8,128)(2,1)S(1)} collective-permute-done((bf16[2,128,256]{2,1,0:T(8,128)(2,1)S(1)}, bf16[2,128,256]{2,1,0:T(8,128)(2,1)S(1)}, u32[]{:S(2)}, u32[]{:S(2)}) %collective-permute-start.1) | collective-permute-done | bytes 131104 | tf_op jit(solution)/shard_map/ppermute | solution.py:47
  18.0 2.3 %collective-permute-done.3 = bf16[2,128,256]{2,1,0:T(8,128)(2,1)S(1)} collective-permute-done((bf16[2,128,256]{2,1,0:T(8,128)(2,1)S(1)}, bf16[2,128,256]{2,1,0:T(8,128)(2,1)S(1)}, u32[]{:S(2)}, u32[]{:S(2)}) %collective-permute-start.3) | collective-permute-done | bytes 131104 | tf_op jit(solution)/shard_map/ppermute | solution.py:47
  20.4 1.7 %collective-permute-start.11 = (bf16[8,128,256]{2,1,0:T(8,128)(2,1)S(1)}, bf16[8,128,256]{2,1,0:T(8,128)(2,1)S(1)}, u32[]{:S(2)}, u32[]{:S(2)}) collective-permute-start(bf16[8,128,256]{2,1,0:T(8,128)(2,1)S(1)} %constant_dynamic-update-slice_fusion.right), channel_id=1, source_target_pairs={{0,1},{1,2},{2,3},{3,0},{4,5},{5,6},{6,7},{7,4},{8,9},{9,10},{10,1... | collective-permute-start | bytes 1572872 | tf_op jit(solution)/shard_map/ppermute | solution.py:47
  22.0 0.9 collective-permute-start.10
  22.9 2.4 %collective-permute-start.9 = (bf16[8,128,256]{2,1,0:T(8,128)(2,1)S(1)}, bf16[8,128,256]{2,1,0:T(8,128)(2,1)}, u32[]{:S(2)}, u32[]{:S(2)}) collective-permute-start(bf16[8,128,256]{2,1,0:T(8,128)(2,1)S(1)} %constant_dynamic-update-slice_fusion.right), channel_id=1, source_target_pairs={{0,3},{1,0},{2,1},{3,2},{4,7},{5,4},{6,5},{7,6},{8,11},{9,8},{10,9... | collective-permute-start | bytes 1572872 | tf_op jit(solution)/shard_map/ppermute | solution.py:47
  25.4 1.9 %collective-permute-start.7 = (bf16[128,256]{1,0:T(8,128)(2,1)S(1)}, bf16[128,256]{1,0:T(8,128)(2,1)S(1)}, u32[]{:S(2)}, u32[]{:S(2)}) collective-permute-start(bf16[128,256]{1,0:T(8,128)(2,1)S(1)} %copy-done.2), channel_id=1, source_target_pairs={{0,64},{1,65},{2,66},{3,67},{4,68},{5,69},{6,70},{7,71},{8,72},{9,... | collective-permute-start | bytes 196616 | tf_op jit(solution)/shard_map/ppermute | solution.py:47
  27.2 1.8 %collective-permute-start.6 = (bf16[128,256]{1,0:T(8,128)(2,1)S(1)}, bf16[128,256]{1,0:T(8,128)(2,1)S(1)}, u32[]{:S(2)}, u32[]{:S(2)}) collective-permute-start(bf16[128,256]{1,0:T(8,128)(2,1)S(1)} %copy-done.2), channel_id=1, source_target_pairs={{0,128},{1,129},{2,130},{3,131},{4,132},{5,133},{6,134},{7,135},{8... | collective-permute-start | bytes 196616 | tf_op jit(solution)/shard_map/ppermute | solution.py:47
  29.1 2.4 %collective-permute-done.7 = bf16[128,256]{1,0:T(8,128)(2,1)S(1)} collective-permute-done((bf16[128,256]{1,0:T(8,128)(2,1)S(1)}, bf16[128,256]{1,0:T(8,128)(2,1)S(1)}, u32[]{:S(2)}, u32[]{:S(2)}) %collective-permute-start.7) | collective-permute-done | bytes 65568 | tf_op jit(solution)/shard_map/ppermute | solution.py:47
  31.4 1.7 %collective-permute-start.5 = (bf16[128,256]{1,0:T(8,128)(2,1)S(1)}, bf16[128,256]{1,0:T(8,128)(2,1)S(1)}, u32[]{:S(2)}, u32[]{:S(2)}) collective-permute-start(bf16[128,256]{1,0:T(8,128)(2,1)S(1)} %copy-done.2), channel_id=1, source_target_pairs={{0,192},{1,193},{2,194},{3,195},{4,196},{5,197},{6,198},{7,199},{8... | collective-permute-start | bytes 196616 | tf_op jit(solution)/shard_map/ppermute | solution.py:47
  33.8 1.9 %collective-permute-done.5 = bf16[128,256]{1,0:T(8,128)(2,1)S(1)} collective-permute-done((bf16[128,256]{1,0:T(8,128)(2,1)S(1)}, bf16[128,256]{1,0:T(8,128)(2,1)S(1)}, u32[]{:S(2)}, u32[]{:S(2)}) %collective-permute-start.5) | collective-permute-done | bytes 65568 | tf_op jit(solution)/shard_map/ppermute | solution.py:47
  35.8 0.5 copy-done.3
  36.4 0.9 collective-permute-done.8.u3
  37.3 1.4 shard_map.64
  38.7 3.2 %shard_map.65 = (f32[4,128,256]{2,1,0:T(8,128)S(1)}, bf16[4,128,256]{2,1,0:T(8,128)(2,1)S(1)}, bf16[8,128,256]{2,1,0:T(8,128)(2,1)S(1)}, bf16[8,128,256]{2,1,0:T(8,128)(2,1)S(1)}, bf16[8,128,256]{2,1,0:T(8,128)(2,1)S(1)}) custom-call(s32[24]{0:T(128)S(1)} %get-tuple-element.91.first_ref, s32[24]{0:T(128)S(1)} %get-tuple-element.92.second_ref, ...), custom_call_target="tpu_custom_call" | custom-call | tf_op jit(solution)/shard_map/pallas_call | solution.py:134
  41.9 0.2 collective-permute-start.15
  42.1 0.3 collective-permute-start.12
  42.4 2.0 %collective-permute-start.13 = (bf16[8,128,256]{2,1,0:T(8,128)(2,1)S(1)}, bf16[8,128,256]{2,1,0:T(8,128)(2,1)S(1)}, u32[]{:S(2)}, u32[]{:S(2)}) collective-permute-start(bf16[8,128,256]{2,1,0:T(8,128)(2,1)S(1)} %get-tuple-element.43), channel_id=1, source_target_pairs={{0,1},{1,2},{2,3},{3,0},{4,5},{5,6},{6,7},{7,4},{8,9},{9,10},{10,1... | collective-permute-start | bytes 1572872 | tf_op jit(solution)/shard_map/ppermute | solution.py:47
  44.5 1.8 %collective-permute-start.16 = (bf16[128,256]{1,0:T(8,128)(2,1)S(1)}, bf16[128,256]{1,0:T(8,128)(2,1)S(1)}, u32[]{:S(2)}, u32[]{:S(2)}) collective-permute-start(bf16[128,256]{1,0:T(8,128)(2,1)S(1)} %get-tuple-element.86), channel_id=1, source_target_pairs={{0,64},{1,65},{2,66},{3,67},{4,68},{5,69},{6,70},{7,71},{8,72},{9,... | collective-permute-start | bytes 196616 | tf_op jit(solution)/shard_map/ppermute | solution.py:47
  46.3 3.2 %collective-permute-start.18 = (bf16[128,256]{1,0:T(8,128)(2,1)S(1)}, bf16[128,256]{1,0:T(8,128)(2,1)S(1)}, u32[]{:S(2)}, u32[]{:S(2)}) collective-permute-start(bf16[128,256]{1,0:T(8,128)(2,1)S(1)} %get-tuple-element.87), channel_id=1, source_target_pairs={{0,192},{1,193},{2,194},{3,195},{4,196},{5,197},{6,198},{7,199},{8... | collective-permute-start | bytes 196616 | tf_op jit(solution)/shard_map/ppermute | solution.py:47
  49.5 2.6 %collective-permute-done.16 = bf16[128,256]{1,0:T(8,128)(2,1)S(1)} collective-permute-done((bf16[128,256]{1,0:T(8,128)(2,1)S(1)}, bf16[128,256]{1,0:T(8,128)(2,1)S(1)}, u32[]{:S(2)}, u32[]{:S(2)}) %collective-permute-start.16) | collective-permute-done | bytes 65568 | tf_op jit(solution)/shard_map/ppermute | solution.py:47
  52.1 0.3 collective-permute-start.17
  52.4 5.7 %collective-permute-done.17 = bf16[128,256]{1,0:T(8,128)(2,1)S(1)} collective-permute-done((bf16[128,256]{1,0:T(8,128)(2,1)S(1)}, bf16[128,256]{1,0:T(8,128)(2,1)S(1)}, u32[]{:S(2)}, u32[]{:S(2)}) %collective-permute-start.17) | collective-permute-done | bytes 65568 | tf_op jit(solution)/shard_map/ppermute | solution.py:47
  58.2 0.2 collective-permute-done.14
  58.4 0.3 fusion.27
  58.8 2.4 %collective-permute-start.21 = (bf16[2,128,256]{2,1,0:T(8,128)(2,1)S(1)}, bf16[2,128,256]{2,1,0:T(8,128)(2,1)S(1)}, u32[]{:S(2)}, u32[]{:S(2)}) collective-permute-start(bf16[2,128,256]{2,1,0:T(8,128)(2,1)S(1)} %get-tuple-element.77), channel_id=1, source_target_pairs={{0,24},{1,25},{2,26},{3,27},{4,28},{5,29},{6,30},{7,31},{8,0},{9,1... | collective-permute-start | bytes 393224 | tf_op jit(solution)/shard_map/ppermute | solution.py:47
  61.2 4.1 %collective-permute-done.19 = bf16[2,128,256]{2,1,0:T(8,128)(2,1)S(1)} collective-permute-done((bf16[2,128,256]{2,1,0:T(8,128)(2,1)S(1)}, bf16[2,128,256]{2,1,0:T(8,128)(2,1)S(1)}, u32[]{:S(2)}, u32[]{:S(2)}) %collective-permute-start.19) | collective-permute-done | bytes 131104 | tf_op jit(solution)/shard_map/ppermute | solution.py:47
  65.3 2.1 %collective-permute-done.20 = bf16[2,128,256]{2,1,0:T(8,128)(2,1)S(1)} collective-permute-done((bf16[2,128,256]{2,1,0:T(8,128)(2,1)S(1)}, bf16[2,128,256]{2,1,0:T(8,128)(2,1)S(1)}, u32[]{:S(2)}, u32[]{:S(2)}) %collective-permute-start.20) | collective-permute-done | bytes 131104 | tf_op jit(solution)/shard_map/ppermute | solution.py:47
  67.5 6.1 %collective-permute-start.22 = (bf16[2,128,256]{2,1,0:T(8,128)(2,1)S(1)}, bf16[2,128,256]{2,1,0:T(8,128)(2,1)S(1)}, u32[]{:S(2)}, u32[]{:S(2)}) collective-permute-start(bf16[2,128,256]{2,1,0:T(8,128)(2,1)S(1)} %pad_maximum_fusion.4), channel_id=1, source_target_pairs={{0,4},{1,5},{2,6},{3,7},{4,0},{5,1},{6,2},{7,3},{8,12},{9,13},{10,... | collective-permute-start | bytes 393224 | tf_op jit(solution)/shard_map/ppermute | solution.py:47
  73.7 4.1 %collective-permute-done.22 = bf16[2,128,256]{2,1,0:T(8,128)(2,1)S(1)} collective-permute-done((bf16[2,128,256]{2,1,0:T(8,128)(2,1)S(1)}, bf16[2,128,256]{2,1,0:T(8,128)(2,1)S(1)}, u32[]{:S(2)}, u32[]{:S(2)}) %collective-permute-start.22) | collective-permute-done | bytes 131104 | tf_op jit(solution)/shard_map/ppermute | solution.py:47
  77.9 2.1 %collective-permute-start.24 = (bf16[2,128,256]{2,1,0:T(8,128)(2,1)S(1)}, bf16[2,128,256]{2,1,0:T(8,128)(2,1)S(1)}, u32[]{:S(2)}, u32[]{:S(2)}) collective-permute-start(bf16[2,128,256]{2,1,0:T(8,128)(2,1)S(1)} %fusion.1), channel_id=1, source_target_pairs={{0,16},{1,17},{2,18},{3,19},{4,20},{5,21},{6,22},{7,23},{8,24},{9,... | collective-permute-start | bytes 393224 | tf_op jit(solution)/shard_map/ppermute | solution.py:47
  80.0 1.2 collective-permute-start.23
  81.2 4.3 %collective-permute-done.25 = bf16[2,128,256]{2,1,0:T(8,128)(2,1)S(1)} collective-permute-done((bf16[2,128,256]{2,1,0:T(8,128)(2,1)S(1)}, bf16[2,128,256]{2,1,0:T(8,128)(2,1)S(1)}, u32[]{:S(2)}, u32[]{:S(2)}) %collective-permute-start.25) | collective-permute-done | bytes 131104 | tf_op jit(solution)/shard_map/ppermute | solution.py:47
  85.5 0.9 collective-permute-done.23
  86.5 0.7 collective-permute-start.33
  87.2 3.6 %collective-permute-start.32 = (bf16[8,128,256]{2,1,0:T(8,128)(2,1)S(1)}, bf16[8,128,256]{2,1,0:T(8,128)(2,1)S(1)}, u32[]{:S(2)}, u32[]{:S(2)}) collective-permute-start(bf16[8,128,256]{2,1,0:T(8,128)(2,1)S(1)} %pad_maximum_fusion.right), channel_id=1, source_target_pairs={{0,2},{1,3},{2,0},{3,1},{4,6},{5,7},{6,4},{7,5},{8,10},{9,11},{10,... | collective-permute-start | bytes 1572872 | tf_op jit(solution)/shard_map/ppermute | solution.py:47
  90.8 2.9 %collective-permute-start.29 = (bf16[128,256]{1,0:T(8,128)(2,1)S(1)}, bf16[128,256]{1,0:T(8,128)(2,1)S(1)}, u32[]{:S(2)}, u32[]{:S(2)}) collective-permute-start(bf16[128,256]{1,0:T(8,128)(2,1)S(1)} %slice_bitcast_fusion.7), channel_id=1, source_target_pairs={{0,64},{1,65},{2,66},{3,67},{4,68},{5,69},{6,70},{7,71},{8,72},{9,... | collective-permute-start | bytes 196616 | tf_op jit(solution)/shard_map/ppermute | solution.py:47
  93.7 1.7 %collective-permute-start.28 = (bf16[128,256]{1,0:T(8,128)(2,1)S(1)}, bf16[128,256]{1,0:T(8,128)(2,1)S(1)}, u32[]{:S(2)}, u32[]{:S(2)}) collective-permute-start(bf16[128,256]{1,0:T(8,128)(2,1)S(1)} %slice_bitcast_fusion.7), channel_id=1, source_target_pairs={{0,128},{1,129},{2,130},{3,131},{4,132},{5,133},{6,134},{7,135},{8... | collective-permute-start | bytes 196616 | tf_op jit(solution)/shard_map/ppermute | solution.py:47
  95.5 2.4 %collective-permute-done.29 = bf16[128,256]{1,0:T(8,128)(2,1)S(1)} collective-permute-done((bf16[128,256]{1,0:T(8,128)(2,1)S(1)}, bf16[128,256]{1,0:T(8,128)(2,1)S(1)}, u32[]{:S(2)}, u32[]{:S(2)}) %collective-permute-start.29) | collective-permute-done | bytes 65568 | tf_op jit(solution)/shard_map/ppermute | solution.py:47
  97.8 1.3 collective-permute-start.27
  99.2 2.9 %collective-permute-done.27 = bf16[128,256]{1,0:T(8,128)(2,1)S(1)} collective-permute-done((bf16[128,256]{1,0:T(8,128)(2,1)S(1)}, bf16[128,256]{1,0:T(8,128)(2,1)S(1)}, u32[]{:S(2)}, u32[]{:S(2)}) %collective-permute-start.27) | collective-permute-done | bytes 65568 | tf_op jit(solution)/shard_map/ppermute | solution.py:47
  102.2 1.4 collective-permute-done.30.u3
  103.7 1.4 shard_map.66
  105.1 2.7 %shard_map.67 = (f32[4,128,256]{2,1,0:T(8,128)S(1)}, bf16[4,128,256]{2,1,0:T(8,128)(2,1)S(1)}, bf16[8,128,256]{2,1,0:T(8,128)(2,1)S(1)}, bf16[8,128,256]{2,1,0:T(8,128)(2,1)S(1)}, bf16[8,128,256]{2,1,0:T(8,128)(2,1)S(1)}) custom-call(s32[24]{0:T(128)S(1)} %get-tuple-element.91.first_ref, s32[24]{0:T(128)S(1)} %get-tuple-element.92.second_ref, ...), custom_call_target="tpu_custom_call" | custom-call | tf_op jit(solution)/shard_map/pallas_call | solution.py:134
  107.7 0.2 collective-permute-start.37
  108.0 0.7 collective-permute-start.34
  108.6 1.7 %collective-permute-start.35 = (bf16[8,128,256]{2,1,0:T(8,128)(2,1)S(1)}, bf16[8,128,256]{2,1,0:T(8,128)(2,1)S(1)}, u32[]{:S(2)}, u32[]{:S(2)}) collective-permute-start(bf16[8,128,256]{2,1,0:T(8,128)(2,1)S(1)} %get-tuple-element.57), channel_id=1, source_target_pairs={{0,1},{1,2},{2,3},{3,0},{4,5},{5,6},{6,7},{7,4},{8,9},{9,10},{10,1... | collective-permute-start | bytes 1572872 | tf_op jit(solution)/shard_map/ppermute | solution.py:47
  110.3 2.1 %collective-permute-start.36 = (bf16[8,128,256]{2,1,0:T(8,128)(2,1)S(1)}, bf16[8,128,256]{2,1,0:T(8,128)(2,1)S(1)}, u32[]{:S(2)}, u32[]{:S(2)}) collective-permute-start(bf16[8,128,256]{2,1,0:T(8,128)(2,1)S(1)} %get-tuple-element.58), channel_id=1, source_target_pairs={{0,3},{1,0},{2,1},{3,2},{4,7},{5,4},{6,5},{7,6},{8,11},{9,8},{10,9... | collective-permute-start | bytes 1572872 | tf_op jit(solution)/shard_map/ppermute | solution.py:47
  112.6 4.2 %collective-permute-start.40 = (bf16[128,256]{1,0:T(8,128)(2,1)S(1)}, bf16[128,256]{1,0:T(8,128)(2,1)S(1)}, u32[]{:S(2)}, u32[]{:S(2)}) collective-permute-start(bf16[128,256]{1,0:T(8,128)(2,1)S(1)} %get-tuple-element.80), channel_id=1, source_target_pairs={{0,192},{1,193},{2,194},{3,195},{4,196},{5,197},{6,198},{7,199},{8... | collective-permute-start | bytes 196616 | tf_op jit(solution)/shard_map/ppermute | solution.py:47
  116.8 2.9 %collective-permute-done.38 = bf16[128,256]{1,0:T(8,128)(2,1)S(1)} collective-permute-done((bf16[128,256]{1,0:T(8,128)(2,1)S(1)}, bf16[128,256]{1,0:T(8,128)(2,1)S(1)}, u32[]{:S(2)}, u32[]{:S(2)}) %collective-permute-start.38) | collective-permute-done | bytes 65568 | tf_op jit(solution)/shard_map/ppermute | solution.py:47
  119.8 5.0 %collective-permute-done.39 = bf16[128,256]{1,0:T(8,128)(2,1)S(1)} collective-permute-done((bf16[128,256]{1,0:T(8,128)(2,1)S(1)}, bf16[128,256]{1,0:T(8,128)(2,1)S(1)}, u32[]{:S(2)}, u32[]{:S(2)}) %collective-permute-start.39) | collective-permute-done | bytes 65568 | tf_op jit(solution)/shard_map/ppermute | solution.py:47
  124.9 0.3 collective-permute-done.35
  125.2 0.3 fusion.23
  125.7 3.2 %collective-permute-start.43 = (bf16[2,128,256]{2,1,0:T(8,128)(2,1)S(1)}, bf16[2,128,256]{2,1,0:T(8,128)(2,1)S(1)}, u32[]{:S(2)}, u32[]{:S(2)}) collective-permute-start(bf16[2,128,256]{2,1,0:T(8,128)(2,1)S(1)} %get-tuple-element.74), channel_id=1, source_target_pairs={{0,24},{1,25},{2,26},{3,27},{4,28},{5,29},{6,30},{7,31},{8,0},{9,1... | collective-permute-start | bytes 393224 | tf_op jit(solution)/shard_map/ppermute | solution.py:47
  128.9 3.2 %collective-permute-done.41 = bf16[2,128,256]{2,1,0:T(8,128)(2,1)S(1)} collective-permute-done((bf16[2,128,256]{2,1,0:T(8,128)(2,1)S(1)}, bf16[2,128,256]{2,1,0:T(8,128)(2,1)S(1)}, u32[]{:S(2)}, u32[]{:S(2)}) %collective-permute-start.41) | collective-permute-done | bytes 131104 | tf_op jit(solution)/shard_map/ppermute | solution.py:47
  132.1 3.0 %collective-permute-done.42 = bf16[2,128,256]{2,1,0:T(8,128)(2,1)S(1)} collective-permute-done((bf16[2,128,256]{2,1,0:T(8,128)(2,1)S(1)}, bf16[2,128,256]{2,1,0:T(8,128)(2,1)S(1)}, u32[]{:S(2)}, u32[]{:S(2)}) %collective-permute-start.42) | collective-permute-done | bytes 131104 | tf_op jit(solution)/shard_map/ppermute | solution.py:47
  135.2 4.3 %collective-permute-start.44 = (bf16[128,256]{1,0:T(8,128)(2,1)S(1)}, bf16[128,256]{1,0:T(8,128)(2,1)S(1)}, u32[]{:S(2)}, u32[]{:S(2)}) collective-permute-start(bf16[128,256]{1,0:T(8,128)(2,1)S(1)} %fusion.10), channel_id=1, source_target_pairs={{0,4},{1,5},{2,6},{3,7},{4,0},{5,1},{6,2},{7,3},{8,12},{9,13},{10,... | collective-permute-start | bytes 196616 | tf_op jit(solution)/shard_map/ppermute | solution.py:47
  139.4 4.0 %collective-permute-done.44 = bf16[128,256]{1,0:T(8,128)(2,1)S(1)} collective-permute-done((bf16[128,256]{1,0:T(8,128)(2,1)S(1)}, bf16[128,256]{1,0:T(8,128)(2,1)S(1)}, u32[]{:S(2)}, u32[]{:S(2)}) %collective-permute-start.44) | collective-permute-done | bytes 65568 | tf_op jit(solution)/shard_map/ppermute | solution.py:47
  143.5 0.7 fusion.9
  (73 shorter events, 1.7 us)
Async XLA Ops:
  0.0 9.9 %copy-start.2 = (bf16[128,256]{1,0:T(8,128)(2,1)S(1)}, bf16[128,256]{1,0:T(8,128)(2,1)}, u32[]{:S(2)}) copy-start(bf16[128,256]{1,0:T(8,128)(2,1)} %param.6) | copy-start | bytes 196612
  0.0 9.9 %collective-permute-start = (bf16[128,256]{1,0:T(8,128)(2,1)}, bf16[128,256]{1,0:T(8,128)(2,1)S(1)}, u32[]{:S(2)}, u32[]{:S(2)}) collective-permute-start(bf16[128,256]{1,0:T(8,128)(2,1)} %param.6), channel_id=1, source_target_pairs={{0,4},{1,5},{2,6},{3,7},{4,0},{5,1},{6,2},{7,3},{8,12},{9,13},{10,... | collective-permute-start | bytes 196616 | tf_op jit(solution)/shard_map/ppermute | solution.py:47
  9.9 27.4 %copy-start = (bf16[24,128,128]{2,1,0:T(8,128)(2,1)S(1)}, bf16[24,128,128]{2,1,0:T(8,128)(2,1)}, u32[]{:S(2)}) copy-start(bf16[24,128,128]{2,1,0:T(8,128)(2,1)} %wins.7) | copy-start | bytes 2359300
  9.9 27.4 %copy-start.1 = (bf16[24,128,128]{2,1,0:T(8,128)(2,1)S(1)}, bf16[24,128,128]{2,1,0:T(8,128)(2,1)}, u32[]{:S(2)}) copy-start(bf16[24,128,128]{2,1,0:T(8,128)(2,1)} %losses.7) | copy-start | bytes 2359300
  9.9 8.1 %collective-permute-start.2 = (bf16[2,128,256]{2,1,0:T(8,128)(2,1)S(1)}, bf16[2,128,256]{2,1,0:T(8,128)(2,1)S(1)}, u32[]{:S(2)}, u32[]{:S(2)}) collective-permute-start(bf16[2,128,256]{2,1,0:T(8,128)(2,1)S(1)} %pad_maximum_fusion.3), channel_id=1, source_target_pairs={{0,16},{1,17},{2,18},{3,19},{4,20},{5,21},{6,22},{7,23},{8,24},{9,... | collective-permute-start | bytes 393224 | tf_op jit(solution)/shard_map/ppermute | solution.py:47
  13.0 5.0 %collective-permute-start.1 = (bf16[2,128,256]{2,1,0:T(8,128)(2,1)S(1)}, bf16[2,128,256]{2,1,0:T(8,128)(2,1)S(1)}, u32[]{:S(2)}, u32[]{:S(2)}) collective-permute-start(bf16[2,128,256]{2,1,0:T(8,128)(2,1)S(1)} %pad_maximum_fusion.3), channel_id=1, source_target_pairs={{0,24},{1,25},{2,26},{3,27},{4,28},{5,29},{6,30},{7,31},{8,0},{9,1... | collective-permute-start | bytes 393224 | tf_op jit(solution)/shard_map/ppermute | solution.py:47
  14.1 6.2 %collective-permute-start.3 = (bf16[2,128,256]{2,1,0:T(8,128)(2,1)S(1)}, bf16[2,128,256]{2,1,0:T(8,128)(2,1)S(1)}, u32[]{:S(2)}, u32[]{:S(2)}) collective-permute-start(bf16[2,128,256]{2,1,0:T(8,128)(2,1)S(1)} %pad_maximum_fusion.3), channel_id=1, source_target_pairs={{0,8},{1,9},{2,10},{3,11},{4,12},{5,13},{6,14},{7,15},{8,16},{9,17... | collective-permute-start | bytes 393224 | tf_op jit(solution)/shard_map/ppermute | solution.py:47
  15.0 5.3 %collective-permute-start.4 = (bf16[128,256]{1,0:T(8,128)(2,1)S(1)}, bf16[128,256]{1,0:T(8,128)(2,1)S(1)}, u32[]{:S(2)}, u32[]{:S(2)}) collective-permute-start(bf16[128,256]{1,0:T(8,128)(2,1)S(1)} %copy-done.2), channel_id=1, source_target_pairs={{0,32},{1,33},{2,34},{3,35},{4,36},{5,37},{6,38},{7,39},{8,40},{9,... | collective-permute-start | bytes 196616 | tf_op jit(solution)/shard_map/ppermute | solution.py:47
  20.4 18.3 %collective-permute-start.11 = (bf16[8,128,256]{2,1,0:T(8,128)(2,1)S(1)}, bf16[8,128,256]{2,1,0:T(8,128)(2,1)S(1)}, u32[]{:S(2)}, u32[]{:S(2)}) collective-permute-start(bf16[8,128,256]{2,1,0:T(8,128)(2,1)S(1)} %constant_dynamic-update-slice_fusion.right), channel_id=1, source_target_pairs={{0,1},{1,2},{2,3},{3,0},{4,5},{5,6},{6,7},{7,4},{8,9},{9,10},{10,1... | collective-permute-start | bytes 1572872 | tf_op jit(solution)/shard_map/ppermute | solution.py:47
  22.0 16.6 %collective-permute-start.10 = (bf16[8,128,256]{2,1,0:T(8,128)(2,1)S(1)}, bf16[8,128,256]{2,1,0:T(8,128)(2,1)S(1)}, u32[]{:S(2)}, u32[]{:S(2)}) collective-permute-start(bf16[8,128,256]{2,1,0:T(8,128)(2,1)S(1)} %constant_dynamic-update-slice_fusion.right), channel_id=1, source_target_pairs={{0,2},{1,3},{2,0},{3,1},{4,6},{5,7},{6,4},{7,5},{8,10},{9,11},{10,... | collective-permute-start | bytes 1572872 | tf_op jit(solution)/shard_map/ppermute | solution.py:47
  22.9 15.7 %collective-permute-start.9 = (bf16[8,128,256]{2,1,0:T(8,128)(2,1)S(1)}, bf16[8,128,256]{2,1,0:T(8,128)(2,1)}, u32[]{:S(2)}, u32[]{:S(2)}) collective-permute-start(bf16[8,128,256]{2,1,0:T(8,128)(2,1)S(1)} %constant_dynamic-update-slice_fusion.right), channel_id=1, source_target_pairs={{0,3},{1,0},{2,1},{3,2},{4,7},{5,4},{6,5},{7,6},{8,11},{9,8},{10,9... | collective-permute-start | bytes 1572872 | tf_op jit(solution)/shard_map/ppermute | solution.py:47
  25.4 6.1 %collective-permute-start.7 = (bf16[128,256]{1,0:T(8,128)(2,1)S(1)}, bf16[128,256]{1,0:T(8,128)(2,1)S(1)}, u32[]{:S(2)}, u32[]{:S(2)}) collective-permute-start(bf16[128,256]{1,0:T(8,128)(2,1)S(1)} %copy-done.2), channel_id=1, source_target_pairs={{0,64},{1,65},{2,66},{3,67},{4,68},{5,69},{6,70},{7,71},{8,72},{9,... | collective-permute-start | bytes 196616 | tf_op jit(solution)/shard_map/ppermute | solution.py:47
  27.2 6.5 %collective-permute-start.6 = (bf16[128,256]{1,0:T(8,128)(2,1)S(1)}, bf16[128,256]{1,0:T(8,128)(2,1)S(1)}, u32[]{:S(2)}, u32[]{:S(2)}) collective-permute-start(bf16[128,256]{1,0:T(8,128)(2,1)S(1)} %copy-done.2), channel_id=1, source_target_pairs={{0,128},{1,129},{2,130},{3,131},{4,132},{5,133},{6,134},{7,135},{8... | collective-permute-start | bytes 196616 | tf_op jit(solution)/shard_map/ppermute | solution.py:47
  31.4 4.3 %collective-permute-start.5 = (bf16[128,256]{1,0:T(8,128)(2,1)S(1)}, bf16[128,256]{1,0:T(8,128)(2,1)S(1)}, u32[]{:S(2)}, u32[]{:S(2)}) collective-permute-start(bf16[128,256]{1,0:T(8,128)(2,1)S(1)} %copy-done.2), channel_id=1, source_target_pairs={{0,192},{1,193},{2,194},{3,195},{4,196},{5,197},{6,198},{7,199},{8... | collective-permute-start | bytes 196616 | tf_op jit(solution)/shard_map/ppermute | solution.py:47
  35.7 0.7 copy-start.3
  35.7 0.7 copy-start.4
  35.7 1.5 %collective-permute-start.8 = (bf16[3,128,256]{2,1,0:T(8,128)(2,1)S(1)}, bf16[3,128,256]{2,1,0:T(8,128)(2,1)S(1)}, u32[]{:S(2)}, u32[]{:S(2)}) collective-permute-start(bf16[3,128,256]{2,1,0:T(8,128)(2,1)S(1)} %pad_maximum_fusion.1.u1), channel_id=1, source_target_pairs={{0,32},{1,33},{2,34},{3,35},{4,36},{5,37},{6,38},{7,39},{8,40},{9,... | collective-permute-start | bytes 589832 | tf_op jit(solution)/shard_map/ppermute | solution.py:47
  41.9 2.5 %collective-permute-start.15 = (bf16[4,128,256]{2,1,0:T(8,128)(2,1)S(1)}, bf16[4,128,256]{2,1,0:T(8,128)(2,1)S(1)}, u32[]{:S(2)}, u32[]{:S(2)}) collective-permute-start(bf16[4,128,256]{2,1,0:T(8,128)(2,1)S(1)} %get-tuple-element.46), channel_id=1, source_target_pairs={{0,32},{1,33},{2,34},{3,35},{4,36},{5,37},{6,38},{7,39},{8,40},{9,... | collective-permute-start | bytes 786440 | tf_op jit(solution)/shard_map/ppermute | solution.py:47
  42.1 16.0 %collective-permute-start.12 = (bf16[8,128,256]{2,1,0:T(8,128)(2,1)S(1)}, bf16[8,128,256]{2,1,0:T(8,128)(2,1)S(1)}, u32[]{:S(2)}, u32[]{:S(2)}) collective-permute-start(bf16[8,128,256]{2,1,0:T(8,128)(2,1)S(1)} %get-tuple-element.42), channel_id=1, source_target_pairs={{0,2},{1,3},{2,0},{3,1},{4,6},{5,7},{6,4},{7,5},{8,10},{9,11},{10,... | collective-permute-start | bytes 1572872 | tf_op jit(solution)/shard_map/ppermute | solution.py:47
  42.4 15.8 %collective-permute-start.13 = (bf16[8,128,256]{2,1,0:T(8,128)(2,1)S(1)}, bf16[8,128,256]{2,1,0:T(8,128)(2,1)S(1)}, u32[]{:S(2)}, u32[]{:S(2)}) collective-permute-start(bf16[8,128,256]{2,1,0:T(8,128)(2,1)S(1)} %get-tuple-element.43), channel_id=1, source_target_pairs={{0,1},{1,2},{2,3},{3,0},{4,5},{5,6},{6,7},{7,4},{8,9},{9,10},{10,1... | collective-permute-start | bytes 1572872 | tf_op jit(solution)/shard_map/ppermute | solution.py:47
  44.4 14.0 %collective-permute-start.14 = (bf16[8,128,256]{2,1,0:T(8,128)(2,1)S(1)}, bf16[8,128,256]{2,1,0:T(8,128)(2,1)S(1)}, u32[]{:S(2)}, u32[]{:S(2)}) collective-permute-start(bf16[8,128,256]{2,1,0:T(8,128)(2,1)S(1)} %get-tuple-element.44), channel_id=1, source_target_pairs={{0,3},{1,0},{2,1},{3,2},{4,7},{5,4},{6,5},{7,6},{8,11},{9,8},{10,9... | collective-permute-start | bytes 1572872 | tf_op jit(solution)/shard_map/ppermute | solution.py:47
  44.5 7.6 %collective-permute-start.16 = (bf16[128,256]{1,0:T(8,128)(2,1)S(1)}, bf16[128,256]{1,0:T(8,128)(2,1)S(1)}, u32[]{:S(2)}, u32[]{:S(2)}) collective-permute-start(bf16[128,256]{1,0:T(8,128)(2,1)S(1)} %get-tuple-element.86), channel_id=1, source_target_pairs={{0,64},{1,65},{2,66},{3,67},{4,68},{5,69},{6,70},{7,71},{8,72},{9,... | collective-permute-start | bytes 196616 | tf_op jit(solution)/shard_map/ppermute | solution.py:47
  46.3 6.1 %collective-permute-start.18 = (bf16[128,256]{1,0:T(8,128)(2,1)S(1)}, bf16[128,256]{1,0:T(8,128)(2,1)S(1)}, u32[]{:S(2)}, u32[]{:S(2)}) collective-permute-start(bf16[128,256]{1,0:T(8,128)(2,1)S(1)} %get-tuple-element.87), channel_id=1, source_target_pairs={{0,192},{1,193},{2,194},{3,195},{4,196},{5,197},{6,198},{7,199},{8... | collective-permute-start | bytes 196616 | tf_op jit(solution)/shard_map/ppermute | solution.py:47
  52.1 6.0 %collective-permute-start.17 = (bf16[128,256]{1,0:T(8,128)(2,1)S(1)}, bf16[128,256]{1,0:T(8,128)(2,1)S(1)}, u32[]{:S(2)}, u32[]{:S(2)}) collective-permute-start(bf16[128,256]{1,0:T(8,128)(2,1)S(1)} %get-tuple-element.88), channel_id=1, source_target_pairs={{0,128},{1,129},{2,130},{3,131},{4,132},{5,133},{6,134},{7,135},{8... | collective-permute-start | bytes 196616 | tf_op jit(solution)/shard_map/ppermute | solution.py:47
  58.7 6.6 %collective-permute-start.19 = (bf16[2,128,256]{2,1,0:T(8,128)(2,1)S(1)}, bf16[2,128,256]{2,1,0:T(8,128)(2,1)S(1)}, u32[]{:S(2)}, u32[]{:S(2)}) collective-permute-start(bf16[2,128,256]{2,1,0:T(8,128)(2,1)S(1)} %get-tuple-element.76), channel_id=1, source_target_pairs={{0,16},{1,17},{2,18},{3,19},{4,20},{5,21},{6,22},{7,23},{8,24},{9,... | collective-permute-start | bytes 393224 | tf_op jit(solution)/shard_map/ppermute | solution.py:47
  58.8 6.5 %collective-permute-start.21 = (bf16[2,128,256]{2,1,0:T(8,128)(2,1)S(1)}, bf16[2,128,256]{2,1,0:T(8,128)(2,1)S(1)}, u32[]{:S(2)}, u32[]{:S(2)}) collective-permute-start(bf16[2,128,256]{2,1,0:T(8,128)(2,1)S(1)} %get-tuple-element.77), channel_id=1, source_target_pairs={{0,24},{1,25},{2,26},{3,27},{4,28},{5,29},{6,30},{7,31},{8,0},{9,1... | collective-permute-start | bytes 393224 | tf_op jit(solution)/shard_map/ppermute | solution.py:47
  61.2 6.2 %collective-permute-start.20 = (bf16[2,128,256]{2,1,0:T(8,128)(2,1)S(1)}, bf16[2,128,256]{2,1,0:T(8,128)(2,1)S(1)}, u32[]{:S(2)}, u32[]{:S(2)}) collective-permute-start(bf16[2,128,256]{2,1,0:T(8,128)(2,1)S(1)} %get-tuple-element.78), channel_id=1, source_target_pairs={{0,8},{1,9},{2,10},{3,11},{4,12},{5,13},{6,14},{7,15},{8,16},{9,17... | collective-permute-start | bytes 393224 | tf_op jit(solution)/shard_map/ppermute | solution.py:47
  67.5 10.2 %collective-permute-start.22 = (bf16[2,128,256]{2,1,0:T(8,128)(2,1)S(1)}, bf16[2,128,256]{2,1,0:T(8,128)(2,1)S(1)}, u32[]{:S(2)}, u32[]{:S(2)}) collective-permute-start(bf16[2,128,256]{2,1,0:T(8,128)(2,1)S(1)} %pad_maximum_fusion.4), channel_id=1, source_target_pairs={{0,4},{1,5},{2,6},{3,7},{4,0},{5,1},{6,2},{7,3},{8,12},{9,13},{10,... | collective-permute-start | bytes 393224 | tf_op jit(solution)/shard_map/ppermute | solution.py:47
  77.8 7.7 %collective-permute-start.25 = (bf16[2,128,256]{2,1,0:T(8,128)(2,1)S(1)}, bf16[2,128,256]{2,1,0:T(8,128)(2,1)S(1)}, u32[]{:S(2)}, u32[]{:S(2)}) collective-permute-start(bf16[2,128,256]{2,1,0:T(8,128)(2,1)S(1)} %fusion.1), channel_id=1, source_target_pairs={{0,8},{1,9},{2,10},{3,11},{4,12},{5,13},{6,14},{7,15},{8,16},{9,17... | collective-permute-start | bytes 393224 | tf_op jit(solution)/shard_map/ppermute | solution.py:47
  77.9 7.6 %collective-permute-start.24 = (bf16[2,128,256]{2,1,0:T(8,128)(2,1)S(1)}, bf16[2,128,256]{2,1,0:T(8,128)(2,1)S(1)}, u32[]{:S(2)}, u32[]{:S(2)}) collective-permute-start(bf16[2,128,256]{2,1,0:T(8,128)(2,1)S(1)} %fusion.1), channel_id=1, source_target_pairs={{0,16},{1,17},{2,18},{3,19},{4,20},{5,21},{6,22},{7,23},{8,24},{9,... | collective-permute-start | bytes 393224 | tf_op jit(solution)/shard_map/ppermute | solution.py:47
  80.0 6.4 %collective-permute-start.23 = (bf16[2,128,256]{2,1,0:T(8,128)(2,1)S(1)}, bf16[2,128,256]{2,1,0:T(8,128)(2,1)S(1)}, u32[]{:S(2)}, u32[]{:S(2)}) collective-permute-start(bf16[2,128,256]{2,1,0:T(8,128)(2,1)S(1)} %fusion.1), channel_id=1, source_target_pairs={{0,24},{1,25},{2,26},{3,27},{4,28},{5,29},{6,30},{7,31},{8,0},{9,1... | collective-permute-start | bytes 393224 | tf_op jit(solution)/shard_map/ppermute | solution.py:47
  81.1 5.3 %collective-permute-start.26 = (bf16[128,256]{1,0:T(8,128)(2,1)S(1)}, bf16[128,256]{1,0:T(8,128)(2,1)S(1)}, u32[]{:S(2)}, u32[]{:S(2)}) collective-permute-start(bf16[128,256]{1,0:T(8,128)(2,1)S(1)} %slice_bitcast_fusion.7), channel_id=1, source_target_pairs={{0,32},{1,33},{2,34},{3,35},{4,36},{5,37},{6,38},{7,39},{8,40},{9,... | collective-permute-start | bytes 196616 | tf_op jit(solution)/shard_map/ppermute | solution.py:47
  86.5 18.6 %collective-permute-start.33 = (bf16[8,128,256]{2,1,0:T(8,128)(2,1)S(1)}, bf16[8,128,256]{2,1,0:T(8,128)(2,1)S(1)}, u32[]{:S(2)}, u32[]{:S(2)}) collective-permute-start(bf16[8,128,256]{2,1,0:T(8,128)(2,1)S(1)} %pad_maximum_fusion.right), channel_id=1, source_target_pairs={{0,1},{1,2},{2,3},{3,0},{4,5},{5,6},{6,7},{7,4},{8,9},{9,10},{10,1... | collective-permute-start | bytes 1572872 | tf_op jit(solution)/shard_map/ppermute | solution.py:47
  87.2 17.9 %collective-permute-start.32 = (bf16[8,128,256]{2,1,0:T(8,128)(2,1)S(1)}, bf16[8,128,256]{2,1,0:T(8,128)(2,1)S(1)}, u32[]{:S(2)}, u32[]{:S(2)}) collective-permute-start(bf16[8,128,256]{2,1,0:T(8,128)(2,1)S(1)} %pad_maximum_fusion.right), channel_id=1, source_target_pairs={{0,2},{1,3},{2,0},{3,1},{4,6},{5,7},{6,4},{7,5},{8,10},{9,11},{10,... | collective-permute-start | bytes 1572872 | tf_op jit(solution)/shard_map/ppermute | solution.py:47
  90.8 14.3 %collective-permute-start.31 = (bf16[8,128,256]{2,1,0:T(8,128)(2,1)S(1)}, bf16[8,128,256]{2,1,0:T(8,128)(2,1)S(1)}, u32[]{:S(2)}, u32[]{:S(2)}) collective-permute-start(bf16[8,128,256]{2,1,0:T(8,128)(2,1)S(1)} %pad_maximum_fusion.right), channel_id=1, source_target_pairs={{0,3},{1,0},{2,1},{3,2},{4,7},{5,4},{6,5},{7,6},{8,11},{9,8},{10,9... | collective-permute-start | bytes 1572872 | tf_op jit(solution)/shard_map/ppermute | solution.py:47
  90.8 7.0 %collective-permute-start.29 = (bf16[128,256]{1,0:T(8,128)(2,1)S(1)}, bf16[128,256]{1,0:T(8,128)(2,1)S(1)}, u32[]{:S(2)}, u32[]{:S(2)}) collective-permute-start(bf16[128,256]{1,0:T(8,128)(2,1)S(1)} %slice_bitcast_fusion.7), channel_id=1, source_target_pairs={{0,64},{1,65},{2,66},{3,67},{4,68},{5,69},{6,70},{7,71},{8,72},{9,... | collective-permute-start | bytes 196616 | tf_op jit(solution)/shard_map/ppermute | solution.py:47
  93.7 5.5 %collective-permute-start.28 = (bf16[128,256]{1,0:T(8,128)(2,1)S(1)}, bf16[128,256]{1,0:T(8,128)(2,1)S(1)}, u32[]{:S(2)}, u32[]{:S(2)}) collective-permute-start(bf16[128,256]{1,0:T(8,128)(2,1)S(1)} %slice_bitcast_fusion.7), channel_id=1, source_target_pairs={{0,128},{1,129},{2,130},{3,131},{4,132},{5,133},{6,134},{7,135},{8... | collective-permute-start | bytes 196616 | tf_op jit(solution)/shard_map/ppermute | solution.py:47
  97.8 4.3 %collective-permute-start.27 = (bf16[128,256]{1,0:T(8,128)(2,1)S(1)}, bf16[128,256]{1,0:T(8,128)(2,1)S(1)}, u32[]{:S(2)}, u32[]{:S(2)}) collective-permute-start(bf16[128,256]{1,0:T(8,128)(2,1)S(1)} %slice_bitcast_fusion.7), channel_id=1, source_target_pairs={{0,192},{1,193},{2,194},{3,195},{4,196},{5,197},{6,198},{7,199},{8... | collective-permute-start | bytes 196616 | tf_op jit(solution)/shard_map/ppermute | solution.py:47
  102.1 1.5 %collective-permute-start.30 = (bf16[3,128,256]{2,1,0:T(8,128)(2,1)S(1)}, bf16[3,128,256]{2,1,0:T(8,128)(2,1)S(1)}, u32[]{:S(2)}, u32[]{:S(2)}) collective-permute-start(bf16[3,128,256]{2,1,0:T(8,128)(2,1)S(1)} %pad_maximum_fusion.2.u1), channel_id=1, source_target_pairs={{0,32},{1,33},{2,34},{3,35},{4,36},{5,37},{6,38},{7,39},{8,40},{9,... | collective-permute-start | bytes 589832 | tf_op jit(solution)/shard_map/ppermute | solution.py:47
  107.7 4.7 %collective-permute-start.37 = (bf16[4,128,256]{2,1,0:T(8,128)(2,1)S(1)}, bf16[4,128,256]{2,1,0:T(8,128)(2,1)S(1)}, u32[]{:S(2)}, u32[]{:S(2)}) collective-permute-start(bf16[4,128,256]{2,1,0:T(8,128)(2,1)S(1)} %get-tuple-element.60), channel_id=1, source_target_pairs={{0,32},{1,33},{2,34},{3,35},{4,36},{5,37},{6,38},{7,39},{8,40},{9,... | collective-permute-start | bytes 786440 | tf_op jit(solution)/shard_map/ppermute | solution.py:47
  108.0 16.9 %collective-permute-start.34 = (bf16[8,128,256]{2,1,0:T(8,128)(2,1)S(1)}, bf16[8,128,256]{2,1,0:T(8,128)(2,1)S(1)}, u32[]{:S(2)}, u32[]{:S(2)}) collective-permute-start(bf16[8,128,256]{2,1,0:T(8,128)(2,1)S(1)} %get-tuple-element.56), channel_id=1, source_target_pairs={{0,2},{1,3},{2,0},{3,1},{4,6},{5,7},{6,4},{7,5},{8,10},{9,11},{10,... | collective-permute-start | bytes 1572872 | tf_op jit(solution)/shard_map/ppermute | solution.py:47
  108.6 16.6 %collective-permute-start.35 = (bf16[8,128,256]{2,1,0:T(8,128)(2,1)S(1)}, bf16[8,128,256]{2,1,0:T(8,128)(2,1)S(1)}, u32[]{:S(2)}, u32[]{:S(2)}) collective-permute-start(bf16[8,128,256]{2,1,0:T(8,128)(2,1)S(1)} %get-tuple-element.57), channel_id=1, source_target_pairs={{0,1},{1,2},{2,3},{3,0},{4,5},{5,6},{6,7},{7,4},{8,9},{9,10},{10,1... | collective-permute-start | bytes 1572872 | tf_op jit(solution)/shard_map/ppermute | solution.py:47
  110.3 14.9 %collective-permute-start.36 = (bf16[8,128,256]{2,1,0:T(8,128)(2,1)S(1)}, bf16[8,128,256]{2,1,0:T(8,128)(2,1)S(1)}, u32[]{:S(2)}, u32[]{:S(2)}) collective-permute-start(bf16[8,128,256]{2,1,0:T(8,128)(2,1)S(1)} %get-tuple-element.58), channel_id=1, source_target_pairs={{0,3},{1,0},{2,1},{3,2},{4,7},{5,4},{6,5},{7,6},{8,11},{9,8},{10,9... | collective-permute-start | bytes 1572872 | tf_op jit(solution)/shard_map/ppermute | solution.py:47
  112.5 7.1 %collective-permute-start.38 = (bf16[128,256]{1,0:T(8,128)(2,1)S(1)}, bf16[128,256]{1,0:T(8,128)(2,1)S(1)}, u32[]{:S(2)}, u32[]{:S(2)}) collective-permute-start(bf16[128,256]{1,0:T(8,128)(2,1)S(1)} %get-tuple-element.79), channel_id=1, source_target_pairs={{0,64},{1,65},{2,66},{3,67},{4,68},{5,69},{6,70},{7,71},{8,72},{9,... | collective-permute-start | bytes 196616 | tf_op jit(solution)/shard_map/ppermute | solution.py:47
  112.6 7.2 %collective-permute-start.40 = (bf16[128,256]{1,0:T(8,128)(2,1)S(1)}, bf16[128,256]{1,0:T(8,128)(2,1)S(1)}, u32[]{:S(2)}, u32[]{:S(2)}) collective-permute-start(bf16[128,256]{1,0:T(8,128)(2,1)S(1)} %get-tuple-element.80), channel_id=1, source_target_pairs={{0,192},{1,193},{2,194},{3,195},{4,196},{5,197},{6,198},{7,199},{8... | collective-permute-start | bytes 196616 | tf_op jit(solution)/shard_map/ppermute | solution.py:47
  119.7 5.2 %collective-permute-start.39 = (bf16[128,256]{1,0:T(8,128)(2,1)S(1)}, bf16[128,256]{1,0:T(8,128)(2,1)S(1)}, u32[]{:S(2)}, u32[]{:S(2)}) collective-permute-start(bf16[128,256]{1,0:T(8,128)(2,1)S(1)} %get-tuple-element.81), channel_id=1, source_target_pairs={{0,128},{1,129},{2,130},{3,131},{4,132},{5,133},{6,134},{7,135},{8... | collective-permute-start | bytes 196616 | tf_op jit(solution)/shard_map/ppermute | solution.py:47
  125.6 6.6 %collective-permute-start.41 = (bf16[2,128,256]{2,1,0:T(8,128)(2,1)S(1)}, bf16[2,128,256]{2,1,0:T(8,128)(2,1)S(1)}, u32[]{:S(2)}, u32[]{:S(2)}) collective-permute-start(bf16[2,128,256]{2,1,0:T(8,128)(2,1)S(1)} %get-tuple-element.73), channel_id=1, source_target_pairs={{0,16},{1,17},{2,18},{3,19},{4,20},{5,21},{6,22},{7,23},{8,24},{9,... | collective-permute-start | bytes 393224 | tf_op jit(solution)/shard_map/ppermute | solution.py:47
  125.7 6.5 %collective-permute-start.43 = (bf16[2,128,256]{2,1,0:T(8,128)(2,1)S(1)}, bf16[2,128,256]{2,1,0:T(8,128)(2,1)S(1)}, u32[]{:S(2)}, u32[]{:S(2)}) collective-permute-start(bf16[2,128,256]{2,1,0:T(8,128)(2,1)S(1)} %get-tuple-element.74), channel_id=1, source_target_pairs={{0,24},{1,25},{2,26},{3,27},{4,28},{5,29},{6,30},{7,31},{8,0},{9,1... | collective-permute-start | bytes 393224 | tf_op jit(solution)/shard_map/ppermute | solution.py:47
  128.9 6.2 %collective-permute-start.42 = (bf16[2,128,256]{2,1,0:T(8,128)(2,1)S(1)}, bf16[2,128,256]{2,1,0:T(8,128)(2,1)S(1)}, u32[]{:S(2)}, u32[]{:S(2)}) collective-permute-start(bf16[2,128,256]{2,1,0:T(8,128)(2,1)S(1)} %get-tuple-element.75), channel_id=1, source_target_pairs={{0,8},{1,9},{2,10},{3,11},{4,12},{5,13},{6,14},{7,15},{8,16},{9,17... | collective-permute-start | bytes 393224 | tf_op jit(solution)/shard_map/ppermute | solution.py:47
  135.2 8.3 %collective-permute-start.44 = (bf16[128,256]{1,0:T(8,128)(2,1)S(1)}, bf16[128,256]{1,0:T(8,128)(2,1)S(1)}, u32[]{:S(2)}, u32[]{:S(2)}) collective-permute-start(bf16[128,256]{1,0:T(8,128)(2,1)S(1)} %fusion.10), channel_id=1, source_target_pairs={{0,4},{1,5},{2,6},{3,7},{4,0},{5,1},{6,2},{7,3},{8,12},{9,13},{10,... | collective-permute-start | bytes 196616 | tf_op jit(solution)/shard_map/ppermute | solution.py:47

commit v4 on v3

--- a/solution.py
+++ b/solution.py
@@ -11,7 +11,7 @@
 
 ITERS = 2
 RATE = 0.01
-GROUP = 4
+GROUP = 8
 AXES = ("zl", "core", "x", "zh", "y")
 SIZES = (4, 2, 4, 2, 4)
 
@@ -165,7 +165,9 @@
     block = embedding
     partner = send(block, shift("zh", 1))
     pair = jnp.stack([block, partner])
-    block, partner = lax.optimization_barrier((block, partner))
+    block, partner, first_place, second_place = lax.optimization_barrier(
+        (block, partner, first_place, second_place)
+    )
     for iteration in range(ITERS):
         inner_parts = {k: send(pair, shift_by_core(inner_axes, -k)) for k in (1, 3, 2)}
         inner_parts = [pair] + [inner_parts[k] for k in (1, 2, 3)]

time: 144 us -> 142 us (0.986)
  starting transfers between devices: 69.6 us -> 64.3 us
  waiting for transfers between devices: 61.4 us -> 64.7 us
    ppermute x45, starting transfers between devices: 69.6 us -> 64.3 us  [send(): return lax.ppermute(values, AXES, pairs)]
    ppermute x45, waiting for transfers between devices: 61.4 us -> 64.7 us  [send(): return lax.ppermute(values, AXES, pairs)]
  transfers between devices with their start and end apart: 45 -> 45, of which waited for: 24 -> 27; matrix products, arithmetic and copies ran while one was open for 1% -> 1% of each run, Pallas kernels for 2% -> 2%
where the time goes in v4:
time: 142 us
  waiting for transfers between devices  64.7 us (46%)
  starting transfers between devices  64.3 us (45%)
  Pallas kernels  8.08 us (6%)
  other arithmetic  1.97 us (1%)
  local copies, waits for them, and re-layouts  1.71 us (1%)
    ppermute x45, waiting for transfers between devices, send(): return lax.ppermute(values, AXES, pairs)  64.7 us
    ppermute x45, starting transfers between devices, send(): return lax.ppermute(values, AXES, pairs)  64.3 us
    pallas_call x4, Pallas kernels, call(): pl.pallas_call(kernel, out_shape=[jax.ShapeDtypeStruct((count, tile, widt...  8.08 us
  transfers between devices with their start and end apart: 45, of which 27 were waited for; matrix products, arithmetic and copies ran while one was open for 1% of the time, Pallas kernels for 2%

profile of v4, /device:TPU:8, one launch (start us, length us, event | category | flops | bytes accessed | tf_op | source)
XLA Modules:
  0.0 141.8 jit_solution(17426361001837979392)
XLA Ops:
  0.0 7.2 %collective-permute-start = (bf16[128,256]{1,0:T(8,128)(2,1)}, bf16[128,256]{1,0:T(8,128)(2,1)S(1)}, u32[]{:S(2)}, u32[]{:S(2)}) collective-permute-start(bf16[128,256]{1,0:T(8,128)(2,1)} %param.6), channel_id=1, source_target_pairs={{0,4},{1,5},{2,6},{3,7},{4,0},{5,1},{6,2},{7,3},{8,12},{9,13},{10,... | collective-permute-start | bytes 196616 | tf_op jit(solution)/shard_map/ppermute | solution.py:47
  7.2 0.9 constant_dynamic-update-slice_fusion.4
  8.1 0.6 copy-done.3
  8.8 1.1 collective-permute-done
  10.0 3.1 %collective-permute-start.2 = (bf16[2,128,256]{2,1,0:T(8,128)(2,1)S(1)}, bf16[2,128,256]{2,1,0:T(8,128)(2,1)S(1)}, u32[]{:S(2)}, u32[]{:S(2)}) collective-permute-start(bf16[2,128,256]{2,1,0:T(8,128)(2,1)S(1)} %pad_maximum_fusion.3), channel_id=1, source_target_pairs={{0,16},{1,17},{2,18},{3,19},{4,20},{5,21},{6,22},{7,23},{8,24},{9,... | collective-permute-start | bytes 393224 | tf_op jit(solution)/shard_map/ppermute | solution.py:47
  13.1 1.1 collective-permute-start.1
  14.2 0.9 collective-permute-start.3
  15.1 2.9 %collective-permute-done.1 = bf16[2,128,256]{2,1,0:T(8,128)(2,1)S(1)} collective-permute-done((bf16[2,128,256]{2,1,0:T(8,128)(2,1)S(1)}, bf16[2,128,256]{2,1,0:T(8,128)(2,1)S(1)}, u32[]{:S(2)}, u32[]{:S(2)}) %collective-permute-start.1) | collective-permute-done | bytes 131104 | tf_op jit(solution)/shard_map/ppermute | solution.py:47
  18.1 2.3 %collective-permute-done.3 = bf16[2,128,256]{2,1,0:T(8,128)(2,1)S(1)} collective-permute-done((bf16[2,128,256]{2,1,0:T(8,128)(2,1)S(1)}, bf16[2,128,256]{2,1,0:T(8,128)(2,1)S(1)}, u32[]{:S(2)}, u32[]{:S(2)}) %collective-permute-start.3) | collective-permute-done | bytes 131104 | tf_op jit(solution)/shard_map/ppermute | solution.py:47
  20.4 1.7 %collective-permute-start.11 = (bf16[8,128,256]{2,1,0:T(8,128)(2,1)S(1)}, bf16[8,128,256]{2,1,0:T(8,128)(2,1)S(1)}, u32[]{:S(2)}, u32[]{:S(2)}) collective-permute-start(bf16[8,128,256]{2,1,0:T(8,128)(2,1)S(1)} %constant_dynamic-update-slice_fusion.right), channel_id=1, source_target_pairs={{0,1},{1,2},{2,3},{3,0},{4,5},{5,6},{6,7},{7,4},{8,9},{9,10},{10,1... | collective-permute-start | bytes 1572872 | tf_op jit(solution)/shard_map/ppermute | solution.py:47
  22.1 0.9 collective-permute-start.10
  23.0 2.4 %collective-permute-start.9 = (bf16[8,128,256]{2,1,0:T(8,128)(2,1)S(1)}, bf16[8,128,256]{2,1,0:T(8,128)(2,1)S(1)}, u32[]{:S(2)}, u32[]{:S(2)}) collective-permute-start(bf16[8,128,256]{2,1,0:T(8,128)(2,1)S(1)} %constant_dynamic-update-slice_fusion.right), channel_id=1, source_target_pairs={{0,3},{1,0},{2,1},{3,2},{4,7},{5,4},{6,5},{7,6},{8,11},{9,8},{10,9... | collective-permute-start | bytes 1572872 | tf_op jit(solution)/shard_map/ppermute | solution.py:47
  25.5 1.8 %collective-permute-start.7 = (bf16[128,256]{1,0:T(8,128)(2,1)S(1)}, bf16[128,256]{1,0:T(8,128)(2,1)S(1)}, u32[]{:S(2)}, u32[]{:S(2)}) collective-permute-start(bf16[128,256]{1,0:T(8,128)(2,1)S(1)} %copy-done.2), channel_id=1, source_target_pairs={{0,64},{1,65},{2,66},{3,67},{4,68},{5,69},{6,70},{7,71},{8,72},{9,... | collective-permute-start | bytes 196616 | tf_op jit(solution)/shard_map/ppermute | solution.py:47
  27.2 1.8 %collective-permute-start.6 = (bf16[128,256]{1,0:T(8,128)(2,1)S(1)}, bf16[128,256]{1,0:T(8,128)(2,1)S(1)}, u32[]{:S(2)}, u32[]{:S(2)}) collective-permute-start(bf16[128,256]{1,0:T(8,128)(2,1)S(1)} %copy-done.2), channel_id=1, source_target_pairs={{0,128},{1,129},{2,130},{3,131},{4,132},{5,133},{6,134},{7,135},{8... | collective-permute-start | bytes 196616 | tf_op jit(solution)/shard_map/ppermute | solution.py:47
  29.1 2.4 %collective-permute-done.7 = bf16[128,256]{1,0:T(8,128)(2,1)S(1)} collective-permute-done((bf16[128,256]{1,0:T(8,128)(2,1)S(1)}, bf16[128,256]{1,0:T(8,128)(2,1)S(1)}, u32[]{:S(2)}, u32[]{:S(2)}) %collective-permute-start.7) | collective-permute-done | bytes 65568 | tf_op jit(solution)/shard_map/ppermute | solution.py:47
  31.5 1.6 %collective-permute-start.5 = (bf16[128,256]{1,0:T(8,128)(2,1)S(1)}, bf16[128,256]{1,0:T(8,128)(2,1)S(1)}, u32[]{:S(2)}, u32[]{:S(2)}) collective-permute-start(bf16[128,256]{1,0:T(8,128)(2,1)S(1)} %copy-done.2), channel_id=1, source_target_pairs={{0,192},{1,193},{2,194},{3,195},{4,196},{5,197},{6,198},{7,199},{8... | collective-permute-start | bytes 196616 | tf_op jit(solution)/shard_map/ppermute | solution.py:47
  33.1 2.7 %collective-permute-done.5 = bf16[128,256]{1,0:T(8,128)(2,1)S(1)} collective-permute-done((bf16[128,256]{1,0:T(8,128)(2,1)S(1)}, bf16[128,256]{1,0:T(8,128)(2,1)S(1)}, u32[]{:S(2)}, u32[]{:S(2)}) %collective-permute-start.5) | collective-permute-done | bytes 65568 | tf_op jit(solution)/shard_map/ppermute | solution.py:47
  36.6 0.8 collective-permute-done.8.u3
  37.3 1.5 %shard_map.64 = (bf16[8,128,256]{2,1,0:T(8,128)(2,1)S(1)}, bf16[8,128,256]{2,1,0:T(8,128)(2,1)S(1)}, f32[8,128,256]{2,1,0:T(8,128)S(1)}, f32[8,128,256]{2,1,0:T(8,128)S(1)}) custom-call(s32[24]{0:T(128)S(1)} %get-tuple-element.36.first_ref, s32[24]{0:T(128)S(1)} %get-tuple-element.37.second_ref, s32[1]{0:T(128)S(6)} %copy.11.live_ref, ...), custom_call_target="tpu_custom_call" | custom-call | tf_op jit(solution)/shard_map/pallas_call | solution.py:134
  38.9 2.5 %shard_map.65 = (f32[4,128,256]{2,1,0:T(8,128)S(1)}, bf16[4,128,256]{2,1,0:T(8,128)(2,1)S(1)}, bf16[8,128,256]{2,1,0:T(8,128)(2,1)S(1)}, bf16[8,128,256]{2,1,0:T(8,128)(2,1)S(1)}, bf16[8,128,256]{2,1,0:T(8,128)(2,1)S(1)}) custom-call(s32[24]{0:T(128)S(1)} %get-tuple-element.36.first_ref, s32[24]{0:T(128)S(1)} %get-tuple-element.37.second_ref, ...), custom_call_target="tpu_custom_call" | custom-call | tf_op jit(solution)/shard_map/pallas_call | solution.py:134
  41.6 2.8 %collective-permute-start.13 = (bf16[8,128,256]{2,1,0:T(8,128)(2,1)S(1)}, bf16[8,128,256]{2,1,0:T(8,128)(2,1)S(1)}, u32[]{:S(2)}, u32[]{:S(2)}) collective-permute-start(bf16[8,128,256]{2,1,0:T(8,128)(2,1)S(1)} %get-tuple-element.47), channel_id=1, source_target_pairs={{0,1},{1,2},{2,3},{3,0},{4,5},{5,6},{6,7},{7,4},{8,9},{9,10},{10,1... | collective-permute-start | bytes 1572872 | tf_op jit(solution)/shard_map/ppermute | solution.py:47
  44.6 1.2 collective-permute-start.16
  45.8 2.7 %collective-permute-start.18 = (bf16[128,256]{1,0:T(8,128)(2,1)S(1)}, bf16[128,256]{1,0:T(8,128)(2,1)S(1)}, u32[]{:S(2)}, u32[]{:S(2)}) collective-permute-start(bf16[128,256]{1,0:T(8,128)(2,1)S(1)} %get-tuple-element.91), channel_id=1, source_target_pairs={{0,192},{1,193},{2,194},{3,195},{4,196},{5,197},{6,198},{7,199},{8... | collective-permute-start | bytes 196616 | tf_op jit(solution)/shard_map/ppermute | solution.py:47
  48.5 2.6 %collective-permute-done.16 = bf16[128,256]{1,0:T(8,128)(2,1)S(1)} collective-permute-done((bf16[128,256]{1,0:T(8,128)(2,1)S(1)}, bf16[128,256]{1,0:T(8,128)(2,1)S(1)}, u32[]{:S(2)}, u32[]{:S(2)}) %collective-permute-start.16) | collective-permute-done | bytes 65568 | tf_op jit(solution)/shard_map/ppermute | solution.py:47
  51.1 0.4 collective-permute-done.18
  51.4 4.9 %collective-permute-done.17 = bf16[128,256]{1,0:T(8,128)(2,1)S(1)} collective-permute-done((bf16[128,256]{1,0:T(8,128)(2,1)S(1)}, bf16[128,256]{1,0:T(8,128)(2,1)S(1)}, u32[]{:S(2)}, u32[]{:S(2)}) %collective-permute-start.17) | collective-permute-done | bytes 65568 | tf_op jit(solution)/shard_map/ppermute | solution.py:47
  56.6 1.3 collective-permute-done.14
  57.9 0.3 fusion.27
  58.4 1.8 %collective-permute-start.21 = (bf16[2,128,256]{2,1,0:T(8,128)(2,1)S(1)}, bf16[2,128,256]{2,1,0:T(8,128)(2,1)S(1)}, u32[]{:S(2)}, u32[]{:S(2)}) collective-permute-start(bf16[2,128,256]{2,1,0:T(8,128)(2,1)S(1)} %get-tuple-element.81), channel_id=1, source_target_pairs={{0,24},{1,25},{2,26},{3,27},{4,28},{5,29},{6,30},{7,31},{8,0},{9,1... | collective-permute-start | bytes 393224 | tf_op jit(solution)/shard_map/ppermute | solution.py:47
  60.1 0.3 collective-permute-start.20
  60.5 4.4 %collective-permute-done.19 = bf16[2,128,256]{2,1,0:T(8,128)(2,1)S(1)} collective-permute-done((bf16[2,128,256]{2,1,0:T(8,128)(2,1)S(1)}, bf16[2,128,256]{2,1,0:T(8,128)(2,1)S(1)}, u32[]{:S(2)}, u32[]{:S(2)}) %collective-permute-start.19) | collective-permute-done | bytes 131104 | tf_op jit(solution)/shard_map/ppermute | solution.py:47
  64.8 1.5 %collective-permute-done.20 = bf16[2,128,256]{2,1,0:T(8,128)(2,1)S(1)} collective-permute-done((bf16[2,128,256]{2,1,0:T(8,128)(2,1)S(1)}, bf16[2,128,256]{2,1,0:T(8,128)(2,1)S(1)}, u32[]{:S(2)}, u32[]{:S(2)}) %collective-permute-start.20) | collective-permute-done | bytes 131104 | tf_op jit(solution)/shard_map/ppermute | solution.py:47
  66.5 6.6 %collective-permute-start.22 = (bf16[2,128,256]{2,1,0:T(8,128)(2,1)S(1)}, bf16[2,128,256]{2,1,0:T(8,128)(2,1)S(1)}, u32[]{:S(2)}, u32[]{:S(2)}) collective-permute-start(bf16[2,128,256]{2,1,0:T(8,128)(2,1)S(1)} %pad_maximum_fusion.4), channel_id=1, source_target_pairs={{0,4},{1,5},{2,6},{3,7},{4,0},{5,1},{6,2},{7,3},{8,12},{9,13},{10,... | collective-permute-start | bytes 393224 | tf_op jit(solution)/shard_map/ppermute | solution.py:47
  73.1 4.4 %collective-permute-done.22 = bf16[2,128,256]{2,1,0:T(8,128)(2,1)S(1)} collective-permute-done((bf16[2,128,256]{2,1,0:T(8,128)(2,1)S(1)}, bf16[2,128,256]{2,1,0:T(8,128)(2,1)S(1)}, u32[]{:S(2)}, u32[]{:S(2)}) %collective-permute-start.22) | collective-permute-done | bytes 131104 | tf_op jit(solution)/shard_map/ppermute | solution.py:47
  77.6 2.0 %collective-permute-start.24 = (bf16[2,128,256]{2,1,0:T(8,128)(2,1)S(1)}, bf16[2,128,256]{2,1,0:T(8,128)(2,1)S(1)}, u32[]{:S(2)}, u32[]{:S(2)}) collective-permute-start(bf16[2,128,256]{2,1,0:T(8,128)(2,1)S(1)} %fusion.1), channel_id=1, source_target_pairs={{0,16},{1,17},{2,18},{3,19},{4,20},{5,21},{6,22},{7,23},{8,24},{9,... | collective-permute-start | bytes 393224 | tf_op jit(solution)/shard_map/ppermute | solution.py:47
  79.6 1.3 collective-permute-start.23
  80.8 4.3 %collective-permute-done.25 = bf16[2,128,256]{2,1,0:T(8,128)(2,1)S(1)} collective-permute-done((bf16[2,128,256]{2,1,0:T(8,128)(2,1)S(1)}, bf16[2,128,256]{2,1,0:T(8,128)(2,1)S(1)}, u32[]{:S(2)}, u32[]{:S(2)}) %collective-permute-start.25) | collective-permute-done | bytes 131104 | tf_op jit(solution)/shard_map/ppermute | solution.py:47
  85.2 0.9 collective-permute-done.23
  86.2 0.8 collective-permute-start.33
  87.0 3.3 %collective-permute-start.32 = (bf16[8,128,256]{2,1,0:T(8,128)(2,1)S(1)}, bf16[8,128,256]{2,1,0:T(8,128)(2,1)S(1)}, u32[]{:S(2)}, u32[]{:S(2)}) collective-permute-start(bf16[8,128,256]{2,1,0:T(8,128)(2,1)S(1)} %pad_maximum_fusion.right), channel_id=1, source_target_pairs={{0,2},{1,3},{2,0},{3,1},{4,6},{5,7},{6,4},{7,5},{8,10},{9,11},{10,... | collective-permute-start | bytes 1572872 | tf_op jit(solution)/shard_map/ppermute | solution.py:47
  90.4 0.7 collective-permute-start.29
  91.1 1.6 %collective-permute-start.28 = (bf16[128,256]{1,0:T(8,128)(2,1)S(1)}, bf16[128,256]{1,0:T(8,128)(2,1)S(1)}, u32[]{:S(2)}, u32[]{:S(2)}) collective-permute-start(bf16[128,256]{1,0:T(8,128)(2,1)S(1)} %slice_bitcast_fusion.7), channel_id=1, source_target_pairs={{0,128},{1,129},{2,130},{3,131},{4,132},{5,133},{6,134},{7,135},{8... | collective-permute-start | bytes 196616 | tf_op jit(solution)/shard_map/ppermute | solution.py:47
  92.7 3.9 %collective-permute-done.29 = bf16[128,256]{1,0:T(8,128)(2,1)S(1)} collective-permute-done((bf16[128,256]{1,0:T(8,128)(2,1)S(1)}, bf16[128,256]{1,0:T(8,128)(2,1)S(1)}, u32[]{:S(2)}, u32[]{:S(2)}) %collective-permute-start.29) | collective-permute-done | bytes 65568 | tf_op jit(solution)/shard_map/ppermute | solution.py:47
  96.6 1.1 collective-permute-done.28
  97.7 3.2 %collective-permute-done.27 = bf16[128,256]{1,0:T(8,128)(2,1)S(1)} collective-permute-done((bf16[128,256]{1,0:T(8,128)(2,1)S(1)}, bf16[128,256]{1,0:T(8,128)(2,1)S(1)}, u32[]{:S(2)}, u32[]{:S(2)}) %collective-permute-start.27) | collective-permute-done | bytes 65568 | tf_op jit(solution)/shard_map/ppermute | solution.py:47
  100.9 1.4 %collective-permute-done.30.u3 = bf16[3,128,256]{2,1,0:T(8,128)(2,1)S(1)} collective-permute-done((bf16[3,128,256]{2,1,0:T(8,128)(2,1)S(1)}, bf16[3,128,256]{2,1,0:T(8,128)(2,1)S(1)}, u32[]{:S(2)}, u32[]{:S(2)}) %collective-permute-start.30) | collective-permute-done | bytes 196640 | tf_op jit(solution)/shard_map/ppermute | solution.py:47
  102.4 1.5 %shard_map.66 = (bf16[8,128,256]{2,1,0:T(8,128)(2,1)S(1)}, bf16[8,128,256]{2,1,0:T(8,128)(2,1)S(1)}, f32[8,128,256]{2,1,0:T(8,128)S(1)}, f32[8,128,256]{2,1,0:T(8,128)S(1)}) custom-call(s32[24]{0:T(128)S(1)} %get-tuple-element.36.first_ref, s32[24]{0:T(128)S(1)} %get-tuple-element.37.second_ref, s32[1]{0:T(128)S(6)} %copy.11.live_ref, ...), custom_call_target="tpu_custom_call" | custom-call | tf_op jit(solution)/shard_map/pallas_call | solution.py:134
  103.9 2.5 %shard_map.67 = (f32[4,128,256]{2,1,0:T(8,128)S(1)}, bf16[4,128,256]{2,1,0:T(8,128)(2,1)S(1)}, bf16[8,128,256]{2,1,0:T(8,128)(2,1)S(1)}, bf16[8,128,256]{2,1,0:T(8,128)(2,1)S(1)}, bf16[8,128,256]{2,1,0:T(8,128)(2,1)S(1)}) custom-call(s32[24]{0:T(128)S(1)} %get-tuple-element.36.first_ref, s32[24]{0:T(128)S(1)} %get-tuple-element.37.second_ref, ...), custom_call_target="tpu_custom_call" | custom-call | tf_op jit(solution)/shard_map/pallas_call | solution.py:134
  106.6 2.0 %collective-permute-start.34 = (bf16[8,128,256]{2,1,0:T(8,128)(2,1)S(1)}, bf16[8,128,256]{2,1,0:T(8,128)(2,1)S(1)}, u32[]{:S(2)}, u32[]{:S(2)}) collective-permute-start(bf16[8,128,256]{2,1,0:T(8,128)(2,1)S(1)} %get-tuple-element.60), channel_id=1, source_target_pairs={{0,2},{1,3},{2,0},{3,1},{4,6},{5,7},{6,4},{7,5},{8,10},{9,11},{10,... | collective-permute-start | bytes 1572872 | tf_op jit(solution)/shard_map/ppermute | solution.py:47
  108.5 1.0 collective-permute-start.35
  109.5 1.1 collective-permute-start.36
  110.8 0.3 collective-permute-start.38
  111.0 3.6 %collective-permute-start.40 = (bf16[128,256]{1,0:T(8,128)(2,1)S(1)}, bf16[128,256]{1,0:T(8,128)(2,1)S(1)}, u32[]{:S(2)}, u32[]{:S(2)}) collective-permute-start(bf16[128,256]{1,0:T(8,128)(2,1)S(1)} %get-tuple-element.84), channel_id=1, source_target_pairs={{0,192},{1,193},{2,194},{3,195},{4,196},{5,197},{6,198},{7,199},{8... | collective-permute-start | bytes 196616 | tf_op jit(solution)/shard_map/ppermute | solution.py:47
  114.7 2.2 %collective-permute-done.38 = bf16[128,256]{1,0:T(8,128)(2,1)S(1)} collective-permute-done((bf16[128,256]{1,0:T(8,128)(2,1)S(1)}, bf16[128,256]{1,0:T(8,128)(2,1)S(1)}, u32[]{:S(2)}, u32[]{:S(2)}) %collective-permute-start.38) | collective-permute-done | bytes 65568 | tf_op jit(solution)/shard_map/ppermute | solution.py:47
  116.9 5.2 %collective-permute-done.39 = bf16[128,256]{1,0:T(8,128)(2,1)S(1)} collective-permute-done((bf16[128,256]{1,0:T(8,128)(2,1)S(1)}, bf16[128,256]{1,0:T(8,128)(2,1)S(1)}, u32[]{:S(2)}, u32[]{:S(2)}) %collective-permute-start.39) | collective-permute-done | bytes 65568 | tf_op jit(solution)/shard_map/ppermute | solution.py:47
  122.1 1.4 collective-permute-done.35
  123.5 0.3 fusion.23
  123.9 2.7 %collective-permute-start.43 = (bf16[2,128,256]{2,1,0:T(8,128)(2,1)S(1)}, bf16[2,128,256]{2,1,0:T(8,128)(2,1)S(1)}, u32[]{:S(2)}, u32[]{:S(2)}) collective-permute-start(bf16[2,128,256]{2,1,0:T(8,128)(2,1)S(1)} %get-tuple-element.78), channel_id=1, source_target_pairs={{0,24},{1,25},{2,26},{3,27},{4,28},{5,29},{6,30},{7,31},{8,0},{9,1... | collective-permute-start | bytes 393224 | tf_op jit(solution)/shard_map/ppermute | solution.py:47
  126.6 3.8 %collective-permute-done.41 = bf16[2,128,256]{2,1,0:T(8,128)(2,1)S(1)} collective-permute-done((bf16[2,128,256]{2,1,0:T(8,128)(2,1)S(1)}, bf16[2,128,256]{2,1,0:T(8,128)(2,1)S(1)}, u32[]{:S(2)}, u32[]{:S(2)}) %collective-permute-start.41) | collective-permute-done | bytes 131104 | tf_op jit(solution)/shard_map/ppermute | solution.py:47
  130.4 0.5 collective-permute-done.43
  130.9 1.8 %collective-permute-done.42 = bf16[2,128,256]{2,1,0:T(8,128)(2,1)S(1)} collective-permute-done((bf16[2,128,256]{2,1,0:T(8,128)(2,1)S(1)}, bf16[2,128,256]{2,1,0:T(8,128)(2,1)S(1)}, u32[]{:S(2)}, u32[]{:S(2)}) %collective-permute-start.42) | collective-permute-done | bytes 131104 | tf_op jit(solution)/shard_map/ppermute | solution.py:47
  132.8 5.2 %collective-permute-start.44 = (bf16[128,256]{1,0:T(8,128)(2,1)S(1)}, bf16[128,256]{1,0:T(8,128)(2,1)S(1)}, u32[]{:S(2)}, u32[]{:S(2)}) collective-permute-start(bf16[128,256]{1,0:T(8,128)(2,1)S(1)} %fusion.10), channel_id=1, source_target_pairs={{0,4},{1,5},{2,6},{3,7},{4,0},{5,1},{6,2},{7,3},{8,12},{9,13},{10,... | collective-permute-start | bytes 196616 | tf_op jit(solution)/shard_map/ppermute | solution.py:47
  138.0 3.1 %collective-permute-done.44 = bf16[128,256]{1,0:T(8,128)(2,1)S(1)} collective-permute-done((bf16[128,256]{1,0:T(8,128)(2,1)S(1)}, bf16[128,256]{1,0:T(8,128)(2,1)S(1)}, u32[]{:S(2)}, u32[]{:S(2)}) %collective-permute-start.44) | collective-permute-done | bytes 65568 | tf_op jit(solution)/shard_map/ppermute | solution.py:47
  141.1 0.7 fusion.9
  (73 shorter events, 1.9 us)
Async XLA Ops:
  0.0 9.9 %collective-permute-start = (bf16[128,256]{1,0:T(8,128)(2,1)}, bf16[128,256]{1,0:T(8,128)(2,1)S(1)}, u32[]{:S(2)}, u32[]{:S(2)}) collective-permute-start(bf16[128,256]{1,0:T(8,128)(2,1)} %param.6), channel_id=1, source_target_pairs={{0,4},{1,5},{2,6},{3,7},{4,0},{5,1},{6,2},{7,3},{8,12},{9,13},{10,... | collective-permute-start | bytes 196616 | tf_op jit(solution)/shard_map/ppermute | solution.py:47
  7.2 2.8 %copy-start.2 = (bf16[128,256]{1,0:T(8,128)(2,1)S(1)}, bf16[128,256]{1,0:T(8,128)(2,1)}, u32[]{:S(2)}) copy-start(bf16[128,256]{1,0:T(8,128)(2,1)} %param.6) | copy-start | bytes 196612
  8.1 0.7 copy-start.3
  8.1 0.7 copy-start.4
  9.9 27.4 %copy-start = (bf16[24,128,128]{2,1,0:T(8,128)(2,1)S(1)}, bf16[24,128,128]{2,1,0:T(8,128)(2,1)}, u32[]{:S(2)}) copy-start(bf16[24,128,128]{2,1,0:T(8,128)(2,1)} %wins.7) | copy-start | bytes 2359300
  9.9 27.4 %copy-start.1 = (bf16[24,128,128]{2,1,0:T(8,128)(2,1)S(1)}, bf16[24,128,128]{2,1,0:T(8,128)(2,1)}, u32[]{:S(2)}) copy-start(bf16[24,128,128]{2,1,0:T(8,128)(2,1)} %losses.7) | copy-start | bytes 2359300
  10.0 8.1 %collective-permute-start.2 = (bf16[2,128,256]{2,1,0:T(8,128)(2,1)S(1)}, bf16[2,128,256]{2,1,0:T(8,128)(2,1)S(1)}, u32[]{:S(2)}, u32[]{:S(2)}) collective-permute-start(bf16[2,128,256]{2,1,0:T(8,128)(2,1)S(1)} %pad_maximum_fusion.3), channel_id=1, source_target_pairs={{0,16},{1,17},{2,18},{3,19},{4,20},{5,21},{6,22},{7,23},{8,24},{9,... | collective-permute-start | bytes 393224 | tf_op jit(solution)/shard_map/ppermute | solution.py:47
  13.1 5.0 %collective-permute-start.1 = (bf16[2,128,256]{2,1,0:T(8,128)(2,1)S(1)}, bf16[2,128,256]{2,1,0:T(8,128)(2,1)S(1)}, u32[]{:S(2)}, u32[]{:S(2)}) collective-permute-start(bf16[2,128,256]{2,1,0:T(8,128)(2,1)S(1)} %pad_maximum_fusion.3), channel_id=1, source_target_pairs={{0,24},{1,25},{2,26},{3,27},{4,28},{5,29},{6,30},{7,31},{8,0},{9,1... | collective-permute-start | bytes 393224 | tf_op jit(solution)/shard_map/ppermute | solution.py:47
  14.2 6.2 %collective-permute-start.3 = (bf16[2,128,256]{2,1,0:T(8,128)(2,1)S(1)}, bf16[2,128,256]{2,1,0:T(8,128)(2,1)S(1)}, u32[]{:S(2)}, u32[]{:S(2)}) collective-permute-start(bf16[2,128,256]{2,1,0:T(8,128)(2,1)S(1)} %pad_maximum_fusion.3), channel_id=1, source_target_pairs={{0,8},{1,9},{2,10},{3,11},{4,12},{5,13},{6,14},{7,15},{8,16},{9,17... | collective-permute-start | bytes 393224 | tf_op jit(solution)/shard_map/ppermute | solution.py:47
  15.1 5.3 %collective-permute-start.4 = (bf16[128,256]{1,0:T(8,128)(2,1)S(1)}, bf16[128,256]{1,0:T(8,128)(2,1)S(1)}, u32[]{:S(2)}, u32[]{:S(2)}) collective-permute-start(bf16[128,256]{1,0:T(8,128)(2,1)S(1)} %copy-done.2), channel_id=1, source_target_pairs={{0,32},{1,33},{2,34},{3,35},{4,36},{5,37},{6,38},{7,39},{8,40},{9,... | collective-permute-start | bytes 196616 | tf_op jit(solution)/shard_map/ppermute | solution.py:47
  20.4 18.4 %collective-permute-start.11 = (bf16[8,128,256]{2,1,0:T(8,128)(2,1)S(1)}, bf16[8,128,256]{2,1,0:T(8,128)(2,1)S(1)}, u32[]{:S(2)}, u32[]{:S(2)}) collective-permute-start(bf16[8,128,256]{2,1,0:T(8,128)(2,1)S(1)} %constant_dynamic-update-slice_fusion.right), channel_id=1, source_target_pairs={{0,1},{1,2},{2,3},{3,0},{4,5},{5,6},{6,7},{7,4},{8,9},{9,10},{10,1... | collective-permute-start | bytes 1572872 | tf_op jit(solution)/shard_map/ppermute | solution.py:47
  22.1 16.8 %collective-permute-start.10 = (bf16[8,128,256]{2,1,0:T(8,128)(2,1)S(1)}, bf16[8,128,256]{2,1,0:T(8,128)(2,1)S(1)}, u32[]{:S(2)}, u32[]{:S(2)}) collective-permute-start(bf16[8,128,256]{2,1,0:T(8,128)(2,1)S(1)} %constant_dynamic-update-slice_fusion.right), channel_id=1, source_target_pairs={{0,2},{1,3},{2,0},{3,1},{4,6},{5,7},{6,4},{7,5},{8,10},{9,11},{10,... | collective-permute-start | bytes 1572872 | tf_op jit(solution)/shard_map/ppermute | solution.py:47
  23.0 15.9 %collective-permute-start.9 = (bf16[8,128,256]{2,1,0:T(8,128)(2,1)S(1)}, bf16[8,128,256]{2,1,0:T(8,128)(2,1)S(1)}, u32[]{:S(2)}, u32[]{:S(2)}) collective-permute-start(bf16[8,128,256]{2,1,0:T(8,128)(2,1)S(1)} %constant_dynamic-update-slice_fusion.right), channel_id=1, source_target_pairs={{0,3},{1,0},{2,1},{3,2},{4,7},{5,4},{6,5},{7,6},{8,11},{9,8},{10,9... | collective-permute-start | bytes 1572872 | tf_op jit(solution)/shard_map/ppermute | solution.py:47
  25.5 6.1 %collective-permute-start.7 = (bf16[128,256]{1,0:T(8,128)(2,1)S(1)}, bf16[128,256]{1,0:T(8,128)(2,1)S(1)}, u32[]{:S(2)}, u32[]{:S(2)}) collective-permute-start(bf16[128,256]{1,0:T(8,128)(2,1)S(1)} %copy-done.2), channel_id=1, source_target_pairs={{0,64},{1,65},{2,66},{3,67},{4,68},{5,69},{6,70},{7,71},{8,72},{9,... | collective-permute-start | bytes 196616 | tf_op jit(solution)/shard_map/ppermute | solution.py:47
  27.2 5.9 %collective-permute-start.6 = (bf16[128,256]{1,0:T(8,128)(2,1)S(1)}, bf16[128,256]{1,0:T(8,128)(2,1)S(1)}, u32[]{:S(2)}, u32[]{:S(2)}) collective-permute-start(bf16[128,256]{1,0:T(8,128)(2,1)S(1)} %copy-done.2), channel_id=1, source_target_pairs={{0,128},{1,129},{2,130},{3,131},{4,132},{5,133},{6,134},{7,135},{8... | collective-permute-start | bytes 196616 | tf_op jit(solution)/shard_map/ppermute | solution.py:47
  31.5 4.3 %collective-permute-start.5 = (bf16[128,256]{1,0:T(8,128)(2,1)S(1)}, bf16[128,256]{1,0:T(8,128)(2,1)S(1)}, u32[]{:S(2)}, u32[]{:S(2)}) collective-permute-start(bf16[128,256]{1,0:T(8,128)(2,1)S(1)} %copy-done.2), channel_id=1, source_target_pairs={{0,192},{1,193},{2,194},{3,195},{4,196},{5,197},{6,198},{7,199},{8... | collective-permute-start | bytes 196616 | tf_op jit(solution)/shard_map/ppermute | solution.py:47
  35.8 1.5 %collective-permute-start.8 = (bf16[3,128,256]{2,1,0:T(8,128)(2,1)S(1)}, bf16[3,128,256]{2,1,0:T(8,128)(2,1)S(1)}, u32[]{:S(2)}, u32[]{:S(2)}) collective-permute-start(bf16[3,128,256]{2,1,0:T(8,128)(2,1)S(1)} %pad_maximum_fusion.1.u1), channel_id=1, source_target_pairs={{0,32},{1,33},{2,34},{3,35},{4,36},{5,37},{6,38},{7,39},{8,40},{9,... | collective-permute-start | bytes 589832 | tf_op jit(solution)/shard_map/ppermute | solution.py:47
  41.4 3.0 %collective-permute-start.15 = (bf16[4,128,256]{2,1,0:T(8,128)(2,1)S(1)}, bf16[4,128,256]{2,1,0:T(8,128)(2,1)S(1)}, u32[]{:S(2)}, u32[]{:S(2)}) collective-permute-start(bf16[4,128,256]{2,1,0:T(8,128)(2,1)S(1)} %get-tuple-element.50), channel_id=1, source_target_pairs={{0,32},{1,33},{2,34},{3,35},{4,36},{5,37},{6,38},{7,39},{8,40},{9,... | collective-permute-start | bytes 786440 | tf_op jit(solution)/shard_map/ppermute | solution.py:47
  41.5 14.9 %collective-permute-start.12 = (bf16[8,128,256]{2,1,0:T(8,128)(2,1)S(1)}, bf16[8,128,256]{2,1,0:T(8,128)(2,1)S(1)}, u32[]{:S(2)}, u32[]{:S(2)}) collective-permute-start(bf16[8,128,256]{2,1,0:T(8,128)(2,1)S(1)} %get-tuple-element.46), channel_id=1, source_target_pairs={{0,2},{1,3},{2,0},{3,1},{4,6},{5,7},{6,4},{7,5},{8,10},{9,11},{10,... | collective-permute-start | bytes 1572872 | tf_op jit(solution)/shard_map/ppermute | solution.py:47
  41.6 14.9 %collective-permute-start.13 = (bf16[8,128,256]{2,1,0:T(8,128)(2,1)S(1)}, bf16[8,128,256]{2,1,0:T(8,128)(2,1)S(1)}, u32[]{:S(2)}, u32[]{:S(2)}) collective-permute-start(bf16[8,128,256]{2,1,0:T(8,128)(2,1)S(1)} %get-tuple-element.47), channel_id=1, source_target_pairs={{0,1},{1,2},{2,3},{3,0},{4,5},{5,6},{6,7},{7,4},{8,9},{9,10},{10,1... | collective-permute-start | bytes 1572872 | tf_op jit(solution)/shard_map/ppermute | solution.py:47
  44.5 13.5 %collective-permute-start.14 = (bf16[8,128,256]{2,1,0:T(8,128)(2,1)S(1)}, bf16[8,128,256]{2,1,0:T(8,128)(2,1)S(1)}, u32[]{:S(2)}, u32[]{:S(2)}) collective-permute-start(bf16[8,128,256]{2,1,0:T(8,128)(2,1)S(1)} %get-tuple-element.48), channel_id=1, source_target_pairs={{0,3},{1,0},{2,1},{3,2},{4,7},{5,4},{6,5},{7,6},{8,11},{9,8},{10,9... | collective-permute-start | bytes 1572872 | tf_op jit(solution)/shard_map/ppermute | solution.py:47
  44.6 6.5 %collective-permute-start.16 = (bf16[128,256]{1,0:T(8,128)(2,1)S(1)}, bf16[128,256]{1,0:T(8,128)(2,1)S(1)}, u32[]{:S(2)}, u32[]{:S(2)}) collective-permute-start(bf16[128,256]{1,0:T(8,128)(2,1)S(1)} %get-tuple-element.90), channel_id=1, source_target_pairs={{0,64},{1,65},{2,66},{3,67},{4,68},{5,69},{6,70},{7,71},{8,72},{9,... | collective-permute-start | bytes 196616 | tf_op jit(solution)/shard_map/ppermute | solution.py:47
  45.8 5.7 %collective-permute-start.18 = (bf16[128,256]{1,0:T(8,128)(2,1)S(1)}, bf16[128,256]{1,0:T(8,128)(2,1)S(1)}, u32[]{:S(2)}, u32[]{:S(2)}) collective-permute-start(bf16[128,256]{1,0:T(8,128)(2,1)S(1)} %get-tuple-element.91), channel_id=1, source_target_pairs={{0,192},{1,193},{2,194},{3,195},{4,196},{5,197},{6,198},{7,199},{8... | collective-permute-start | bytes 196616 | tf_op jit(solution)/shard_map/ppermute | solution.py:47
  51.1 5.3 %collective-permute-start.17 = (bf16[128,256]{1,0:T(8,128)(2,1)S(1)}, bf16[128,256]{1,0:T(8,128)(2,1)S(1)}, u32[]{:S(2)}, u32[]{:S(2)}) collective-permute-start(bf16[128,256]{1,0:T(8,128)(2,1)S(1)} %get-tuple-element.92), channel_id=1, source_target_pairs={{0,128},{1,129},{2,130},{3,131},{4,132},{5,133},{6,134},{7,135},{8... | collective-permute-start | bytes 196616 | tf_op jit(solution)/shard_map/ppermute | solution.py:47
  58.3 6.6 %collective-permute-start.19 = (bf16[2,128,256]{2,1,0:T(8,128)(2,1)S(1)}, bf16[2,128,256]{2,1,0:T(8,128)(2,1)S(1)}, u32[]{:S(2)}, u32[]{:S(2)}) collective-permute-start(bf16[2,128,256]{2,1,0:T(8,128)(2,1)S(1)} %get-tuple-element.80), channel_id=1, source_target_pairs={{0,16},{1,17},{2,18},{3,19},{4,20},{5,21},{6,22},{7,23},{8,24},{9,... | collective-permute-start | bytes 393224 | tf_op jit(solution)/shard_map/ppermute | solution.py:47
  58.4 6.5 %collective-permute-start.21 = (bf16[2,128,256]{2,1,0:T(8,128)(2,1)S(1)}, bf16[2,128,256]{2,1,0:T(8,128)(2,1)S(1)}, u32[]{:S(2)}, u32[]{:S(2)}) collective-permute-start(bf16[2,128,256]{2,1,0:T(8,128)(2,1)S(1)} %get-tuple-element.81), channel_id=1, source_target_pairs={{0,24},{1,25},{2,26},{3,27},{4,28},{5,29},{6,30},{7,31},{8,0},{9,1... | collective-permute-start | bytes 393224 | tf_op jit(solution)/shard_map/ppermute | solution.py:47
  60.1 6.2 %collective-permute-start.20 = (bf16[2,128,256]{2,1,0:T(8,128)(2,1)S(1)}, bf16[2,128,256]{2,1,0:T(8,128)(2,1)S(1)}, u32[]{:S(2)}, u32[]{:S(2)}) collective-permute-start(bf16[2,128,256]{2,1,0:T(8,128)(2,1)S(1)} %get-tuple-element.82), channel_id=1, source_target_pairs={{0,8},{1,9},{2,10},{3,11},{4,12},{5,13},{6,14},{7,15},{8,16},{9,17... | collective-permute-start | bytes 393224 | tf_op jit(solution)/shard_map/ppermute | solution.py:47
  66.5 11.0 %collective-permute-start.22 = (bf16[2,128,256]{2,1,0:T(8,128)(2,1)S(1)}, bf16[2,128,256]{2,1,0:T(8,128)(2,1)S(1)}, u32[]{:S(2)}, u32[]{:S(2)}) collective-permute-start(bf16[2,128,256]{2,1,0:T(8,128)(2,1)S(1)} %pad_maximum_fusion.4), channel_id=1, source_target_pairs={{0,4},{1,5},{2,6},{3,7},{4,0},{5,1},{6,2},{7,3},{8,12},{9,13},{10,... | collective-permute-start | bytes 393224 | tf_op jit(solution)/shard_map/ppermute | solution.py:47
  77.5 7.7 %collective-permute-start.25 = (bf16[2,128,256]{2,1,0:T(8,128)(2,1)S(1)}, bf16[2,128,256]{2,1,0:T(8,128)(2,1)S(1)}, u32[]{:S(2)}, u32[]{:S(2)}) collective-permute-start(bf16[2,128,256]{2,1,0:T(8,128)(2,1)S(1)} %fusion.1), channel_id=1, source_target_pairs={{0,8},{1,9},{2,10},{3,11},{4,12},{5,13},{6,14},{7,15},{8,16},{9,17... | collective-permute-start | bytes 393224 | tf_op jit(solution)/shard_map/ppermute | solution.py:47
  77.6 7.6 %collective-permute-start.24 = (bf16[2,128,256]{2,1,0:T(8,128)(2,1)S(1)}, bf16[2,128,256]{2,1,0:T(8,128)(2,1)S(1)}, u32[]{:S(2)}, u32[]{:S(2)}) collective-permute-start(bf16[2,128,256]{2,1,0:T(8,128)(2,1)S(1)} %fusion.1), channel_id=1, source_target_pairs={{0,16},{1,17},{2,18},{3,19},{4,20},{5,21},{6,22},{7,23},{8,24},{9,... | collective-permute-start | bytes 393224 | tf_op jit(solution)/shard_map/ppermute | solution.py:47
  79.6 6.5 %collective-permute-start.23 = (bf16[2,128,256]{2,1,0:T(8,128)(2,1)S(1)}, bf16[2,128,256]{2,1,0:T(8,128)(2,1)S(1)}, u32[]{:S(2)}, u32[]{:S(2)}) collective-permute-start(bf16[2,128,256]{2,1,0:T(8,128)(2,1)S(1)} %fusion.1), channel_id=1, source_target_pairs={{0,24},{1,25},{2,26},{3,27},{4,28},{5,29},{6,30},{7,31},{8,0},{9,1... | collective-permute-start | bytes 393224 | tf_op jit(solution)/shard_map/ppermute | solution.py:47
  80.8 5.3 %collective-permute-start.26 = (bf16[128,256]{1,0:T(8,128)(2,1)S(1)}, bf16[128,256]{1,0:T(8,128)(2,1)S(1)}, u32[]{:S(2)}, u32[]{:S(2)}) collective-permute-start(bf16[128,256]{1,0:T(8,128)(2,1)S(1)} %slice_bitcast_fusion.7), channel_id=1, source_target_pairs={{0,32},{1,33},{2,34},{3,35},{4,36},{5,37},{6,38},{7,39},{8,40},{9,... | collective-permute-start | bytes 196616 | tf_op jit(solution)/shard_map/ppermute | solution.py:47
  86.2 17.8 %collective-permute-start.33 = (bf16[8,128,256]{2,1,0:T(8,128)(2,1)S(1)}, bf16[8,128,256]{2,1,0:T(8,128)(2,1)S(1)}, u32[]{:S(2)}, u32[]{:S(2)}) collective-permute-start(bf16[8,128,256]{2,1,0:T(8,128)(2,1)S(1)} %pad_maximum_fusion.right), channel_id=1, source_target_pairs={{0,1},{1,2},{2,3},{3,0},{4,5},{5,6},{6,7},{7,4},{8,9},{9,10},{10,1... | collective-permute-start | bytes 1572872 | tf_op jit(solution)/shard_map/ppermute | solution.py:47
  87.0 17.0 %collective-permute-start.32 = (bf16[8,128,256]{2,1,0:T(8,128)(2,1)S(1)}, bf16[8,128,256]{2,1,0:T(8,128)(2,1)S(1)}, u32[]{:S(2)}, u32[]{:S(2)}) collective-permute-start(bf16[8,128,256]{2,1,0:T(8,128)(2,1)S(1)} %pad_maximum_fusion.right), channel_id=1, source_target_pairs={{0,2},{1,3},{2,0},{3,1},{4,6},{5,7},{6,4},{7,5},{8,10},{9,11},{10,... | collective-permute-start | bytes 1572872 | tf_op jit(solution)/shard_map/ppermute | solution.py:47
  90.3 13.6 %collective-permute-start.31 = (bf16[8,128,256]{2,1,0:T(8,128)(2,1)S(1)}, bf16[8,128,256]{2,1,0:T(8,128)(2,1)S(1)}, u32[]{:S(2)}, u32[]{:S(2)}) collective-permute-start(bf16[8,128,256]{2,1,0:T(8,128)(2,1)S(1)} %pad_maximum_fusion.right), channel_id=1, source_target_pairs={{0,3},{1,0},{2,1},{3,2},{4,7},{5,4},{6,5},{7,6},{8,11},{9,8},{10,9... | collective-permute-start | bytes 1572872 | tf_op jit(solution)/shard_map/ppermute | solution.py:47
  90.4 6.2 %collective-permute-start.29 = (bf16[128,256]{1,0:T(8,128)(2,1)S(1)}, bf16[128,256]{1,0:T(8,128)(2,1)S(1)}, u32[]{:S(2)}, u32[]{:S(2)}) collective-permute-start(bf16[128,256]{1,0:T(8,128)(2,1)S(1)} %slice_bitcast_fusion.7), channel_id=1, source_target_pairs={{0,64},{1,65},{2,66},{3,67},{4,68},{5,69},{6,70},{7,71},{8,72},{9,... | collective-permute-start | bytes 196616 | tf_op jit(solution)/shard_map/ppermute | solution.py:47
  91.1 6.6 %collective-permute-start.28 = (bf16[128,256]{1,0:T(8,128)(2,1)S(1)}, bf16[128,256]{1,0:T(8,128)(2,1)S(1)}, u32[]{:S(2)}, u32[]{:S(2)}) collective-permute-start(bf16[128,256]{1,0:T(8,128)(2,1)S(1)} %slice_bitcast_fusion.7), channel_id=1, source_target_pairs={{0,128},{1,129},{2,130},{3,131},{4,132},{5,133},{6,134},{7,135},{8... | collective-permute-start | bytes 196616 | tf_op jit(solution)/shard_map/ppermute | solution.py:47
  96.6 4.3 %collective-permute-start.27 = (bf16[128,256]{1,0:T(8,128)(2,1)S(1)}, bf16[128,256]{1,0:T(8,128)(2,1)S(1)}, u32[]{:S(2)}, u32[]{:S(2)}) collective-permute-start(bf16[128,256]{1,0:T(8,128)(2,1)S(1)} %slice_bitcast_fusion.7), channel_id=1, source_target_pairs={{0,192},{1,193},{2,194},{3,195},{4,196},{5,197},{6,198},{7,199},{8... | collective-permute-start | bytes 196616 | tf_op jit(solution)/shard_map/ppermute | solution.py:47
  100.8 1.5 %collective-permute-start.30 = (bf16[3,128,256]{2,1,0:T(8,128)(2,1)S(1)}, bf16[3,128,256]{2,1,0:T(8,128)(2,1)S(1)}, u32[]{:S(2)}, u32[]{:S(2)}) collective-permute-start(bf16[3,128,256]{2,1,0:T(8,128)(2,1)S(1)} %pad_maximum_fusion.2.u1), channel_id=1, source_target_pairs={{0,32},{1,33},{2,34},{3,35},{4,36},{5,37},{6,38},{7,39},{8,40},{9,... | collective-permute-start | bytes 589832 | tf_op jit(solution)/shard_map/ppermute | solution.py:47
  106.5 4.2 %collective-permute-start.37 = (bf16[4,128,256]{2,1,0:T(8,128)(2,1)S(1)}, bf16[4,128,256]{2,1,0:T(8,128)(2,1)S(1)}, u32[]{:S(2)}, u32[]{:S(2)}) collective-permute-start(bf16[4,128,256]{2,1,0:T(8,128)(2,1)S(1)} %get-tuple-element.64), channel_id=1, source_target_pairs={{0,32},{1,33},{2,34},{3,35},{4,36},{5,37},{6,38},{7,39},{8,40},{9,... | collective-permute-start | bytes 786440 | tf_op jit(solution)/shard_map/ppermute | solution.py:47
  106.6 15.5 %collective-permute-start.34 = (bf16[8,128,256]{2,1,0:T(8,128)(2,1)S(1)}, bf16[8,128,256]{2,1,0:T(8,128)(2,1)S(1)}, u32[]{:S(2)}, u32[]{:S(2)}) collective-permute-start(bf16[8,128,256]{2,1,0:T(8,128)(2,1)S(1)} %get-tuple-element.60), channel_id=1, source_target_pairs={{0,2},{1,3},{2,0},{3,1},{4,6},{5,7},{6,4},{7,5},{8,10},{9,11},{10,... | collective-permute-start | bytes 1572872 | tf_op jit(solution)/shard_map/ppermute | solution.py:47
  108.5 14.9 %collective-permute-start.35 = (bf16[8,128,256]{2,1,0:T(8,128)(2,1)S(1)}, bf16[8,128,256]{2,1,0:T(8,128)(2,1)S(1)}, u32[]{:S(2)}, u32[]{:S(2)}) collective-permute-start(bf16[8,128,256]{2,1,0:T(8,128)(2,1)S(1)} %get-tuple-element.61), channel_id=1, source_target_pairs={{0,1},{1,2},{2,3},{3,0},{4,5},{5,6},{6,7},{7,4},{8,9},{9,10},{10,1... | collective-permute-start | bytes 1572872 | tf_op jit(solution)/shard_map/ppermute | solution.py:47
  109.5 13.9 %collective-permute-start.36 = (bf16[8,128,256]{2,1,0:T(8,128)(2,1)S(1)}, bf16[8,128,256]{2,1,0:T(8,128)(2,1)S(1)}, u32[]{:S(2)}, u32[]{:S(2)}) collective-permute-start(bf16[8,128,256]{2,1,0:T(8,128)(2,1)S(1)} %get-tuple-element.62), channel_id=1, source_target_pairs={{0,3},{1,0},{2,1},{3,2},{4,7},{5,4},{6,5},{7,6},{8,11},{9,8},{10,9... | collective-permute-start | bytes 1572872 | tf_op jit(solution)/shard_map/ppermute | solution.py:47
  110.8 6.1 %collective-permute-start.38 = (bf16[128,256]{1,0:T(8,128)(2,1)S(1)}, bf16[128,256]{1,0:T(8,128)(2,1)S(1)}, u32[]{:S(2)}, u32[]{:S(2)}) collective-permute-start(bf16[128,256]{1,0:T(8,128)(2,1)S(1)} %get-tuple-element.83), channel_id=1, source_target_pairs={{0,64},{1,65},{2,66},{3,67},{4,68},{5,69},{6,70},{7,71},{8,72},{9,... | collective-permute-start | bytes 196616 | tf_op jit(solution)/shard_map/ppermute | solution.py:47
  111.0 5.9 %collective-permute-start.40 = (bf16[128,256]{1,0:T(8,128)(2,1)S(1)}, bf16[128,256]{1,0:T(8,128)(2,1)S(1)}, u32[]{:S(2)}, u32[]{:S(2)}) collective-permute-start(bf16[128,256]{1,0:T(8,128)(2,1)S(1)} %get-tuple-element.84), channel_id=1, source_target_pairs={{0,192},{1,193},{2,194},{3,195},{4,196},{5,197},{6,198},{7,199},{8... | collective-permute-start | bytes 196616 | tf_op jit(solution)/shard_map/ppermute | solution.py:47
  116.9 5.2 %collective-permute-start.39 = (bf16[128,256]{1,0:T(8,128)(2,1)S(1)}, bf16[128,256]{1,0:T(8,128)(2,1)S(1)}, u32[]{:S(2)}, u32[]{:S(2)}) collective-permute-start(bf16[128,256]{1,0:T(8,128)(2,1)S(1)} %get-tuple-element.85), channel_id=1, source_target_pairs={{0,128},{1,129},{2,130},{3,131},{4,132},{5,133},{6,134},{7,135},{8... | collective-permute-start | bytes 196616 | tf_op jit(solution)/shard_map/ppermute | solution.py:47
  123.8 6.6 %collective-permute-start.41 = (bf16[2,128,256]{2,1,0:T(8,128)(2,1)S(1)}, bf16[2,128,256]{2,1,0:T(8,128)(2,1)S(1)}, u32[]{:S(2)}, u32[]{:S(2)}) collective-permute-start(bf16[2,128,256]{2,1,0:T(8,128)(2,1)S(1)} %get-tuple-element.77), channel_id=1, source_target_pairs={{0,16},{1,17},{2,18},{3,19},{4,20},{5,21},{6,22},{7,23},{8,24},{9,... | collective-permute-start | bytes 393224 | tf_op jit(solution)/shard_map/ppermute | solution.py:47
  123.9 7.0 %collective-permute-start.43 = (bf16[2,128,256]{2,1,0:T(8,128)(2,1)S(1)}, bf16[2,128,256]{2,1,0:T(8,128)(2,1)S(1)}, u32[]{:S(2)}, u32[]{:S(2)}) collective-permute-start(bf16[2,128,256]{2,1,0:T(8,128)(2,1)S(1)} %get-tuple-element.78), channel_id=1, source_target_pairs={{0,24},{1,25},{2,26},{3,27},{4,28},{5,29},{6,30},{7,31},{8,0},{9,1... | collective-permute-start | bytes 393224 | tf_op jit(solution)/shard_map/ppermute | solution.py:47
  126.6 6.2 %collective-permute-start.42 = (bf16[2,128,256]{2,1,0:T(8,128)(2,1)S(1)}, bf16[2,128,256]{2,1,0:T(8,128)(2,1)S(1)}, u32[]{:S(2)}, u32[]{:S(2)}) collective-permute-start(bf16[2,128,256]{2,1,0:T(8,128)(2,1)S(1)} %get-tuple-element.79), channel_id=1, source_target_pairs={{0,8},{1,9},{2,10},{3,11},{4,12},{5,13},{6,14},{7,15},{8,16},{9,17... | collective-permute-start | bytes 393224 | tf_op jit(solution)/shard_map/ppermute | solution.py:47
  132.8 8.3 %collective-permute-start.44 = (bf16[128,256]{1,0:T(8,128)(2,1)S(1)}, bf16[128,256]{1,0:T(8,128)(2,1)S(1)}, u32[]{:S(2)}, u32[]{:S(2)}) collective-permute-start(bf16[128,256]{1,0:T(8,128)(2,1)S(1)} %fusion.10), channel_id=1, source_target_pairs={{0,4},{1,5},{2,6},{3,7},{4,0},{5,1},{6,2},{7,3},{8,12},{9,13},{10,... | collective-permute-start | bytes 196616 | tf_op jit(solution)/shard_map/ppermute | solution.py:47

commit v5 on v4

--- a/solution.py
+++ b/solution.py
@@ -11,7 +11,7 @@
 
 ITERS = 2
 RATE = 0.01
-GROUP = 8
+OWN_GROUP, GROUP = 4, 8
 AXES = ("zl", "core", "x", "zh", "y")
 SIZES = (4, 2, 4, 2, 4)
 
@@ -59,14 +59,15 @@
 
 
 def visit_slots(
-    first_ref, second_ref, live_ref, slots, begin, end, left, turned, right, wins, losses, first_sum, second_sum
+    first_ref, second_ref, live_ref, slots, begin, end, left, turned, right, wins, losses, first_sum, second_sum,
+    group=GROUP,
 ):
     count = list_slots(second_ref, live_ref[0], slots, begin, end, wins.shape[0])
 
     def step(turn, carry):
         work = []
-        for member in range(GROUP):
-            place = turn * GROUP + member
+        for member in range(group):
+            place = turn * group + member
             slot = slots[place]
             p = first_ref[slot]
             q = jnp.clip(second_ref[slot] - begin, 0, end - begin - 1)
@@ -90,7 +91,7 @@
             second_sum[q] += second
         return carry
 
-    lax.fori_loop(0, (count + GROUP - 1) // GROUP, step, 0)
+    lax.fori_loop(0, (count + group - 1) // group, step, 0)
 
 
 def own_kernel(
@@ -106,7 +107,8 @@
     first_sum[...] = jnp.zeros_like(first_sum)
     second_sum[...] = jnp.zeros_like(second_sum)
     visit_slots(
-        first_ref, second_ref, live_ref, slots, 0, 8, left, turned, right, wins, losses, first_sum, second_sum
+        first_ref, second_ref, live_ref, slots, 0, 8, left, turned, right, wins, losses, first_sum, second_sum,
+        group=OWN_GROUP,
     )
 
 

time: 142 us -> 142 us (level)
  starting transfers between devices: 64.3 us -> 71.6 us
  waiting for transfers between devices: 64.7 us -> 58.6 us
  Pallas kernels: 8.08 us -> 6.36 us
    ppermute x45, starting transfers between devices: 64.3 us -> 71.6 us  [send(): return lax.ppermute(values, AXES, pairs)]
    ppermute x45, waiting for transfers between devices: 64.7 us -> 58.6 us  [send(): return lax.ppermute(values, AXES, pairs)]
    pallas_call x4, Pallas kernels: 8.08 us -> 6.36 us  [call(): pl.pallas_call(kernel, out_shape=[jax.ShapeDtypeStruct((count, tile, widt...]
  transfers between devices with their start and end apart: 45 -> 45, of which waited for: 27 -> 24; matrix products, arithmetic and copies ran while one was open for 1% -> 1% of each run, Pallas kernels for 2% -> 2%
where the time goes in v5:
time: 142 us; the launch traced here: 141 us
  starting transfers between devices  71.6 us (50%)
  waiting for transfers between devices  58.6 us (41%)
  Pallas kernels  6.36 us (4%)
  other arithmetic  1.97 us (1%)
  local copies, waits for them, and re-layouts  1.71 us (1%)
    ppermute x45, starting transfers between devices, send(): return lax.ppermute(values, AXES, pairs)  71.6 us
    ppermute x45, waiting for transfers between devices, send(): return lax.ppermute(values, AXES, pairs)  58.6 us
    pallas_call x4, Pallas kernels, call(): pl.pallas_call(kernel, out_shape=[jax.ShapeDtypeStruct((count, tile, widt...  6.36 us
  transfers between devices with their start and end apart: 45, of which 24 were waited for; matrix products, arithmetic and copies ran while one was open for 1% of the time, Pallas kernels for 2%

profile of v5, /device:TPU:8, one launch (start us, length us, event | category | flops | bytes accessed | tf_op | source)
XLA Modules:
  0.0 141.2 jit_solution(13494779596794290954)
XLA Ops:
  0.0 7.2 %collective-permute-start = (bf16[128,256]{1,0:T(8,128)(2,1)}, bf16[128,256]{1,0:T(8,128)(2,1)S(1)}, u32[]{:S(2)}, u32[]{:S(2)}) collective-permute-start(bf16[128,256]{1,0:T(8,128)(2,1)} %param.6), channel_id=1, source_target_pairs={{0,4},{1,5},{2,6},{3,7},{4,0},{5,1},{6,2},{7,3},{8,12},{9,13},{10,... | collective-permute-start | bytes 196616 | tf_op jit(solution)/shard_map/ppermute | solution.py:47
  7.2 0.9 constant_dynamic-update-slice_fusion.4
  8.1 0.6 copy-done.3
  8.8 1.1 collective-permute-done
  10.0 3.1 %collective-permute-start.2 = (bf16[2,128,256]{2,1,0:T(8,128)(2,1)S(1)}, bf16[2,128,256]{2,1,0:T(8,128)(2,1)S(1)}, u32[]{:S(2)}, u32[]{:S(2)}) collective-permute-start(bf16[2,128,256]{2,1,0:T(8,128)(2,1)S(1)} %pad_maximum_fusion.3), channel_id=1, source_target_pairs={{0,16},{1,17},{2,18},{3,19},{4,20},{5,21},{6,22},{7,23},{8,24},{9,... | collective-permute-start | bytes 393224 | tf_op jit(solution)/shard_map/ppermute | solution.py:47
  13.1 1.1 collective-permute-start.1
  14.2 0.9 collective-permute-start.3
  15.1 2.9 %collective-permute-done.1 = bf16[2,128,256]{2,1,0:T(8,128)(2,1)S(1)} collective-permute-done((bf16[2,128,256]{2,1,0:T(8,128)(2,1)S(1)}, bf16[2,128,256]{2,1,0:T(8,128)(2,1)S(1)}, u32[]{:S(2)}, u32[]{:S(2)}) %collective-permute-start.1) | collective-permute-done | bytes 131104 | tf_op jit(solution)/shard_map/ppermute | solution.py:47
  18.1 2.3 %collective-permute-done.3 = bf16[2,128,256]{2,1,0:T(8,128)(2,1)S(1)} collective-permute-done((bf16[2,128,256]{2,1,0:T(8,128)(2,1)S(1)}, bf16[2,128,256]{2,1,0:T(8,128)(2,1)S(1)}, u32[]{:S(2)}, u32[]{:S(2)}) %collective-permute-start.3) | collective-permute-done | bytes 131104 | tf_op jit(solution)/shard_map/ppermute | solution.py:47
  20.4 1.7 %collective-permute-start.11 = (bf16[8,128,256]{2,1,0:T(8,128)(2,1)S(1)}, bf16[8,128,256]{2,1,0:T(8,128)(2,1)S(1)}, u32[]{:S(2)}, u32[]{:S(2)}) collective-permute-start(bf16[8,128,256]{2,1,0:T(8,128)(2,1)S(1)} %constant_dynamic-update-slice_fusion.right), channel_id=1, source_target_pairs={{0,1},{1,2},{2,3},{3,0},{4,5},{5,6},{6,7},{7,4},{8,9},{9,10},{10,1... | collective-permute-start | bytes 1572872 | tf_op jit(solution)/shard_map/ppermute | solution.py:47
  22.1 0.9 collective-permute-start.10
  23.0 2.4 %collective-permute-start.9 = (bf16[8,128,256]{2,1,0:T(8,128)(2,1)S(1)}, bf16[8,128,256]{2,1,0:T(8,128)(2,1)S(1)}, u32[]{:S(2)}, u32[]{:S(2)}) collective-permute-start(bf16[8,128,256]{2,1,0:T(8,128)(2,1)S(1)} %constant_dynamic-update-slice_fusion.right), channel_id=1, source_target_pairs={{0,3},{1,0},{2,1},{3,2},{4,7},{5,4},{6,5},{7,6},{8,11},{9,8},{10,9... | collective-permute-start | bytes 1572872 | tf_op jit(solution)/shard_map/ppermute | solution.py:47
  25.5 1.8 %collective-permute-start.7 = (bf16[128,256]{1,0:T(8,128)(2,1)S(1)}, bf16[128,256]{1,0:T(8,128)(2,1)S(1)}, u32[]{:S(2)}, u32[]{:S(2)}) collective-permute-start(bf16[128,256]{1,0:T(8,128)(2,1)S(1)} %copy-done.2), channel_id=1, source_target_pairs={{0,64},{1,65},{2,66},{3,67},{4,68},{5,69},{6,70},{7,71},{8,72},{9,... | collective-permute-start | bytes 196616 | tf_op jit(solution)/shard_map/ppermute | solution.py:47
  27.2 1.8 %collective-permute-start.6 = (bf16[128,256]{1,0:T(8,128)(2,1)S(1)}, bf16[128,256]{1,0:T(8,128)(2,1)S(1)}, u32[]{:S(2)}, u32[]{:S(2)}) collective-permute-start(bf16[128,256]{1,0:T(8,128)(2,1)S(1)} %copy-done.2), channel_id=1, source_target_pairs={{0,128},{1,129},{2,130},{3,131},{4,132},{5,133},{6,134},{7,135},{8... | collective-permute-start | bytes 196616 | tf_op jit(solution)/shard_map/ppermute | solution.py:47
  29.1 2.4 %collective-permute-done.7 = bf16[128,256]{1,0:T(8,128)(2,1)S(1)} collective-permute-done((bf16[128,256]{1,0:T(8,128)(2,1)S(1)}, bf16[128,256]{1,0:T(8,128)(2,1)S(1)}, u32[]{:S(2)}, u32[]{:S(2)}) %collective-permute-start.7) | collective-permute-done | bytes 65568 | tf_op jit(solution)/shard_map/ppermute | solution.py:47
  31.5 1.6 %collective-permute-start.5 = (bf16[128,256]{1,0:T(8,128)(2,1)S(1)}, bf16[128,256]{1,0:T(8,128)(2,1)S(1)}, u32[]{:S(2)}, u32[]{:S(2)}) collective-permute-start(bf16[128,256]{1,0:T(8,128)(2,1)S(1)} %copy-done.2), channel_id=1, source_target_pairs={{0,192},{1,193},{2,194},{3,195},{4,196},{5,197},{6,198},{7,199},{8... | collective-permute-start | bytes 196616 | tf_op jit(solution)/shard_map/ppermute | solution.py:47
  33.1 2.7 %collective-permute-done.5 = bf16[128,256]{1,0:T(8,128)(2,1)S(1)} collective-permute-done((bf16[128,256]{1,0:T(8,128)(2,1)S(1)}, bf16[128,256]{1,0:T(8,128)(2,1)S(1)}, u32[]{:S(2)}, u32[]{:S(2)}) %collective-permute-start.5) | collective-permute-done | bytes 65568 | tf_op jit(solution)/shard_map/ppermute | solution.py:47
  36.6 0.8 collective-permute-done.8.u3
  37.3 1.4 shard_map.64
  38.7 1.8 %shard_map.65 = (f32[4,128,256]{2,1,0:T(8,128)S(1)}, bf16[4,128,256]{2,1,0:T(8,128)(2,1)S(1)}, bf16[8,128,256]{2,1,0:T(8,128)(2,1)S(1)}, bf16[8,128,256]{2,1,0:T(8,128)(2,1)S(1)}, bf16[8,128,256]{2,1,0:T(8,128)(2,1)S(1)}) custom-call(s32[24]{0:T(128)S(1)} %get-tuple-element.36.first_ref, s32[24]{0:T(128)S(1)} %get-tuple-element.37.second_ref, ...), custom_call_target="tpu_custom_call" | custom-call | tf_op jit(solution)/shard_map/pallas_call | solution.py:136
  40.8 1.2 collective-permute-start.12
  42.0 1.6 %collective-permute-start.13 = (bf16[8,128,256]{2,1,0:T(8,128)(2,1)S(1)}, bf16[8,128,256]{2,1,0:T(8,128)(2,1)S(1)}, u32[]{:S(2)}, u32[]{:S(2)}) collective-permute-start(bf16[8,128,256]{2,1,0:T(8,128)(2,1)S(1)} %get-tuple-element.47), channel_id=1, source_target_pairs={{0,1},{1,2},{2,3},{3,0},{4,5},{5,6},{6,7},{7,4},{8,9},{9,10},{10,1... | collective-permute-start | bytes 1572872 | tf_op jit(solution)/shard_map/ppermute | solution.py:47
  44.2 1.2 collective-permute-start.16
  45.3 3.0 %collective-permute-start.18 = (bf16[128,256]{1,0:T(8,128)(2,1)S(1)}, bf16[128,256]{1,0:T(8,128)(2,1)S(1)}, u32[]{:S(2)}, u32[]{:S(2)}) collective-permute-start(bf16[128,256]{1,0:T(8,128)(2,1)S(1)} %get-tuple-element.91), channel_id=1, source_target_pairs={{0,192},{1,193},{2,194},{3,195},{4,196},{5,197},{6,198},{7,199},{8... | collective-permute-start | bytes 196616 | tf_op jit(solution)/shard_map/ppermute | solution.py:47
  48.3 2.4 %collective-permute-done.16 = bf16[128,256]{1,0:T(8,128)(2,1)S(1)} collective-permute-done((bf16[128,256]{1,0:T(8,128)(2,1)S(1)}, bf16[128,256]{1,0:T(8,128)(2,1)S(1)}, u32[]{:S(2)}, u32[]{:S(2)}) %collective-permute-start.16) | collective-permute-done | bytes 65568 | tf_op jit(solution)/shard_map/ppermute | solution.py:47
  50.7 0.9 collective-permute-start.17
  51.5 4.3 %collective-permute-done.17 = bf16[128,256]{1,0:T(8,128)(2,1)S(1)} collective-permute-done((bf16[128,256]{1,0:T(8,128)(2,1)S(1)}, bf16[128,256]{1,0:T(8,128)(2,1)S(1)}, u32[]{:S(2)}, u32[]{:S(2)}) %collective-permute-start.17) | collective-permute-done | bytes 65568 | tf_op jit(solution)/shard_map/ppermute | solution.py:47
  55.9 1.2 collective-permute-done.14
  57.5 1.3 collective-permute-start.19
  58.8 1.2 collective-permute-start.21
  60.0 0.8 collective-permute-start.20
  60.8 3.2 %collective-permute-done.19 = bf16[2,128,256]{2,1,0:T(8,128)(2,1)S(1)} collective-permute-done((bf16[2,128,256]{2,1,0:T(8,128)(2,1)S(1)}, bf16[2,128,256]{2,1,0:T(8,128)(2,1)S(1)}, u32[]{:S(2)}, u32[]{:S(2)}) %collective-permute-start.19) | collective-permute-done | bytes 131104 | tf_op jit(solution)/shard_map/ppermute | solution.py:47
  64.0 2.1 %collective-permute-done.20 = bf16[2,128,256]{2,1,0:T(8,128)(2,1)S(1)} collective-permute-done((bf16[2,128,256]{2,1,0:T(8,128)(2,1)S(1)}, bf16[2,128,256]{2,1,0:T(8,128)(2,1)S(1)}, u32[]{:S(2)}, u32[]{:S(2)}) %collective-permute-start.20) | collective-permute-done | bytes 131104 | tf_op jit(solution)/shard_map/ppermute | solution.py:47
  66.3 7.3 %collective-permute-start.22 = (bf16[2,128,256]{2,1,0:T(8,128)(2,1)S(1)}, bf16[2,128,256]{2,1,0:T(8,128)(2,1)S(1)}, u32[]{:S(2)}, u32[]{:S(2)}) collective-permute-start(bf16[2,128,256]{2,1,0:T(8,128)(2,1)S(1)} %pad_maximum_fusion.4), channel_id=1, source_target_pairs={{0,4},{1,5},{2,6},{3,7},{4,0},{5,1},{6,2},{7,3},{8,12},{9,13},{10,... | collective-permute-start | bytes 393224 | tf_op jit(solution)/shard_map/ppermute | solution.py:47
  73.6 3.9 %collective-permute-done.22 = bf16[2,128,256]{2,1,0:T(8,128)(2,1)S(1)} collective-permute-done((bf16[2,128,256]{2,1,0:T(8,128)(2,1)S(1)}, bf16[2,128,256]{2,1,0:T(8,128)(2,1)S(1)}, u32[]{:S(2)}, u32[]{:S(2)}) %collective-permute-start.22) | collective-permute-done | bytes 131104 | tf_op jit(solution)/shard_map/ppermute | solution.py:47
  77.6 1.9 %collective-permute-start.24 = (bf16[2,128,256]{2,1,0:T(8,128)(2,1)S(1)}, bf16[2,128,256]{2,1,0:T(8,128)(2,1)S(1)}, u32[]{:S(2)}, u32[]{:S(2)}) collective-permute-start(bf16[2,128,256]{2,1,0:T(8,128)(2,1)S(1)} %fusion.1), channel_id=1, source_target_pairs={{0,16},{1,17},{2,18},{3,19},{4,20},{5,21},{6,22},{7,23},{8,24},{9,... | collective-permute-start | bytes 393224 | tf_op jit(solution)/shard_map/ppermute | solution.py:47
  79.6 1.3 collective-permute-start.23
  80.9 4.3 %collective-permute-done.25 = bf16[2,128,256]{2,1,0:T(8,128)(2,1)S(1)} collective-permute-done((bf16[2,128,256]{2,1,0:T(8,128)(2,1)S(1)}, bf16[2,128,256]{2,1,0:T(8,128)(2,1)S(1)}, u32[]{:S(2)}, u32[]{:S(2)}) %collective-permute-start.25) | collective-permute-done | bytes 131104 | tf_op jit(solution)/shard_map/ppermute | solution.py:47
  85.2 0.9 collective-permute-done.23
  86.2 1.2 collective-permute-start.33
  87.3 0.9 collective-permute-start.32
  88.2 2.3 %collective-permute-start.31 = (bf16[8,128,256]{2,1,0:T(8,128)(2,1)S(1)}, bf16[8,128,256]{2,1,0:T(8,128)(2,1)S(1)}, u32[]{:S(2)}, u32[]{:S(2)}) collective-permute-start(bf16[8,128,256]{2,1,0:T(8,128)(2,1)S(1)} %pad_maximum_fusion.right), channel_id=1, source_target_pairs={{0,3},{1,0},{2,1},{3,2},{4,7},{5,4},{6,5},{7,6},{8,11},{9,8},{10,9... | collective-permute-start | bytes 1572872 | tf_op jit(solution)/shard_map/ppermute | solution.py:47
  90.5 0.6 collective-permute-start.29
  91.1 2.5 %collective-permute-start.28 = (bf16[128,256]{1,0:T(8,128)(2,1)S(1)}, bf16[128,256]{1,0:T(8,128)(2,1)S(1)}, u32[]{:S(2)}, u32[]{:S(2)}) collective-permute-start(bf16[128,256]{1,0:T(8,128)(2,1)S(1)} %slice_bitcast_fusion.7), channel_id=1, source_target_pairs={{0,128},{1,129},{2,130},{3,131},{4,132},{5,133},{6,134},{7,135},{8... | collective-permute-start | bytes 196616 | tf_op jit(solution)/shard_map/ppermute | solution.py:47
  93.6 3.0 %collective-permute-done.29 = bf16[128,256]{1,0:T(8,128)(2,1)S(1)} collective-permute-done((bf16[128,256]{1,0:T(8,128)(2,1)S(1)}, bf16[128,256]{1,0:T(8,128)(2,1)S(1)}, u32[]{:S(2)}, u32[]{:S(2)}) %collective-permute-start.29) | collective-permute-done | bytes 65568 | tf_op jit(solution)/shard_map/ppermute | solution.py:47
  96.7 1.4 collective-permute-start.27
  98.0 2.9 %collective-permute-done.27 = bf16[128,256]{1,0:T(8,128)(2,1)S(1)} collective-permute-done((bf16[128,256]{1,0:T(8,128)(2,1)S(1)}, bf16[128,256]{1,0:T(8,128)(2,1)S(1)}, u32[]{:S(2)}, u32[]{:S(2)}) %collective-permute-start.27) | collective-permute-done | bytes 65568 | tf_op jit(solution)/shard_map/ppermute | solution.py:47
  101.1 1.4 %collective-permute-done.30.u3 = bf16[3,128,256]{2,1,0:T(8,128)(2,1)S(1)} collective-permute-done((bf16[3,128,256]{2,1,0:T(8,128)(2,1)S(1)}, bf16[3,128,256]{2,1,0:T(8,128)(2,1)S(1)}, u32[]{:S(2)}, u32[]{:S(2)}) %collective-permute-start.30) | collective-permute-done | bytes 196640 | tf_op jit(solution)/shard_map/ppermute | solution.py:47
  102.5 1.4 shard_map.66
  103.9 1.8 %shard_map.67 = (f32[4,128,256]{2,1,0:T(8,128)S(1)}, bf16[4,128,256]{2,1,0:T(8,128)(2,1)S(1)}, bf16[8,128,256]{2,1,0:T(8,128)(2,1)S(1)}, bf16[8,128,256]{2,1,0:T(8,128)(2,1)S(1)}, bf16[8,128,256]{2,1,0:T(8,128)(2,1)S(1)}) custom-call(s32[24]{0:T(128)S(1)} %get-tuple-element.36.first_ref, s32[24]{0:T(128)S(1)} %get-tuple-element.37.second_ref, ...), custom_call_target="tpu_custom_call" | custom-call | tf_op jit(solution)/shard_map/pallas_call | solution.py:136
  105.9 1.4 collective-permute-start.34
  107.3 1.5 %collective-permute-start.35 = (bf16[8,128,256]{2,1,0:T(8,128)(2,1)S(1)}, bf16[8,128,256]{2,1,0:T(8,128)(2,1)S(1)}, u32[]{:S(2)}, u32[]{:S(2)}) collective-permute-start(bf16[8,128,256]{2,1,0:T(8,128)(2,1)S(1)} %get-tuple-element.61), channel_id=1, source_target_pairs={{0,1},{1,2},{2,3},{3,0},{4,5},{5,6},{6,7},{7,4},{8,9},{9,10},{10,1... | collective-permute-start | bytes 1572872 | tf_op jit(solution)/shard_map/ppermute | solution.py:47
  109.5 1.5 %collective-permute-start.38 = (bf16[128,256]{1,0:T(8,128)(2,1)S(1)}, bf16[128,256]{1,0:T(8,128)(2,1)S(1)}, u32[]{:S(2)}, u32[]{:S(2)}) collective-permute-start(bf16[128,256]{1,0:T(8,128)(2,1)S(1)} %get-tuple-element.83), channel_id=1, source_target_pairs={{0,64},{1,65},{2,66},{3,67},{4,68},{5,69},{6,70},{7,71},{8,72},{9,... | collective-permute-start | bytes 196616 | tf_op jit(solution)/shard_map/ppermute | solution.py:47
  111.0 2.9 %collective-permute-start.40 = (bf16[128,256]{1,0:T(8,128)(2,1)S(1)}, bf16[128,256]{1,0:T(8,128)(2,1)S(1)}, u32[]{:S(2)}, u32[]{:S(2)}) collective-permute-start(bf16[128,256]{1,0:T(8,128)(2,1)S(1)} %get-tuple-element.84), channel_id=1, source_target_pairs={{0,192},{1,193},{2,194},{3,195},{4,196},{5,197},{6,198},{7,199},{8... | collective-permute-start | bytes 196616 | tf_op jit(solution)/shard_map/ppermute | solution.py:47
  113.9 2.8 %collective-permute-done.38 = bf16[128,256]{1,0:T(8,128)(2,1)S(1)} collective-permute-done((bf16[128,256]{1,0:T(8,128)(2,1)S(1)}, bf16[128,256]{1,0:T(8,128)(2,1)S(1)}, u32[]{:S(2)}, u32[]{:S(2)}) %collective-permute-start.38) | collective-permute-done | bytes 65568 | tf_op jit(solution)/shard_map/ppermute | solution.py:47
  116.9 4.9 %collective-permute-done.39 = bf16[128,256]{1,0:T(8,128)(2,1)S(1)} collective-permute-done((bf16[128,256]{1,0:T(8,128)(2,1)S(1)}, bf16[128,256]{1,0:T(8,128)(2,1)S(1)}, u32[]{:S(2)}, u32[]{:S(2)}) %collective-permute-start.39) | collective-permute-done | bytes 65568 | tf_op jit(solution)/shard_map/ppermute | solution.py:47
  122.6 1.2 collective-permute-start.41
  123.8 2.1 %collective-permute-start.43 = (bf16[2,128,256]{2,1,0:T(8,128)(2,1)S(1)}, bf16[2,128,256]{2,1,0:T(8,128)(2,1)S(1)}, u32[]{:S(2)}, u32[]{:S(2)}) collective-permute-start(bf16[2,128,256]{2,1,0:T(8,128)(2,1)S(1)} %get-tuple-element.78), channel_id=1, source_target_pairs={{0,24},{1,25},{2,26},{3,27},{4,28},{5,29},{6,30},{7,31},{8,0},{9,1... | collective-permute-start | bytes 393224 | tf_op jit(solution)/shard_map/ppermute | solution.py:47
  125.9 3.2 %collective-permute-done.41 = bf16[2,128,256]{2,1,0:T(8,128)(2,1)S(1)} collective-permute-done((bf16[2,128,256]{2,1,0:T(8,128)(2,1)S(1)}, bf16[2,128,256]{2,1,0:T(8,128)(2,1)S(1)}, u32[]{:S(2)}, u32[]{:S(2)}) %collective-permute-start.41) | collective-permute-done | bytes 131104 | tf_op jit(solution)/shard_map/ppermute | solution.py:47
  129.2 1.0 collective-permute-done.43
  130.2 1.9 %collective-permute-done.42 = bf16[2,128,256]{2,1,0:T(8,128)(2,1)S(1)} collective-permute-done((bf16[2,128,256]{2,1,0:T(8,128)(2,1)S(1)}, bf16[2,128,256]{2,1,0:T(8,128)(2,1)S(1)}, u32[]{:S(2)}, u32[]{:S(2)}) %collective-permute-start.42) | collective-permute-done | bytes 131104 | tf_op jit(solution)/shard_map/ppermute | solution.py:47
  132.2 6.1 %collective-permute-start.44 = (bf16[128,256]{1,0:T(8,128)(2,1)S(1)}, bf16[128,256]{1,0:T(8,128)(2,1)S(1)}, u32[]{:S(2)}, u32[]{:S(2)}) collective-permute-start(bf16[128,256]{1,0:T(8,128)(2,1)S(1)} %fusion.10), channel_id=1, source_target_pairs={{0,4},{1,5},{2,6},{3,7},{4,0},{5,1},{6,2},{7,3},{8,12},{9,13},{10,... | collective-permute-start | bytes 196616 | tf_op jit(solution)/shard_map/ppermute | solution.py:47
  138.3 2.2 %collective-permute-done.44 = bf16[128,256]{1,0:T(8,128)(2,1)S(1)} collective-permute-done((bf16[128,256]{1,0:T(8,128)(2,1)S(1)}, bf16[128,256]{1,0:T(8,128)(2,1)S(1)}, u32[]{:S(2)}, u32[]{:S(2)}) %collective-permute-start.44) | collective-permute-done | bytes 65568 | tf_op jit(solution)/shard_map/ppermute | solution.py:47
  140.6 0.7 fusion.9
  (73 shorter events, 3.9 us)
Async XLA Ops:
  0.0 9.9 %collective-permute-start = (bf16[128,256]{1,0:T(8,128)(2,1)}, bf16[128,256]{1,0:T(8,128)(2,1)S(1)}, u32[]{:S(2)}, u32[]{:S(2)}) collective-permute-start(bf16[128,256]{1,0:T(8,128)(2,1)} %param.6), channel_id=1, source_target_pairs={{0,4},{1,5},{2,6},{3,7},{4,0},{5,1},{6,2},{7,3},{8,12},{9,13},{10,... | collective-permute-start | bytes 196616 | tf_op jit(solution)/shard_map/ppermute | solution.py:47
  7.2 2.8 %copy-start.2 = (bf16[128,256]{1,0:T(8,128)(2,1)S(1)}, bf16[128,256]{1,0:T(8,128)(2,1)}, u32[]{:S(2)}) copy-start(bf16[128,256]{1,0:T(8,128)(2,1)} %param.6) | copy-start | bytes 196612
  8.1 0.7 copy-start.3
  8.1 0.7 copy-start.4
  9.9 27.4 %copy-start = (bf16[24,128,128]{2,1,0:T(8,128)(2,1)S(1)}, bf16[24,128,128]{2,1,0:T(8,128)(2,1)}, u32[]{:S(2)}) copy-start(bf16[24,128,128]{2,1,0:T(8,128)(2,1)} %wins.7) | copy-start | bytes 2359300
  9.9 27.4 %copy-start.1 = (bf16[24,128,128]{2,1,0:T(8,128)(2,1)S(1)}, bf16[24,128,128]{2,1,0:T(8,128)(2,1)}, u32[]{:S(2)}) copy-start(bf16[24,128,128]{2,1,0:T(8,128)(2,1)} %losses.7) | copy-start | bytes 2359300
  10.0 8.1 %collective-permute-start.2 = (bf16[2,128,256]{2,1,0:T(8,128)(2,1)S(1)}, bf16[2,128,256]{2,1,0:T(8,128)(2,1)S(1)}, u32[]{:S(2)}, u32[]{:S(2)}) collective-permute-start(bf16[2,128,256]{2,1,0:T(8,128)(2,1)S(1)} %pad_maximum_fusion.3), channel_id=1, source_target_pairs={{0,16},{1,17},{2,18},{3,19},{4,20},{5,21},{6,22},{7,23},{8,24},{9,... | collective-permute-start | bytes 393224 | tf_op jit(solution)/shard_map/ppermute | solution.py:47
  13.1 5.0 %collective-permute-start.1 = (bf16[2,128,256]{2,1,0:T(8,128)(2,1)S(1)}, bf16[2,128,256]{2,1,0:T(8,128)(2,1)S(1)}, u32[]{:S(2)}, u32[]{:S(2)}) collective-permute-start(bf16[2,128,256]{2,1,0:T(8,128)(2,1)S(1)} %pad_maximum_fusion.3), channel_id=1, source_target_pairs={{0,24},{1,25},{2,26},{3,27},{4,28},{5,29},{6,30},{7,31},{8,0},{9,1... | collective-permute-start | bytes 393224 | tf_op jit(solution)/shard_map/ppermute | solution.py:47
  14.2 6.2 %collective-permute-start.3 = (bf16[2,128,256]{2,1,0:T(8,128)(2,1)S(1)}, bf16[2,128,256]{2,1,0:T(8,128)(2,1)S(1)}, u32[]{:S(2)}, u32[]{:S(2)}) collective-permute-start(bf16[2,128,256]{2,1,0:T(8,128)(2,1)S(1)} %pad_maximum_fusion.3), channel_id=1, source_target_pairs={{0,8},{1,9},{2,10},{3,11},{4,12},{5,13},{6,14},{7,15},{8,16},{9,17... | collective-permute-start | bytes 393224 | tf_op jit(solution)/shard_map/ppermute | solution.py:47
  15.1 5.3 %collective-permute-start.4 = (bf16[128,256]{1,0:T(8,128)(2,1)S(1)}, bf16[128,256]{1,0:T(8,128)(2,1)S(1)}, u32[]{:S(2)}, u32[]{:S(2)}) collective-permute-start(bf16[128,256]{1,0:T(8,128)(2,1)S(1)} %copy-done.2), channel_id=1, source_target_pairs={{0,32},{1,33},{2,34},{3,35},{4,36},{5,37},{6,38},{7,39},{8,40},{9,... | collective-permute-start | bytes 196616 | tf_op jit(solution)/shard_map/ppermute | solution.py:47
  20.4 18.3 %collective-permute-start.11 = (bf16[8,128,256]{2,1,0:T(8,128)(2,1)S(1)}, bf16[8,128,256]{2,1,0:T(8,128)(2,1)S(1)}, u32[]{:S(2)}, u32[]{:S(2)}) collective-permute-start(bf16[8,128,256]{2,1,0:T(8,128)(2,1)S(1)} %constant_dynamic-update-slice_fusion.right), channel_id=1, source_target_pairs={{0,1},{1,2},{2,3},{3,0},{4,5},{5,6},{6,7},{7,4},{8,9},{9,10},{10,1... | collective-permute-start | bytes 1572872 | tf_op jit(solution)/shard_map/ppermute | solution.py:47
  22.1 16.6 %collective-permute-start.10 = (bf16[8,128,256]{2,1,0:T(8,128)(2,1)S(1)}, bf16[8,128,256]{2,1,0:T(8,128)(2,1)S(1)}, u32[]{:S(2)}, u32[]{:S(2)}) collective-permute-start(bf16[8,128,256]{2,1,0:T(8,128)(2,1)S(1)} %constant_dynamic-update-slice_fusion.right), channel_id=1, source_target_pairs={{0,2},{1,3},{2,0},{3,1},{4,6},{5,7},{6,4},{7,5},{8,10},{9,11},{10,... | collective-permute-start | bytes 1572872 | tf_op jit(solution)/shard_map/ppermute | solution.py:47
  23.0 15.7 %collective-permute-start.9 = (bf16[8,128,256]{2,1,0:T(8,128)(2,1)S(1)}, bf16[8,128,256]{2,1,0:T(8,128)(2,1)S(1)}, u32[]{:S(2)}, u32[]{:S(2)}) collective-permute-start(bf16[8,128,256]{2,1,0:T(8,128)(2,1)S(1)} %constant_dynamic-update-slice_fusion.right), channel_id=1, source_target_pairs={{0,3},{1,0},{2,1},{3,2},{4,7},{5,4},{6,5},{7,6},{8,11},{9,8},{10,9... | collective-permute-start | bytes 1572872 | tf_op jit(solution)/shard_map/ppermute | solution.py:47
  25.5 6.1 %collective-permute-start.7 = (bf16[128,256]{1,0:T(8,128)(2,1)S(1)}, bf16[128,256]{1,0:T(8,128)(2,1)S(1)}, u32[]{:S(2)}, u32[]{:S(2)}) collective-permute-start(bf16[128,256]{1,0:T(8,128)(2,1)S(1)} %copy-done.2), channel_id=1, source_target_pairs={{0,64},{1,65},{2,66},{3,67},{4,68},{5,69},{6,70},{7,71},{8,72},{9,... | collective-permute-start | bytes 196616 | tf_op jit(solution)/shard_map/ppermute | solution.py:47
  27.2 5.9 %collective-permute-start.6 = (bf16[128,256]{1,0:T(8,128)(2,1)S(1)}, bf16[128,256]{1,0:T(8,128)(2,1)S(1)}, u32[]{:S(2)}, u32[]{:S(2)}) collective-permute-start(bf16[128,256]{1,0:T(8,128)(2,1)S(1)} %copy-done.2), channel_id=1, source_target_pairs={{0,128},{1,129},{2,130},{3,131},{4,132},{5,133},{6,134},{7,135},{8... | collective-permute-start | bytes 196616 | tf_op jit(solution)/shard_map/ppermute | solution.py:47
  31.5 4.3 %collective-permute-start.5 = (bf16[128,256]{1,0:T(8,128)(2,1)S(1)}, bf16[128,256]{1,0:T(8,128)(2,1)S(1)}, u32[]{:S(2)}, u32[]{:S(2)}) collective-permute-start(bf16[128,256]{1,0:T(8,128)(2,1)S(1)} %copy-done.2), channel_id=1, source_target_pairs={{0,192},{1,193},{2,194},{3,195},{4,196},{5,197},{6,198},{7,199},{8... | collective-permute-start | bytes 196616 | tf_op jit(solution)/shard_map/ppermute | solution.py:47
  35.8 1.5 %collective-permute-start.8 = (bf16[3,128,256]{2,1,0:T(8,128)(2,1)S(1)}, bf16[3,128,256]{2,1,0:T(8,128)(2,1)S(1)}, u32[]{:S(2)}, u32[]{:S(2)}) collective-permute-start(bf16[3,128,256]{2,1,0:T(8,128)(2,1)S(1)} %pad_maximum_fusion.1.u1), channel_id=1, source_target_pairs={{0,32},{1,33},{2,34},{3,35},{4,36},{5,37},{6,38},{7,39},{8,40},{9,... | collective-permute-start | bytes 589832 | tf_op jit(solution)/shard_map/ppermute | solution.py:47
  40.6 3.5 %collective-permute-start.15 = (bf16[4,128,256]{2,1,0:T(8,128)(2,1)S(1)}, bf16[4,128,256]{2,1,0:T(8,128)(2,1)S(1)}, u32[]{:S(2)}, u32[]{:S(2)}) collective-permute-start(bf16[4,128,256]{2,1,0:T(8,128)(2,1)S(1)} %get-tuple-element.50), channel_id=1, source_target_pairs={{0,32},{1,33},{2,34},{3,35},{4,36},{5,37},{6,38},{7,39},{8,40},{9,... | collective-permute-start | bytes 786440 | tf_op jit(solution)/shard_map/ppermute | solution.py:47
  40.8 15.1 %collective-permute-start.12 = (bf16[8,128,256]{2,1,0:T(8,128)(2,1)S(1)}, bf16[8,128,256]{2,1,0:T(8,128)(2,1)S(1)}, u32[]{:S(2)}, u32[]{:S(2)}) collective-permute-start(bf16[8,128,256]{2,1,0:T(8,128)(2,1)S(1)} %get-tuple-element.46), channel_id=1, source_target_pairs={{0,2},{1,3},{2,0},{3,1},{4,6},{5,7},{6,4},{7,5},{8,10},{9,11},{10,... | collective-permute-start | bytes 1572872 | tf_op jit(solution)/shard_map/ppermute | solution.py:47
  42.0 13.9 %collective-permute-start.13 = (bf16[8,128,256]{2,1,0:T(8,128)(2,1)S(1)}, bf16[8,128,256]{2,1,0:T(8,128)(2,1)S(1)}, u32[]{:S(2)}, u32[]{:S(2)}) collective-permute-start(bf16[8,128,256]{2,1,0:T(8,128)(2,1)S(1)} %get-tuple-element.47), channel_id=1, source_target_pairs={{0,1},{1,2},{2,3},{3,0},{4,5},{5,6},{6,7},{7,4},{8,9},{9,10},{10,1... | collective-permute-start | bytes 1572872 | tf_op jit(solution)/shard_map/ppermute | solution.py:47
  43.6 13.5 %collective-permute-start.14 = (bf16[8,128,256]{2,1,0:T(8,128)(2,1)S(1)}, bf16[8,128,256]{2,1,0:T(8,128)(2,1)S(1)}, u32[]{:S(2)}, u32[]{:S(2)}) collective-permute-start(bf16[8,128,256]{2,1,0:T(8,128)(2,1)S(1)} %get-tuple-element.48), channel_id=1, source_target_pairs={{0,3},{1,0},{2,1},{3,2},{4,7},{5,4},{6,5},{7,6},{8,11},{9,8},{10,9... | collective-permute-start | bytes 1572872 | tf_op jit(solution)/shard_map/ppermute | solution.py:47
  44.2 6.5 %collective-permute-start.16 = (bf16[128,256]{1,0:T(8,128)(2,1)S(1)}, bf16[128,256]{1,0:T(8,128)(2,1)S(1)}, u32[]{:S(2)}, u32[]{:S(2)}) collective-permute-start(bf16[128,256]{1,0:T(8,128)(2,1)S(1)} %get-tuple-element.90), channel_id=1, source_target_pairs={{0,64},{1,65},{2,66},{3,67},{4,68},{5,69},{6,70},{7,71},{8,72},{9,... | collective-permute-start | bytes 196616 | tf_op jit(solution)/shard_map/ppermute | solution.py:47
  45.3 6.2 %collective-permute-start.18 = (bf16[128,256]{1,0:T(8,128)(2,1)S(1)}, bf16[128,256]{1,0:T(8,128)(2,1)S(1)}, u32[]{:S(2)}, u32[]{:S(2)}) collective-permute-start(bf16[128,256]{1,0:T(8,128)(2,1)S(1)} %get-tuple-element.91), channel_id=1, source_target_pairs={{0,192},{1,193},{2,194},{3,195},{4,196},{5,197},{6,198},{7,199},{8... | collective-permute-start | bytes 196616 | tf_op jit(solution)/shard_map/ppermute | solution.py:47
  50.7 5.2 %collective-permute-start.17 = (bf16[128,256]{1,0:T(8,128)(2,1)S(1)}, bf16[128,256]{1,0:T(8,128)(2,1)S(1)}, u32[]{:S(2)}, u32[]{:S(2)}) collective-permute-start(bf16[128,256]{1,0:T(8,128)(2,1)S(1)} %get-tuple-element.92), channel_id=1, source_target_pairs={{0,128},{1,129},{2,130},{3,131},{4,132},{5,133},{6,134},{7,135},{8... | collective-permute-start | bytes 196616 | tf_op jit(solution)/shard_map/ppermute | solution.py:47
  57.5 6.6 %collective-permute-start.19 = (bf16[2,128,256]{2,1,0:T(8,128)(2,1)S(1)}, bf16[2,128,256]{2,1,0:T(8,128)(2,1)S(1)}, u32[]{:S(2)}, u32[]{:S(2)}) collective-permute-start(bf16[2,128,256]{2,1,0:T(8,128)(2,1)S(1)} %get-tuple-element.80), channel_id=1, source_target_pairs={{0,16},{1,17},{2,18},{3,19},{4,20},{5,21},{6,22},{7,23},{8,24},{9,... | collective-permute-start | bytes 393224 | tf_op jit(solution)/shard_map/ppermute | solution.py:47
  58.8 5.3 %collective-permute-start.21 = (bf16[2,128,256]{2,1,0:T(8,128)(2,1)S(1)}, bf16[2,128,256]{2,1,0:T(8,128)(2,1)S(1)}, u32[]{:S(2)}, u32[]{:S(2)}) collective-permute-start(bf16[2,128,256]{2,1,0:T(8,128)(2,1)S(1)} %get-tuple-element.81), channel_id=1, source_target_pairs={{0,24},{1,25},{2,26},{3,27},{4,28},{5,29},{6,30},{7,31},{8,0},{9,1... | collective-permute-start | bytes 393224 | tf_op jit(solution)/shard_map/ppermute | solution.py:47
  60.0 6.2 %collective-permute-start.20 = (bf16[2,128,256]{2,1,0:T(8,128)(2,1)S(1)}, bf16[2,128,256]{2,1,0:T(8,128)(2,1)S(1)}, u32[]{:S(2)}, u32[]{:S(2)}) collective-permute-start(bf16[2,128,256]{2,1,0:T(8,128)(2,1)S(1)} %get-tuple-element.82), channel_id=1, source_target_pairs={{0,8},{1,9},{2,10},{3,11},{4,12},{5,13},{6,14},{7,15},{8,16},{9,17... | collective-permute-start | bytes 393224 | tf_op jit(solution)/shard_map/ppermute | solution.py:47
  66.3 11.1 %collective-permute-start.22 = (bf16[2,128,256]{2,1,0:T(8,128)(2,1)S(1)}, bf16[2,128,256]{2,1,0:T(8,128)(2,1)S(1)}, u32[]{:S(2)}, u32[]{:S(2)}) collective-permute-start(bf16[2,128,256]{2,1,0:T(8,128)(2,1)S(1)} %pad_maximum_fusion.4), channel_id=1, source_target_pairs={{0,4},{1,5},{2,6},{3,7},{4,0},{5,1},{6,2},{7,3},{8,12},{9,13},{10,... | collective-permute-start | bytes 393224 | tf_op jit(solution)/shard_map/ppermute | solution.py:47
  77.5 7.7 %collective-permute-start.25 = (bf16[2,128,256]{2,1,0:T(8,128)(2,1)S(1)}, bf16[2,128,256]{2,1,0:T(8,128)(2,1)S(1)}, u32[]{:S(2)}, u32[]{:S(2)}) collective-permute-start(bf16[2,128,256]{2,1,0:T(8,128)(2,1)S(1)} %fusion.1), channel_id=1, source_target_pairs={{0,8},{1,9},{2,10},{3,11},{4,12},{5,13},{6,14},{7,15},{8,16},{9,17... | collective-permute-start | bytes 393224 | tf_op jit(solution)/shard_map/ppermute | solution.py:47
  77.6 7.6 %collective-permute-start.24 = (bf16[2,128,256]{2,1,0:T(8,128)(2,1)S(1)}, bf16[2,128,256]{2,1,0:T(8,128)(2,1)S(1)}, u32[]{:S(2)}, u32[]{:S(2)}) collective-permute-start(bf16[2,128,256]{2,1,0:T(8,128)(2,1)S(1)} %fusion.1), channel_id=1, source_target_pairs={{0,16},{1,17},{2,18},{3,19},{4,20},{5,21},{6,22},{7,23},{8,24},{9,... | collective-permute-start | bytes 393224 | tf_op jit(solution)/shard_map/ppermute | solution.py:47
  79.6 6.5 %collective-permute-start.23 = (bf16[2,128,256]{2,1,0:T(8,128)(2,1)S(1)}, bf16[2,128,256]{2,1,0:T(8,128)(2,1)S(1)}, u32[]{:S(2)}, u32[]{:S(2)}) collective-permute-start(bf16[2,128,256]{2,1,0:T(8,128)(2,1)S(1)} %fusion.1), channel_id=1, source_target_pairs={{0,24},{1,25},{2,26},{3,27},{4,28},{5,29},{6,30},{7,31},{8,0},{9,1... | collective-permute-start | bytes 393224 | tf_op jit(solution)/shard_map/ppermute | solution.py:47
  80.9 5.3 %collective-permute-start.26 = (bf16[128,256]{1,0:T(8,128)(2,1)S(1)}, bf16[128,256]{1,0:T(8,128)(2,1)S(1)}, u32[]{:S(2)}, u32[]{:S(2)}) collective-permute-start(bf16[128,256]{1,0:T(8,128)(2,1)S(1)} %slice_bitcast_fusion.7), channel_id=1, source_target_pairs={{0,32},{1,33},{2,34},{3,35},{4,36},{5,37},{6,38},{7,39},{8,40},{9,... | collective-permute-start | bytes 196616 | tf_op jit(solution)/shard_map/ppermute | solution.py:47
  86.2 17.7 %collective-permute-start.33 = (bf16[8,128,256]{2,1,0:T(8,128)(2,1)S(1)}, bf16[8,128,256]{2,1,0:T(8,128)(2,1)S(1)}, u32[]{:S(2)}, u32[]{:S(2)}) collective-permute-start(bf16[8,128,256]{2,1,0:T(8,128)(2,1)S(1)} %pad_maximum_fusion.right), channel_id=1, source_target_pairs={{0,1},{1,2},{2,3},{3,0},{4,5},{5,6},{6,7},{7,4},{8,9},{9,10},{10,1... | collective-permute-start | bytes 1572872 | tf_op jit(solution)/shard_map/ppermute | solution.py:47
  87.3 16.5 %collective-permute-start.32 = (bf16[8,128,256]{2,1,0:T(8,128)(2,1)S(1)}, bf16[8,128,256]{2,1,0:T(8,128)(2,1)S(1)}, u32[]{:S(2)}, u32[]{:S(2)}) collective-permute-start(bf16[8,128,256]{2,1,0:T(8,128)(2,1)S(1)} %pad_maximum_fusion.right), channel_id=1, source_target_pairs={{0,2},{1,3},{2,0},{3,1},{4,6},{5,7},{6,4},{7,5},{8,10},{9,11},{10,... | collective-permute-start | bytes 1572872 | tf_op jit(solution)/shard_map/ppermute | solution.py:47
  88.2 15.7 %collective-permute-start.31 = (bf16[8,128,256]{2,1,0:T(8,128)(2,1)S(1)}, bf16[8,128,256]{2,1,0:T(8,128)(2,1)S(1)}, u32[]{:S(2)}, u32[]{:S(2)}) collective-permute-start(bf16[8,128,256]{2,1,0:T(8,128)(2,1)S(1)} %pad_maximum_fusion.right), channel_id=1, source_target_pairs={{0,3},{1,0},{2,1},{3,2},{4,7},{5,4},{6,5},{7,6},{8,11},{9,8},{10,9... | collective-permute-start | bytes 1572872 | tf_op jit(solution)/shard_map/ppermute | solution.py:47
  90.5 6.2 %collective-permute-start.29 = (bf16[128,256]{1,0:T(8,128)(2,1)S(1)}, bf16[128,256]{1,0:T(8,128)(2,1)S(1)}, u32[]{:S(2)}, u32[]{:S(2)}) collective-permute-start(bf16[128,256]{1,0:T(8,128)(2,1)S(1)} %slice_bitcast_fusion.7), channel_id=1, source_target_pairs={{0,64},{1,65},{2,66},{3,67},{4,68},{5,69},{6,70},{7,71},{8,72},{9,... | collective-permute-start | bytes 196616 | tf_op jit(solution)/shard_map/ppermute | solution.py:47
  91.1 6.9 %collective-permute-start.28 = (bf16[128,256]{1,0:T(8,128)(2,1)S(1)}, bf16[128,256]{1,0:T(8,128)(2,1)S(1)}, u32[]{:S(2)}, u32[]{:S(2)}) collective-permute-start(bf16[128,256]{1,0:T(8,128)(2,1)S(1)} %slice_bitcast_fusion.7), channel_id=1, source_target_pairs={{0,128},{1,129},{2,130},{3,131},{4,132},{5,133},{6,134},{7,135},{8... | collective-permute-start | bytes 196616 | tf_op jit(solution)/shard_map/ppermute | solution.py:47
  96.7 4.3 %collective-permute-start.27 = (bf16[128,256]{1,0:T(8,128)(2,1)S(1)}, bf16[128,256]{1,0:T(8,128)(2,1)S(1)}, u32[]{:S(2)}, u32[]{:S(2)}) collective-permute-start(bf16[128,256]{1,0:T(8,128)(2,1)S(1)} %slice_bitcast_fusion.7), channel_id=1, source_target_pairs={{0,192},{1,193},{2,194},{3,195},{4,196},{5,197},{6,198},{7,199},{8... | collective-permute-start | bytes 196616 | tf_op jit(solution)/shard_map/ppermute | solution.py:47
  101.0 1.5 %collective-permute-start.30 = (bf16[3,128,256]{2,1,0:T(8,128)(2,1)S(1)}, bf16[3,128,256]{2,1,0:T(8,128)(2,1)S(1)}, u32[]{:S(2)}, u32[]{:S(2)}) collective-permute-start(bf16[3,128,256]{2,1,0:T(8,128)(2,1)S(1)} %pad_maximum_fusion.2.u1), channel_id=1, source_target_pairs={{0,32},{1,33},{2,34},{3,35},{4,36},{5,37},{6,38},{7,39},{8,40},{9,... | collective-permute-start | bytes 589832 | tf_op jit(solution)/shard_map/ppermute | solution.py:47
  105.7 3.7 %collective-permute-start.37 = (bf16[4,128,256]{2,1,0:T(8,128)(2,1)S(1)}, bf16[4,128,256]{2,1,0:T(8,128)(2,1)S(1)}, u32[]{:S(2)}, u32[]{:S(2)}) collective-permute-start(bf16[4,128,256]{2,1,0:T(8,128)(2,1)S(1)} %get-tuple-element.64), channel_id=1, source_target_pairs={{0,32},{1,33},{2,34},{3,35},{4,36},{5,37},{6,38},{7,39},{8,40},{9,... | collective-permute-start | bytes 786440 | tf_op jit(solution)/shard_map/ppermute | solution.py:47
  105.9 15.9 %collective-permute-start.34 = (bf16[8,128,256]{2,1,0:T(8,128)(2,1)S(1)}, bf16[8,128,256]{2,1,0:T(8,128)(2,1)S(1)}, u32[]{:S(2)}, u32[]{:S(2)}) collective-permute-start(bf16[8,128,256]{2,1,0:T(8,128)(2,1)S(1)} %get-tuple-element.60), channel_id=1, source_target_pairs={{0,2},{1,3},{2,0},{3,1},{4,6},{5,7},{6,4},{7,5},{8,10},{9,11},{10,... | collective-permute-start | bytes 1572872 | tf_op jit(solution)/shard_map/ppermute | solution.py:47
  107.3 14.9 %collective-permute-start.35 = (bf16[8,128,256]{2,1,0:T(8,128)(2,1)S(1)}, bf16[8,128,256]{2,1,0:T(8,128)(2,1)S(1)}, u32[]{:S(2)}, u32[]{:S(2)}) collective-permute-start(bf16[8,128,256]{2,1,0:T(8,128)(2,1)S(1)} %get-tuple-element.61), channel_id=1, source_target_pairs={{0,1},{1,2},{2,3},{3,0},{4,5},{5,6},{6,7},{7,4},{8,9},{9,10},{10,1... | collective-permute-start | bytes 1572872 | tf_op jit(solution)/shard_map/ppermute | solution.py:47
  108.9 13.4 %collective-permute-start.36 = (bf16[8,128,256]{2,1,0:T(8,128)(2,1)S(1)}, bf16[8,128,256]{2,1,0:T(8,128)(2,1)S(1)}, u32[]{:S(2)}, u32[]{:S(2)}) collective-permute-start(bf16[8,128,256]{2,1,0:T(8,128)(2,1)S(1)} %get-tuple-element.62), channel_id=1, source_target_pairs={{0,3},{1,0},{2,1},{3,2},{4,7},{5,4},{6,5},{7,6},{8,11},{9,8},{10,9... | collective-permute-start | bytes 1572872 | tf_op jit(solution)/shard_map/ppermute | solution.py:47
  109.5 7.1 %collective-permute-start.38 = (bf16[128,256]{1,0:T(8,128)(2,1)S(1)}, bf16[128,256]{1,0:T(8,128)(2,1)S(1)}, u32[]{:S(2)}, u32[]{:S(2)}) collective-permute-start(bf16[128,256]{1,0:T(8,128)(2,1)S(1)} %get-tuple-element.83), channel_id=1, source_target_pairs={{0,64},{1,65},{2,66},{3,67},{4,68},{5,69},{6,70},{7,71},{8,72},{9,... | collective-permute-start | bytes 196616 | tf_op jit(solution)/shard_map/ppermute | solution.py:47
  111.0 5.9 %collective-permute-start.40 = (bf16[128,256]{1,0:T(8,128)(2,1)S(1)}, bf16[128,256]{1,0:T(8,128)(2,1)S(1)}, u32[]{:S(2)}, u32[]{:S(2)}) collective-permute-start(bf16[128,256]{1,0:T(8,128)(2,1)S(1)} %get-tuple-element.84), channel_id=1, source_target_pairs={{0,192},{1,193},{2,194},{3,195},{4,196},{5,197},{6,198},{7,199},{8... | collective-permute-start | bytes 196616 | tf_op jit(solution)/shard_map/ppermute | solution.py:47
  116.6 5.2 %collective-permute-start.39 = (bf16[128,256]{1,0:T(8,128)(2,1)S(1)}, bf16[128,256]{1,0:T(8,128)(2,1)S(1)}, u32[]{:S(2)}, u32[]{:S(2)}) collective-permute-start(bf16[128,256]{1,0:T(8,128)(2,1)S(1)} %get-tuple-element.85), channel_id=1, source_target_pairs={{0,128},{1,129},{2,130},{3,131},{4,132},{5,133},{6,134},{7,135},{8... | collective-permute-start | bytes 196616 | tf_op jit(solution)/shard_map/ppermute | solution.py:47
  122.6 6.6 %collective-permute-start.41 = (bf16[2,128,256]{2,1,0:T(8,128)(2,1)S(1)}, bf16[2,128,256]{2,1,0:T(8,128)(2,1)S(1)}, u32[]{:S(2)}, u32[]{:S(2)}) collective-permute-start(bf16[2,128,256]{2,1,0:T(8,128)(2,1)S(1)} %get-tuple-element.77), channel_id=1, source_target_pairs={{0,16},{1,17},{2,18},{3,19},{4,20},{5,21},{6,22},{7,23},{8,24},{9,... | collective-permute-start | bytes 393224 | tf_op jit(solution)/shard_map/ppermute | solution.py:47
  123.8 6.3 %collective-permute-start.43 = (bf16[2,128,256]{2,1,0:T(8,128)(2,1)S(1)}, bf16[2,128,256]{2,1,0:T(8,128)(2,1)S(1)}, u32[]{:S(2)}, u32[]{:S(2)}) collective-permute-start(bf16[2,128,256]{2,1,0:T(8,128)(2,1)S(1)} %get-tuple-element.78), channel_id=1, source_target_pairs={{0,24},{1,25},{2,26},{3,27},{4,28},{5,29},{6,30},{7,31},{8,0},{9,1... | collective-permute-start | bytes 393224 | tf_op jit(solution)/shard_map/ppermute | solution.py:47
  125.9 6.2 %collective-permute-start.42 = (bf16[2,128,256]{2,1,0:T(8,128)(2,1)S(1)}, bf16[2,128,256]{2,1,0:T(8,128)(2,1)S(1)}, u32[]{:S(2)}, u32[]{:S(2)}) collective-permute-start(bf16[2,128,256]{2,1,0:T(8,128)(2,1)S(1)} %get-tuple-element.79), channel_id=1, source_target_pairs={{0,8},{1,9},{2,10},{3,11},{4,12},{5,13},{6,14},{7,15},{8,16},{9,17... | collective-permute-start | bytes 393224 | tf_op jit(solution)/shard_map/ppermute | solution.py:47
  132.2 8.3 %collective-permute-start.44 = (bf16[128,256]{1,0:T(8,128)(2,1)S(1)}, bf16[128,256]{1,0:T(8,128)(2,1)S(1)}, u32[]{:S(2)}, u32[]{:S(2)}) collective-permute-start(bf16[128,256]{1,0:T(8,128)(2,1)S(1)} %fusion.10), channel_id=1, source_target_pairs={{0,4},{1,5},{2,6},{3,7},{4,0},{5,1},{6,2},{7,3},{8,12},{9,13},{10,... | collective-permute-start | bytes 196616 | tf_op jit(solution)/shard_map/ppermute | solution.py:47

commit v6 on v4

--- a/solution.py
+++ b/solution.py
@@ -174,7 +174,8 @@
         other = send(block, shift("core", 1))
         line = jnp.concatenate(inner_parts)
         line, block, other = lax.optimization_barrier((line, block, other))
-        mine = jnp.stack([send(block, shift("zl", -k)) for k in (1, 2, 3)])
+        mine = {k: send(block, shift("zl", -k)) for k in (2, 1, 3)}
+        mine = jnp.stack([mine[k] for k in (1, 2, 3)])
         theirs = send(mine, shift("core", 1))
         left_parts = (block[None], mine, other[None], theirs)
         right_parts = {k: send(line, shift_by_core(outer_axes, -k)) for k in (1, 3, 2)}

time: 142 us -> 142 us (level)
  waiting for transfers between devices: 64.7 us -> 62.8 us
  starting transfers between devices: 64.3 us -> 66 us
    ppermute x45, waiting for transfers between devices: 64.7 us -> 62.8 us  [send(): return lax.ppermute(values, AXES, pairs)]
    ppermute x45, starting transfers between devices: 64.3 us -> 66 us  [send(): return lax.ppermute(values, AXES, pairs)]
where the time goes in v6:
time: 142 us
  starting transfers between devices  66 us (46%)
  waiting for transfers between devices  62.8 us (44%)
  Pallas kernels  8.07 us (6%)
  other arithmetic  1.97 us (1%)
  local copies, waits for them, and re-layouts  1.71 us (1%)
    ppermute x45, starting transfers between devices, send(): return lax.ppermute(values, AXES, pairs)  66 us
    ppermute x45, waiting for transfers between devices, send(): return lax.ppermute(values, AXES, pairs)  62.8 us
    pallas_call x4, Pallas kernels, call(): pl.pallas_call(kernel, out_shape=[jax.ShapeDtypeStruct((count, tile, widt...  8.07 us
  transfers between devices with their start and end apart: 45, of which 27 were waited for; matrix products, arithmetic and copies ran while one was open for 1% of the time, Pallas kernels for 2%

profile of v6, /device:TPU:8, one launch (start us, length us, event | category | flops | bytes accessed | tf_op | source)
XLA Modules:
  0.0 141.6 jit_solution(17426361001837979392)
XLA Ops:
  0.0 7.2 %collective-permute-start = (bf16[128,256]{1,0:T(8,128)(2,1)}, bf16[128,256]{1,0:T(8,128)(2,1)S(1)}, u32[]{:S(2)}, u32[]{:S(2)}) collective-permute-start(bf16[128,256]{1,0:T(8,128)(2,1)} %param.6), channel_id=1, source_target_pairs={{0,4},{1,5},{2,6},{3,7},{4,0},{5,1},{6,2},{7,3},{8,12},{9,13},{10,... | collective-permute-start | bytes 196616 | tf_op jit(solution)/shard_map/ppermute | solution.py:47
  7.2 0.9 constant_dynamic-update-slice_fusion.4
  8.1 0.6 copy-done.3
  8.8 1.1 collective-permute-done
  10.0 3.1 %collective-permute-start.2 = (bf16[2,128,256]{2,1,0:T(8,128)(2,1)S(1)}, bf16[2,128,256]{2,1,0:T(8,128)(2,1)S(1)}, u32[]{:S(2)}, u32[]{:S(2)}) collective-permute-start(bf16[2,128,256]{2,1,0:T(8,128)(2,1)S(1)} %pad_maximum_fusion.3), channel_id=1, source_target_pairs={{0,16},{1,17},{2,18},{3,19},{4,20},{5,21},{6,22},{7,23},{8,24},{9,... | collective-permute-start | bytes 393224 | tf_op jit(solution)/shard_map/ppermute | solution.py:47
  13.1 1.1 collective-permute-start.1
  14.2 0.9 collective-permute-start.3
  15.1 2.9 %collective-permute-done.1 = bf16[2,128,256]{2,1,0:T(8,128)(2,1)S(1)} collective-permute-done((bf16[2,128,256]{2,1,0:T(8,128)(2,1)S(1)}, bf16[2,128,256]{2,1,0:T(8,128)(2,1)S(1)}, u32[]{:S(2)}, u32[]{:S(2)}) %collective-permute-start.1) | collective-permute-done | bytes 131104 | tf_op jit(solution)/shard_map/ppermute | solution.py:47
  18.1 2.3 %collective-permute-done.3 = bf16[2,128,256]{2,1,0:T(8,128)(2,1)S(1)} collective-permute-done((bf16[2,128,256]{2,1,0:T(8,128)(2,1)S(1)}, bf16[2,128,256]{2,1,0:T(8,128)(2,1)S(1)}, u32[]{:S(2)}, u32[]{:S(2)}) %collective-permute-start.3) | collective-permute-done | bytes 131104 | tf_op jit(solution)/shard_map/ppermute | solution.py:47
  20.4 1.7 %collective-permute-start.11 = (bf16[8,128,256]{2,1,0:T(8,128)(2,1)S(1)}, bf16[8,128,256]{2,1,0:T(8,128)(2,1)S(1)}, u32[]{:S(2)}, u32[]{:S(2)}) collective-permute-start(bf16[8,128,256]{2,1,0:T(8,128)(2,1)S(1)} %constant_dynamic-update-slice_fusion.right), channel_id=1, source_target_pairs={{0,1},{1,2},{2,3},{3,0},{4,5},{5,6},{6,7},{7,4},{8,9},{9,10},{10,1... | collective-permute-start | bytes 1572872 | tf_op jit(solution)/shard_map/ppermute | solution.py:47
  22.1 0.9 collective-permute-start.10
  23.0 2.4 %collective-permute-start.9 = (bf16[8,128,256]{2,1,0:T(8,128)(2,1)S(1)}, bf16[8,128,256]{2,1,0:T(8,128)(2,1)S(1)}, u32[]{:S(2)}, u32[]{:S(2)}) collective-permute-start(bf16[8,128,256]{2,1,0:T(8,128)(2,1)S(1)} %constant_dynamic-update-slice_fusion.right), channel_id=1, source_target_pairs={{0,3},{1,0},{2,1},{3,2},{4,7},{5,4},{6,5},{7,6},{8,11},{9,8},{10,9... | collective-permute-start | bytes 1572872 | tf_op jit(solution)/shard_map/ppermute | solution.py:47
  25.5 1.8 %collective-permute-start.7 = (bf16[128,256]{1,0:T(8,128)(2,1)S(1)}, bf16[128,256]{1,0:T(8,128)(2,1)S(1)}, u32[]{:S(2)}, u32[]{:S(2)}) collective-permute-start(bf16[128,256]{1,0:T(8,128)(2,1)S(1)} %copy-done.2), channel_id=1, source_target_pairs={{0,64},{1,65},{2,66},{3,67},{4,68},{5,69},{6,70},{7,71},{8,72},{9,... | collective-permute-start | bytes 196616 | tf_op jit(solution)/shard_map/ppermute | solution.py:47
  27.2 1.8 %collective-permute-start.6 = (bf16[128,256]{1,0:T(8,128)(2,1)S(1)}, bf16[128,256]{1,0:T(8,128)(2,1)S(1)}, u32[]{:S(2)}, u32[]{:S(2)}) collective-permute-start(bf16[128,256]{1,0:T(8,128)(2,1)S(1)} %copy-done.2), channel_id=1, source_target_pairs={{0,128},{1,129},{2,130},{3,131},{4,132},{5,133},{6,134},{7,135},{8... | collective-permute-start | bytes 196616 | tf_op jit(solution)/shard_map/ppermute | solution.py:47
  29.1 2.4 %collective-permute-done.7 = bf16[128,256]{1,0:T(8,128)(2,1)S(1)} collective-permute-done((bf16[128,256]{1,0:T(8,128)(2,1)S(1)}, bf16[128,256]{1,0:T(8,128)(2,1)S(1)}, u32[]{:S(2)}, u32[]{:S(2)}) %collective-permute-start.7) | collective-permute-done | bytes 65568 | tf_op jit(solution)/shard_map/ppermute | solution.py:47
  31.5 1.6 %collective-permute-start.5 = (bf16[128,256]{1,0:T(8,128)(2,1)S(1)}, bf16[128,256]{1,0:T(8,128)(2,1)S(1)}, u32[]{:S(2)}, u32[]{:S(2)}) collective-permute-start(bf16[128,256]{1,0:T(8,128)(2,1)S(1)} %copy-done.2), channel_id=1, source_target_pairs={{0,192},{1,193},{2,194},{3,195},{4,196},{5,197},{6,198},{7,199},{8... | collective-permute-start | bytes 196616 | tf_op jit(solution)/shard_map/ppermute | solution.py:47
  33.1 2.7 %collective-permute-done.5 = bf16[128,256]{1,0:T(8,128)(2,1)S(1)} collective-permute-done((bf16[128,256]{1,0:T(8,128)(2,1)S(1)}, bf16[128,256]{1,0:T(8,128)(2,1)S(1)}, u32[]{:S(2)}, u32[]{:S(2)}) %collective-permute-start.5) | collective-permute-done | bytes 65568 | tf_op jit(solution)/shard_map/ppermute | solution.py:47
  36.6 0.8 collective-permute-done.8.u3
  37.3 1.5 %shard_map.64 = (bf16[8,128,256]{2,1,0:T(8,128)(2,1)S(1)}, bf16[8,128,256]{2,1,0:T(8,128)(2,1)S(1)}, f32[8,128,256]{2,1,0:T(8,128)S(1)}, f32[8,128,256]{2,1,0:T(8,128)S(1)}) custom-call(s32[24]{0:T(128)S(1)} %get-tuple-element.36.first_ref, s32[24]{0:T(128)S(1)} %get-tuple-element.37.second_ref, s32[1]{0:T(128)S(6)} %copy.11.live_ref, ...), custom_call_target="tpu_custom_call" | custom-call | tf_op jit(solution)/shard_map/pallas_call | solution.py:134
  38.9 2.5 %shard_map.65 = (f32[4,128,256]{2,1,0:T(8,128)S(1)}, bf16[4,128,256]{2,1,0:T(8,128)(2,1)S(1)}, bf16[8,128,256]{2,1,0:T(8,128)(2,1)S(1)}, bf16[8,128,256]{2,1,0:T(8,128)(2,1)S(1)}, bf16[8,128,256]{2,1,0:T(8,128)(2,1)S(1)}) custom-call(s32[24]{0:T(128)S(1)} %get-tuple-element.36.first_ref, s32[24]{0:T(128)S(1)} %get-tuple-element.37.second_ref, ...), custom_call_target="tpu_custom_call" | custom-call | tf_op jit(solution)/shard_map/pallas_call | solution.py:134
  41.7 2.1 %collective-permute-start.13 = (bf16[8,128,256]{2,1,0:T(8,128)(2,1)S(1)}, bf16[8,128,256]{2,1,0:T(8,128)(2,1)S(1)}, u32[]{:S(2)}, u32[]{:S(2)}) collective-permute-start(bf16[8,128,256]{2,1,0:T(8,128)(2,1)S(1)} %get-tuple-element.47), channel_id=1, source_target_pairs={{0,1},{1,2},{2,3},{3,0},{4,5},{5,6},{6,7},{7,4},{8,9},{9,10},{10,1... | collective-permute-start | bytes 1572872 | tf_op jit(solution)/shard_map/ppermute | solution.py:47
  44.0 2.0 %collective-permute-start.16 = (bf16[128,256]{1,0:T(8,128)(2,1)S(1)}, bf16[128,256]{1,0:T(8,128)(2,1)S(1)}, u32[]{:S(2)}, u32[]{:S(2)}) collective-permute-start(bf16[128,256]{1,0:T(8,128)(2,1)S(1)} %get-tuple-element.90), channel_id=1, source_target_pairs={{0,64},{1,65},{2,66},{3,67},{4,68},{5,69},{6,70},{7,71},{8,72},{9,... | collective-permute-start | bytes 196616 | tf_op jit(solution)/shard_map/ppermute | solution.py:47
  46.0 1.9 %collective-permute-start.18 = (bf16[128,256]{1,0:T(8,128)(2,1)S(1)}, bf16[128,256]{1,0:T(8,128)(2,1)S(1)}, u32[]{:S(2)}, u32[]{:S(2)}) collective-permute-start(bf16[128,256]{1,0:T(8,128)(2,1)S(1)} %get-tuple-element.91), channel_id=1, source_target_pairs={{0,192},{1,193},{2,194},{3,195},{4,196},{5,197},{6,198},{7,199},{8... | collective-permute-start | bytes 196616 | tf_op jit(solution)/shard_map/ppermute | solution.py:47
  47.9 3.1 %collective-permute-done.16 = bf16[128,256]{1,0:T(8,128)(2,1)S(1)} collective-permute-done((bf16[128,256]{1,0:T(8,128)(2,1)S(1)}, bf16[128,256]{1,0:T(8,128)(2,1)S(1)}, u32[]{:S(2)}, u32[]{:S(2)}) %collective-permute-start.16) | collective-permute-done | bytes 65568 | tf_op jit(solution)/shard_map/ppermute | solution.py:47
  51.0 0.6 collective-permute-done.18
  51.7 4.6 %collective-permute-done.17 = bf16[128,256]{1,0:T(8,128)(2,1)S(1)} collective-permute-done((bf16[128,256]{1,0:T(8,128)(2,1)S(1)}, bf16[128,256]{1,0:T(8,128)(2,1)S(1)}, u32[]{:S(2)}, u32[]{:S(2)}) %collective-permute-start.17) | collective-permute-done | bytes 65568 | tf_op jit(solution)/shard_map/ppermute | solution.py:47
  56.3 1.6 %collective-permute-done.14 = bf16[8,128,256]{2,1,0:T(8,128)(2,1)S(1)} collective-permute-done((bf16[8,128,256]{2,1,0:T(8,128)(2,1)S(1)}, bf16[8,128,256]{2,1,0:T(8,128)(2,1)S(1)}, u32[]{:S(2)}, u32[]{:S(2)}) %collective-permute-start.14) | collective-permute-done | bytes 524320 | tf_op jit(solution)/shard_map/ppermute | solution.py:47
  58.3 0.6 collective-permute-start.19
  58.9 1.2 collective-permute-start.21
  60.1 0.8 collective-permute-start.20
  60.9 3.9 %collective-permute-done.19 = bf16[2,128,256]{2,1,0:T(8,128)(2,1)S(1)} collective-permute-done((bf16[2,128,256]{2,1,0:T(8,128)(2,1)S(1)}, bf16[2,128,256]{2,1,0:T(8,128)(2,1)S(1)}, u32[]{:S(2)}, u32[]{:S(2)}) %collective-permute-start.19) | collective-permute-done | bytes 131104 | tf_op jit(solution)/shard_map/ppermute | solution.py:47
  64.9 1.4 %collective-permute-done.20 = bf16[2,128,256]{2,1,0:T(8,128)(2,1)S(1)} collective-permute-done((bf16[2,128,256]{2,1,0:T(8,128)(2,1)S(1)}, bf16[2,128,256]{2,1,0:T(8,128)(2,1)S(1)}, u32[]{:S(2)}, u32[]{:S(2)}) %collective-permute-start.20) | collective-permute-done | bytes 131104 | tf_op jit(solution)/shard_map/ppermute | solution.py:47
  66.5 7.2 %collective-permute-start.22 = (bf16[2,128,256]{2,1,0:T(8,128)(2,1)S(1)}, bf16[2,128,256]{2,1,0:T(8,128)(2,1)S(1)}, u32[]{:S(2)}, u32[]{:S(2)}) collective-permute-start(bf16[2,128,256]{2,1,0:T(8,128)(2,1)S(1)} %pad_maximum_fusion.4), channel_id=1, source_target_pairs={{0,4},{1,5},{2,6},{3,7},{4,0},{5,1},{6,2},{7,3},{8,12},{9,13},{10,... | collective-permute-start | bytes 393224 | tf_op jit(solution)/shard_map/ppermute | solution.py:47
  73.7 3.6 %collective-permute-done.22 = bf16[2,128,256]{2,1,0:T(8,128)(2,1)S(1)} collective-permute-done((bf16[2,128,256]{2,1,0:T(8,128)(2,1)S(1)}, bf16[2,128,256]{2,1,0:T(8,128)(2,1)S(1)}, u32[]{:S(2)}, u32[]{:S(2)}) %collective-permute-start.22) | collective-permute-done | bytes 131104 | tf_op jit(solution)/shard_map/ppermute | solution.py:47
  77.5 2.2 %collective-permute-start.24 = (bf16[2,128,256]{2,1,0:T(8,128)(2,1)S(1)}, bf16[2,128,256]{2,1,0:T(8,128)(2,1)S(1)}, u32[]{:S(2)}, u32[]{:S(2)}) collective-permute-start(bf16[2,128,256]{2,1,0:T(8,128)(2,1)S(1)} %fusion.1), channel_id=1, source_target_pairs={{0,16},{1,17},{2,18},{3,19},{4,20},{5,21},{6,22},{7,23},{8,24},{9,... | collective-permute-start | bytes 393224 | tf_op jit(solution)/shard_map/ppermute | solution.py:47
  79.7 1.0 collective-permute-start.23
  80.7 4.3 %collective-permute-done.25 = bf16[2,128,256]{2,1,0:T(8,128)(2,1)S(1)} collective-permute-done((bf16[2,128,256]{2,1,0:T(8,128)(2,1)S(1)}, bf16[2,128,256]{2,1,0:T(8,128)(2,1)S(1)}, u32[]{:S(2)}, u32[]{:S(2)}) %collective-permute-start.25) | collective-permute-done | bytes 131104 | tf_op jit(solution)/shard_map/ppermute | solution.py:47
  85.0 0.9 collective-permute-done.23
  86.0 1.3 collective-permute-start.33
  87.3 3.0 %collective-permute-start.32 = (bf16[8,128,256]{2,1,0:T(8,128)(2,1)S(1)}, bf16[8,128,256]{2,1,0:T(8,128)(2,1)S(1)}, u32[]{:S(2)}, u32[]{:S(2)}) collective-permute-start(bf16[8,128,256]{2,1,0:T(8,128)(2,1)S(1)} %pad_maximum_fusion.right), channel_id=1, source_target_pairs={{0,2},{1,3},{2,0},{3,1},{4,6},{5,7},{6,4},{7,5},{8,10},{9,11},{10,... | collective-permute-start | bytes 1572872 | tf_op jit(solution)/shard_map/ppermute | solution.py:47
  90.7 0.9 collective-permute-start.29
  91.6 1.6 %collective-permute-start.28 = (bf16[128,256]{1,0:T(8,128)(2,1)S(1)}, bf16[128,256]{1,0:T(8,128)(2,1)S(1)}, u32[]{:S(2)}, u32[]{:S(2)}) collective-permute-start(bf16[128,256]{1,0:T(8,128)(2,1)S(1)} %slice_bitcast_fusion.7), channel_id=1, source_target_pairs={{0,128},{1,129},{2,130},{3,131},{4,132},{5,133},{6,134},{7,135},{8... | collective-permute-start | bytes 196616 | tf_op jit(solution)/shard_map/ppermute | solution.py:47
  93.2 3.6 %collective-permute-done.29 = bf16[128,256]{1,0:T(8,128)(2,1)S(1)} collective-permute-done((bf16[128,256]{1,0:T(8,128)(2,1)S(1)}, bf16[128,256]{1,0:T(8,128)(2,1)S(1)}, u32[]{:S(2)}, u32[]{:S(2)}) %collective-permute-start.29) | collective-permute-done | bytes 65568 | tf_op jit(solution)/shard_map/ppermute | solution.py:47
  96.9 1.2 collective-permute-done.28
  98.1 2.9 %collective-permute-done.27 = bf16[128,256]{1,0:T(8,128)(2,1)S(1)} collective-permute-done((bf16[128,256]{1,0:T(8,128)(2,1)S(1)}, bf16[128,256]{1,0:T(8,128)(2,1)S(1)}, u32[]{:S(2)}, u32[]{:S(2)}) %collective-permute-start.27) | collective-permute-done | bytes 65568 | tf_op jit(solution)/shard_map/ppermute | solution.py:47
  101.2 1.4 %collective-permute-done.30.u3 = bf16[3,128,256]{2,1,0:T(8,128)(2,1)S(1)} collective-permute-done((bf16[3,128,256]{2,1,0:T(8,128)(2,1)S(1)}, bf16[3,128,256]{2,1,0:T(8,128)(2,1)S(1)}, u32[]{:S(2)}, u32[]{:S(2)}) %collective-permute-start.30) | collective-permute-done | bytes 196640 | tf_op jit(solution)/shard_map/ppermute | solution.py:47
  102.6 1.5 %shard_map.66 = (bf16[8,128,256]{2,1,0:T(8,128)(2,1)S(1)}, bf16[8,128,256]{2,1,0:T(8,128)(2,1)S(1)}, f32[8,128,256]{2,1,0:T(8,128)S(1)}, f32[8,128,256]{2,1,0:T(8,128)S(1)}) custom-call(s32[24]{0:T(128)S(1)} %get-tuple-element.36.first_ref, s32[24]{0:T(128)S(1)} %get-tuple-element.37.second_ref, s32[1]{0:T(128)S(6)} %copy.11.live_ref, ...), custom_call_target="tpu_custom_call" | custom-call | tf_op jit(solution)/shard_map/pallas_call | solution.py:134
  104.2 2.5 %shard_map.67 = (f32[4,128,256]{2,1,0:T(8,128)S(1)}, bf16[4,128,256]{2,1,0:T(8,128)(2,1)S(1)}, bf16[8,128,256]{2,1,0:T(8,128)(2,1)S(1)}, bf16[8,128,256]{2,1,0:T(8,128)(2,1)S(1)}, bf16[8,128,256]{2,1,0:T(8,128)(2,1)S(1)}) custom-call(s32[24]{0:T(128)S(1)} %get-tuple-element.36.first_ref, s32[24]{0:T(128)S(1)} %get-tuple-element.37.second_ref, ...), custom_call_target="tpu_custom_call" | custom-call | tf_op jit(solution)/shard_map/pallas_call | solution.py:134
  106.9 1.6 %collective-permute-start.34 = (bf16[8,128,256]{2,1,0:T(8,128)(2,1)S(1)}, bf16[8,128,256]{2,1,0:T(8,128)(2,1)S(1)}, u32[]{:S(2)}, u32[]{:S(2)}) collective-permute-start(bf16[8,128,256]{2,1,0:T(8,128)(2,1)S(1)} %get-tuple-element.60), channel_id=1, source_target_pairs={{0,2},{1,3},{2,0},{3,1},{4,6},{5,7},{6,4},{7,5},{8,10},{9,11},{10,... | collective-permute-start | bytes 1572872 | tf_op jit(solution)/shard_map/ppermute | solution.py:47
  108.6 0.5 collective-permute-start.35
  109.0 1.5 %collective-permute-start.36 = (bf16[8,128,256]{2,1,0:T(8,128)(2,1)S(1)}, bf16[8,128,256]{2,1,0:T(8,128)(2,1)S(1)}, u32[]{:S(2)}, u32[]{:S(2)}) collective-permute-start(bf16[8,128,256]{2,1,0:T(8,128)(2,1)S(1)} %get-tuple-element.62), channel_id=1, source_target_pairs={{0,3},{1,0},{2,1},{3,2},{4,7},{5,4},{6,5},{7,6},{8,11},{9,8},{10,9... | collective-permute-start | bytes 1572872 | tf_op jit(solution)/shard_map/ppermute | solution.py:47
  110.7 1.8 %collective-permute-start.38 = (bf16[128,256]{1,0:T(8,128)(2,1)S(1)}, bf16[128,256]{1,0:T(8,128)(2,1)S(1)}, u32[]{:S(2)}, u32[]{:S(2)}) collective-permute-start(bf16[128,256]{1,0:T(8,128)(2,1)S(1)} %get-tuple-element.83), channel_id=1, source_target_pairs={{0,64},{1,65},{2,66},{3,67},{4,68},{5,69},{6,70},{7,71},{8,72},{9,... | collective-permute-start | bytes 196616 | tf_op jit(solution)/shard_map/ppermute | solution.py:47
  112.5 2.1 %collective-permute-start.40 = (bf16[128,256]{1,0:T(8,128)(2,1)S(1)}, bf16[128,256]{1,0:T(8,128)(2,1)S(1)}, u32[]{:S(2)}, u32[]{:S(2)}) collective-permute-start(bf16[128,256]{1,0:T(8,128)(2,1)S(1)} %get-tuple-element.84), channel_id=1, source_target_pairs={{0,192},{1,193},{2,194},{3,195},{4,196},{5,197},{6,198},{7,199},{8... | collective-permute-start | bytes 196616 | tf_op jit(solution)/shard_map/ppermute | solution.py:47
  114.6 2.4 %collective-permute-done.38 = bf16[128,256]{1,0:T(8,128)(2,1)S(1)} collective-permute-done((bf16[128,256]{1,0:T(8,128)(2,1)S(1)}, bf16[128,256]{1,0:T(8,128)(2,1)S(1)}, u32[]{:S(2)}, u32[]{:S(2)}) %collective-permute-start.38) | collective-permute-done | bytes 65568 | tf_op jit(solution)/shard_map/ppermute | solution.py:47
  117.0 0.4 collective-permute-done.40
  117.4 4.9 %collective-permute-done.39 = bf16[128,256]{1,0:T(8,128)(2,1)S(1)} collective-permute-done((bf16[128,256]{1,0:T(8,128)(2,1)S(1)}, bf16[128,256]{1,0:T(8,128)(2,1)S(1)}, u32[]{:S(2)}, u32[]{:S(2)}) %collective-permute-start.39) | collective-permute-done | bytes 65568 | tf_op jit(solution)/shard_map/ppermute | solution.py:47
  122.4 1.0 collective-permute-done.35
  123.7 0.6 collective-permute-start.41
  124.4 2.0 %collective-permute-start.43 = (bf16[2,128,256]{2,1,0:T(8,128)(2,1)S(1)}, bf16[2,128,256]{2,1,0:T(8,128)(2,1)S(1)}, u32[]{:S(2)}, u32[]{:S(2)}) collective-permute-start(bf16[2,128,256]{2,1,0:T(8,128)(2,1)S(1)} %get-tuple-element.78), channel_id=1, source_target_pairs={{0,24},{1,25},{2,26},{3,27},{4,28},{5,29},{6,30},{7,31},{8,0},{9,1... | collective-permute-start | bytes 393224 | tf_op jit(solution)/shard_map/ppermute | solution.py:47
  126.4 3.9 %collective-permute-done.41 = bf16[2,128,256]{2,1,0:T(8,128)(2,1)S(1)} collective-permute-done((bf16[2,128,256]{2,1,0:T(8,128)(2,1)S(1)}, bf16[2,128,256]{2,1,0:T(8,128)(2,1)S(1)}, u32[]{:S(2)}, u32[]{:S(2)}) %collective-permute-start.41) | collective-permute-done | bytes 131104 | tf_op jit(solution)/shard_map/ppermute | solution.py:47
  130.6 1.9 %collective-permute-done.42 = bf16[2,128,256]{2,1,0:T(8,128)(2,1)S(1)} collective-permute-done((bf16[2,128,256]{2,1,0:T(8,128)(2,1)S(1)}, bf16[2,128,256]{2,1,0:T(8,128)(2,1)S(1)}, u32[]{:S(2)}, u32[]{:S(2)}) %collective-permute-start.42) | collective-permute-done | bytes 131104 | tf_op jit(solution)/shard_map/ppermute | solution.py:47
  132.6 6.0 %collective-permute-start.44 = (bf16[128,256]{1,0:T(8,128)(2,1)S(1)}, bf16[128,256]{1,0:T(8,128)(2,1)S(1)}, u32[]{:S(2)}, u32[]{:S(2)}) collective-permute-start(bf16[128,256]{1,0:T(8,128)(2,1)S(1)} %fusion.10), channel_id=1, source_target_pairs={{0,4},{1,5},{2,6},{3,7},{4,0},{5,1},{6,2},{7,3},{8,12},{9,13},{10,... | collective-permute-start | bytes 196616 | tf_op jit(solution)/shard_map/ppermute | solution.py:47
  138.6 2.3 %collective-permute-done.44 = bf16[128,256]{1,0:T(8,128)(2,1)S(1)} collective-permute-done((bf16[128,256]{1,0:T(8,128)(2,1)S(1)}, bf16[128,256]{1,0:T(8,128)(2,1)S(1)}, u32[]{:S(2)}, u32[]{:S(2)}) %collective-permute-start.44) | collective-permute-done | bytes 65568 | tf_op jit(solution)/shard_map/ppermute | solution.py:47
  140.9 0.7 fusion.9
  (73 shorter events, 3.2 us)
Async XLA Ops:
  0.0 9.9 %collective-permute-start = (bf16[128,256]{1,0:T(8,128)(2,1)}, bf16[128,256]{1,0:T(8,128)(2,1)S(1)}, u32[]{:S(2)}, u32[]{:S(2)}) collective-permute-start(bf16[128,256]{1,0:T(8,128)(2,1)} %param.6), channel_id=1, source_target_pairs={{0,4},{1,5},{2,6},{3,7},{4,0},{5,1},{6,2},{7,3},{8,12},{9,13},{10,... | collective-permute-start | bytes 196616 | tf_op jit(solution)/shard_map/ppermute | solution.py:47
  7.2 2.8 %copy-start.2 = (bf16[128,256]{1,0:T(8,128)(2,1)S(1)}, bf16[128,256]{1,0:T(8,128)(2,1)}, u32[]{:S(2)}) copy-start(bf16[128,256]{1,0:T(8,128)(2,1)} %param.6) | copy-start | bytes 196612
  8.1 0.7 copy-start.3
  8.1 0.7 copy-start.4
  9.9 27.4 %copy-start = (bf16[24,128,128]{2,1,0:T(8,128)(2,1)S(1)}, bf16[24,128,128]{2,1,0:T(8,128)(2,1)}, u32[]{:S(2)}) copy-start(bf16[24,128,128]{2,1,0:T(8,128)(2,1)} %wins.7) | copy-start | bytes 2359300
  9.9 27.4 %copy-start.1 = (bf16[24,128,128]{2,1,0:T(8,128)(2,1)S(1)}, bf16[24,128,128]{2,1,0:T(8,128)(2,1)}, u32[]{:S(2)}) copy-start(bf16[24,128,128]{2,1,0:T(8,128)(2,1)} %losses.7) | copy-start | bytes 2359300
  10.0 8.1 %collective-permute-start.2 = (bf16[2,128,256]{2,1,0:T(8,128)(2,1)S(1)}, bf16[2,128,256]{2,1,0:T(8,128)(2,1)S(1)}, u32[]{:S(2)}, u32[]{:S(2)}) collective-permute-start(bf16[2,128,256]{2,1,0:T(8,128)(2,1)S(1)} %pad_maximum_fusion.3), channel_id=1, source_target_pairs={{0,16},{1,17},{2,18},{3,19},{4,20},{5,21},{6,22},{7,23},{8,24},{9,... | collective-permute-start | bytes 393224 | tf_op jit(solution)/shard_map/ppermute | solution.py:47
  13.1 5.0 %collective-permute-start.1 = (bf16[2,128,256]{2,1,0:T(8,128)(2,1)S(1)}, bf16[2,128,256]{2,1,0:T(8,128)(2,1)S(1)}, u32[]{:S(2)}, u32[]{:S(2)}) collective-permute-start(bf16[2,128,256]{2,1,0:T(8,128)(2,1)S(1)} %pad_maximum_fusion.3), channel_id=1, source_target_pairs={{0,24},{1,25},{2,26},{3,27},{4,28},{5,29},{6,30},{7,31},{8,0},{9,1... | collective-permute-start | bytes 393224 | tf_op jit(solution)/shard_map/ppermute | solution.py:47
  14.2 6.2 %collective-permute-start.3 = (bf16[2,128,256]{2,1,0:T(8,128)(2,1)S(1)}, bf16[2,128,256]{2,1,0:T(8,128)(2,1)S(1)}, u32[]{:S(2)}, u32[]{:S(2)}) collective-permute-start(bf16[2,128,256]{2,1,0:T(8,128)(2,1)S(1)} %pad_maximum_fusion.3), channel_id=1, source_target_pairs={{0,8},{1,9},{2,10},{3,11},{4,12},{5,13},{6,14},{7,15},{8,16},{9,17... | collective-permute-start | bytes 393224 | tf_op jit(solution)/shard_map/ppermute | solution.py:47
  15.1 5.3 %collective-permute-start.4 = (bf16[128,256]{1,0:T(8,128)(2,1)S(1)}, bf16[128,256]{1,0:T(8,128)(2,1)S(1)}, u32[]{:S(2)}, u32[]{:S(2)}) collective-permute-start(bf16[128,256]{1,0:T(8,128)(2,1)S(1)} %copy-done.2), channel_id=1, source_target_pairs={{0,32},{1,33},{2,34},{3,35},{4,36},{5,37},{6,38},{7,39},{8,40},{9,... | collective-permute-start | bytes 196616 | tf_op jit(solution)/shard_map/ppermute | solution.py:47
  20.4 18.4 %collective-permute-start.11 = (bf16[8,128,256]{2,1,0:T(8,128)(2,1)S(1)}, bf16[8,128,256]{2,1,0:T(8,128)(2,1)S(1)}, u32[]{:S(2)}, u32[]{:S(2)}) collective-permute-start(bf16[8,128,256]{2,1,0:T(8,128)(2,1)S(1)} %constant_dynamic-update-slice_fusion.right), channel_id=1, source_target_pairs={{0,1},{1,2},{2,3},{3,0},{4,5},{5,6},{6,7},{7,4},{8,9},{9,10},{10,1... | collective-permute-start | bytes 1572872 | tf_op jit(solution)/shard_map/ppermute | solution.py:47
  22.1 16.8 %collective-permute-start.10 = (bf16[8,128,256]{2,1,0:T(8,128)(2,1)S(1)}, bf16[8,128,256]{2,1,0:T(8,128)(2,1)S(1)}, u32[]{:S(2)}, u32[]{:S(2)}) collective-permute-start(bf16[8,128,256]{2,1,0:T(8,128)(2,1)S(1)} %constant_dynamic-update-slice_fusion.right), channel_id=1, source_target_pairs={{0,2},{1,3},{2,0},{3,1},{4,6},{5,7},{6,4},{7,5},{8,10},{9,11},{10,... | collective-permute-start | bytes 1572872 | tf_op jit(solution)/shard_map/ppermute | solution.py:47
  23.0 15.9 %collective-permute-start.9 = (bf16[8,128,256]{2,1,0:T(8,128)(2,1)S(1)}, bf16[8,128,256]{2,1,0:T(8,128)(2,1)S(1)}, u32[]{:S(2)}, u32[]{:S(2)}) collective-permute-start(bf16[8,128,256]{2,1,0:T(8,128)(2,1)S(1)} %constant_dynamic-update-slice_fusion.right), channel_id=1, source_target_pairs={{0,3},{1,0},{2,1},{3,2},{4,7},{5,4},{6,5},{7,6},{8,11},{9,8},{10,9... | collective-permute-start | bytes 1572872 | tf_op jit(solution)/shard_map/ppermute | solution.py:47
  25.5 6.1 %collective-permute-start.7 = (bf16[128,256]{1,0:T(8,128)(2,1)S(1)}, bf16[128,256]{1,0:T(8,128)(2,1)S(1)}, u32[]{:S(2)}, u32[]{:S(2)}) collective-permute-start(bf16[128,256]{1,0:T(8,128)(2,1)S(1)} %copy-done.2), channel_id=1, source_target_pairs={{0,64},{1,65},{2,66},{3,67},{4,68},{5,69},{6,70},{7,71},{8,72},{9,... | collective-permute-start | bytes 196616 | tf_op jit(solution)/shard_map/ppermute | solution.py:47
  27.2 5.9 %collective-permute-start.6 = (bf16[128,256]{1,0:T(8,128)(2,1)S(1)}, bf16[128,256]{1,0:T(8,128)(2,1)S(1)}, u32[]{:S(2)}, u32[]{:S(2)}) collective-permute-start(bf16[128,256]{1,0:T(8,128)(2,1)S(1)} %copy-done.2), channel_id=1, source_target_pairs={{0,128},{1,129},{2,130},{3,131},{4,132},{5,133},{6,134},{7,135},{8... | collective-permute-start | bytes 196616 | tf_op jit(solution)/shard_map/ppermute | solution.py:47
  31.5 4.3 %collective-permute-start.5 = (bf16[128,256]{1,0:T(8,128)(2,1)S(1)}, bf16[128,256]{1,0:T(8,128)(2,1)S(1)}, u32[]{:S(2)}, u32[]{:S(2)}) collective-permute-start(bf16[128,256]{1,0:T(8,128)(2,1)S(1)} %copy-done.2), channel_id=1, source_target_pairs={{0,192},{1,193},{2,194},{3,195},{4,196},{5,197},{6,198},{7,199},{8... | collective-permute-start | bytes 196616 | tf_op jit(solution)/shard_map/ppermute | solution.py:47
  35.8 1.5 %collective-permute-start.8 = (bf16[3,128,256]{2,1,0:T(8,128)(2,1)S(1)}, bf16[3,128,256]{2,1,0:T(8,128)(2,1)S(1)}, u32[]{:S(2)}, u32[]{:S(2)}) collective-permute-start(bf16[3,128,256]{2,1,0:T(8,128)(2,1)S(1)} %pad_maximum_fusion.1.u1), channel_id=1, source_target_pairs={{0,32},{1,33},{2,34},{3,35},{4,36},{5,37},{6,38},{7,39},{8,40},{9,... | collective-permute-start | bytes 589832 | tf_op jit(solution)/shard_map/ppermute | solution.py:47
  41.4 2.5 %collective-permute-start.15 = (bf16[4,128,256]{2,1,0:T(8,128)(2,1)S(1)}, bf16[4,128,256]{2,1,0:T(8,128)(2,1)S(1)}, u32[]{:S(2)}, u32[]{:S(2)}) collective-permute-start(bf16[4,128,256]{2,1,0:T(8,128)(2,1)S(1)} %get-tuple-element.50), channel_id=1, source_target_pairs={{0,32},{1,33},{2,34},{3,35},{4,36},{5,37},{6,38},{7,39},{8,40},{9,... | collective-permute-start | bytes 786440 | tf_op jit(solution)/shard_map/ppermute | solution.py:47
  41.7 14.7 %collective-permute-start.12 = (bf16[8,128,256]{2,1,0:T(8,128)(2,1)S(1)}, bf16[8,128,256]{2,1,0:T(8,128)(2,1)S(1)}, u32[]{:S(2)}, u32[]{:S(2)}) collective-permute-start(bf16[8,128,256]{2,1,0:T(8,128)(2,1)S(1)} %get-tuple-element.46), channel_id=1, source_target_pairs={{0,2},{1,3},{2,0},{3,1},{4,6},{5,7},{6,4},{7,5},{8,10},{9,11},{10,... | collective-permute-start | bytes 1572872 | tf_op jit(solution)/shard_map/ppermute | solution.py:47
  41.7 14.7 %collective-permute-start.13 = (bf16[8,128,256]{2,1,0:T(8,128)(2,1)S(1)}, bf16[8,128,256]{2,1,0:T(8,128)(2,1)S(1)}, u32[]{:S(2)}, u32[]{:S(2)}) collective-permute-start(bf16[8,128,256]{2,1,0:T(8,128)(2,1)S(1)} %get-tuple-element.47), channel_id=1, source_target_pairs={{0,1},{1,2},{2,3},{3,0},{4,5},{5,6},{6,7},{7,4},{8,9},{9,10},{10,1... | collective-permute-start | bytes 1572872 | tf_op jit(solution)/shard_map/ppermute | solution.py:47
  43.8 14.2 %collective-permute-start.14 = (bf16[8,128,256]{2,1,0:T(8,128)(2,1)S(1)}, bf16[8,128,256]{2,1,0:T(8,128)(2,1)S(1)}, u32[]{:S(2)}, u32[]{:S(2)}) collective-permute-start(bf16[8,128,256]{2,1,0:T(8,128)(2,1)S(1)} %get-tuple-element.48), channel_id=1, source_target_pairs={{0,3},{1,0},{2,1},{3,2},{4,7},{5,4},{6,5},{7,6},{8,11},{9,8},{10,9... | collective-permute-start | bytes 1572872 | tf_op jit(solution)/shard_map/ppermute | solution.py:47
  44.0 7.0 %collective-permute-start.16 = (bf16[128,256]{1,0:T(8,128)(2,1)S(1)}, bf16[128,256]{1,0:T(8,128)(2,1)S(1)}, u32[]{:S(2)}, u32[]{:S(2)}) collective-permute-start(bf16[128,256]{1,0:T(8,128)(2,1)S(1)} %get-tuple-element.90), channel_id=1, source_target_pairs={{0,64},{1,65},{2,66},{3,67},{4,68},{5,69},{6,70},{7,71},{8,72},{9,... | collective-permute-start | bytes 196616 | tf_op jit(solution)/shard_map/ppermute | solution.py:47
  46.0 5.7 %collective-permute-start.18 = (bf16[128,256]{1,0:T(8,128)(2,1)S(1)}, bf16[128,256]{1,0:T(8,128)(2,1)S(1)}, u32[]{:S(2)}, u32[]{:S(2)}) collective-permute-start(bf16[128,256]{1,0:T(8,128)(2,1)S(1)} %get-tuple-element.91), channel_id=1, source_target_pairs={{0,192},{1,193},{2,194},{3,195},{4,196},{5,197},{6,198},{7,199},{8... | collective-permute-start | bytes 196616 | tf_op jit(solution)/shard_map/ppermute | solution.py:47
  51.0 5.3 %collective-permute-start.17 = (bf16[128,256]{1,0:T(8,128)(2,1)S(1)}, bf16[128,256]{1,0:T(8,128)(2,1)S(1)}, u32[]{:S(2)}, u32[]{:S(2)}) collective-permute-start(bf16[128,256]{1,0:T(8,128)(2,1)S(1)} %get-tuple-element.92), channel_id=1, source_target_pairs={{0,128},{1,129},{2,130},{3,131},{4,132},{5,133},{6,134},{7,135},{8... | collective-permute-start | bytes 196616 | tf_op jit(solution)/shard_map/ppermute | solution.py:47
  58.3 6.6 %collective-permute-start.19 = (bf16[2,128,256]{2,1,0:T(8,128)(2,1)S(1)}, bf16[2,128,256]{2,1,0:T(8,128)(2,1)S(1)}, u32[]{:S(2)}, u32[]{:S(2)}) collective-permute-start(bf16[2,128,256]{2,1,0:T(8,128)(2,1)S(1)} %get-tuple-element.80), channel_id=1, source_target_pairs={{0,16},{1,17},{2,18},{3,19},{4,20},{5,21},{6,22},{7,23},{8,24},{9,... | collective-permute-start | bytes 393224 | tf_op jit(solution)/shard_map/ppermute | solution.py:47
  58.9 5.9 %collective-permute-start.21 = (bf16[2,128,256]{2,1,0:T(8,128)(2,1)S(1)}, bf16[2,128,256]{2,1,0:T(8,128)(2,1)S(1)}, u32[]{:S(2)}, u32[]{:S(2)}) collective-permute-start(bf16[2,128,256]{2,1,0:T(8,128)(2,1)S(1)} %get-tuple-element.81), channel_id=1, source_target_pairs={{0,24},{1,25},{2,26},{3,27},{4,28},{5,29},{6,30},{7,31},{8,0},{9,1... | collective-permute-start | bytes 393224 | tf_op jit(solution)/shard_map/ppermute | solution.py:47
  60.1 6.2 %collective-permute-start.20 = (bf16[2,128,256]{2,1,0:T(8,128)(2,1)S(1)}, bf16[2,128,256]{2,1,0:T(8,128)(2,1)S(1)}, u32[]{:S(2)}, u32[]{:S(2)}) collective-permute-start(bf16[2,128,256]{2,1,0:T(8,128)(2,1)S(1)} %get-tuple-element.82), channel_id=1, source_target_pairs={{0,8},{1,9},{2,10},{3,11},{4,12},{5,13},{6,14},{7,15},{8,16},{9,17... | collective-permute-start | bytes 393224 | tf_op jit(solution)/shard_map/ppermute | solution.py:47
  66.5 10.8 %collective-permute-start.22 = (bf16[2,128,256]{2,1,0:T(8,128)(2,1)S(1)}, bf16[2,128,256]{2,1,0:T(8,128)(2,1)S(1)}, u32[]{:S(2)}, u32[]{:S(2)}) collective-permute-start(bf16[2,128,256]{2,1,0:T(8,128)(2,1)S(1)} %pad_maximum_fusion.4), channel_id=1, source_target_pairs={{0,4},{1,5},{2,6},{3,7},{4,0},{5,1},{6,2},{7,3},{8,12},{9,13},{10,... | collective-permute-start | bytes 393224 | tf_op jit(solution)/shard_map/ppermute | solution.py:47
  77.4 7.7 %collective-permute-start.25 = (bf16[2,128,256]{2,1,0:T(8,128)(2,1)S(1)}, bf16[2,128,256]{2,1,0:T(8,128)(2,1)S(1)}, u32[]{:S(2)}, u32[]{:S(2)}) collective-permute-start(bf16[2,128,256]{2,1,0:T(8,128)(2,1)S(1)} %fusion.1), channel_id=1, source_target_pairs={{0,8},{1,9},{2,10},{3,11},{4,12},{5,13},{6,14},{7,15},{8,16},{9,17... | collective-permute-start | bytes 393224 | tf_op jit(solution)/shard_map/ppermute | solution.py:47
  77.5 7.6 %collective-permute-start.24 = (bf16[2,128,256]{2,1,0:T(8,128)(2,1)S(1)}, bf16[2,128,256]{2,1,0:T(8,128)(2,1)S(1)}, u32[]{:S(2)}, u32[]{:S(2)}) collective-permute-start(bf16[2,128,256]{2,1,0:T(8,128)(2,1)S(1)} %fusion.1), channel_id=1, source_target_pairs={{0,16},{1,17},{2,18},{3,19},{4,20},{5,21},{6,22},{7,23},{8,24},{9,... | collective-permute-start | bytes 393224 | tf_op jit(solution)/shard_map/ppermute | solution.py:47
  79.7 6.2 %collective-permute-start.23 = (bf16[2,128,256]{2,1,0:T(8,128)(2,1)S(1)}, bf16[2,128,256]{2,1,0:T(8,128)(2,1)S(1)}, u32[]{:S(2)}, u32[]{:S(2)}) collective-permute-start(bf16[2,128,256]{2,1,0:T(8,128)(2,1)S(1)} %fusion.1), channel_id=1, source_target_pairs={{0,24},{1,25},{2,26},{3,27},{4,28},{5,29},{6,30},{7,31},{8,0},{9,1... | collective-permute-start | bytes 393224 | tf_op jit(solution)/shard_map/ppermute | solution.py:47
  80.7 5.3 %collective-permute-start.26 = (bf16[128,256]{1,0:T(8,128)(2,1)S(1)}, bf16[128,256]{1,0:T(8,128)(2,1)S(1)}, u32[]{:S(2)}, u32[]{:S(2)}) collective-permute-start(bf16[128,256]{1,0:T(8,128)(2,1)S(1)} %slice_bitcast_fusion.7), channel_id=1, source_target_pairs={{0,32},{1,33},{2,34},{3,35},{4,36},{5,37},{6,38},{7,39},{8,40},{9,... | collective-permute-start | bytes 196616 | tf_op jit(solution)/shard_map/ppermute | solution.py:47
  86.0 18.1 %collective-permute-start.33 = (bf16[8,128,256]{2,1,0:T(8,128)(2,1)S(1)}, bf16[8,128,256]{2,1,0:T(8,128)(2,1)S(1)}, u32[]{:S(2)}, u32[]{:S(2)}) collective-permute-start(bf16[8,128,256]{2,1,0:T(8,128)(2,1)S(1)} %pad_maximum_fusion.right), channel_id=1, source_target_pairs={{0,1},{1,2},{2,3},{3,0},{4,5},{5,6},{6,7},{7,4},{8,9},{9,10},{10,1... | collective-permute-start | bytes 1572872 | tf_op jit(solution)/shard_map/ppermute | solution.py:47
  87.3 16.9 %collective-permute-start.32 = (bf16[8,128,256]{2,1,0:T(8,128)(2,1)S(1)}, bf16[8,128,256]{2,1,0:T(8,128)(2,1)S(1)}, u32[]{:S(2)}, u32[]{:S(2)}) collective-permute-start(bf16[8,128,256]{2,1,0:T(8,128)(2,1)S(1)} %pad_maximum_fusion.right), channel_id=1, source_target_pairs={{0,2},{1,3},{2,0},{3,1},{4,6},{5,7},{6,4},{7,5},{8,10},{9,11},{10,... | collective-permute-start | bytes 1572872 | tf_op jit(solution)/shard_map/ppermute | solution.py:47
  90.3 13.9 %collective-permute-start.31 = (bf16[8,128,256]{2,1,0:T(8,128)(2,1)S(1)}, bf16[8,128,256]{2,1,0:T(8,128)(2,1)S(1)}, u32[]{:S(2)}, u32[]{:S(2)}) collective-permute-start(bf16[8,128,256]{2,1,0:T(8,128)(2,1)S(1)} %pad_maximum_fusion.right), channel_id=1, source_target_pairs={{0,3},{1,0},{2,1},{3,2},{4,7},{5,4},{6,5},{7,6},{8,11},{9,8},{10,9... | collective-permute-start | bytes 1572872 | tf_op jit(solution)/shard_map/ppermute | solution.py:47
  90.7 6.1 %collective-permute-start.29 = (bf16[128,256]{1,0:T(8,128)(2,1)S(1)}, bf16[128,256]{1,0:T(8,128)(2,1)S(1)}, u32[]{:S(2)}, u32[]{:S(2)}) collective-permute-start(bf16[128,256]{1,0:T(8,128)(2,1)S(1)} %slice_bitcast_fusion.7), channel_id=1, source_target_pairs={{0,64},{1,65},{2,66},{3,67},{4,68},{5,69},{6,70},{7,71},{8,72},{9,... | collective-permute-start | bytes 196616 | tf_op jit(solution)/shard_map/ppermute | solution.py:47
  91.6 6.6 %collective-permute-start.28 = (bf16[128,256]{1,0:T(8,128)(2,1)S(1)}, bf16[128,256]{1,0:T(8,128)(2,1)S(1)}, u32[]{:S(2)}, u32[]{:S(2)}) collective-permute-start(bf16[128,256]{1,0:T(8,128)(2,1)S(1)} %slice_bitcast_fusion.7), channel_id=1, source_target_pairs={{0,128},{1,129},{2,130},{3,131},{4,132},{5,133},{6,134},{7,135},{8... | collective-permute-start | bytes 196616 | tf_op jit(solution)/shard_map/ppermute | solution.py:47
  96.8 4.3 %collective-permute-start.27 = (bf16[128,256]{1,0:T(8,128)(2,1)S(1)}, bf16[128,256]{1,0:T(8,128)(2,1)S(1)}, u32[]{:S(2)}, u32[]{:S(2)}) collective-permute-start(bf16[128,256]{1,0:T(8,128)(2,1)S(1)} %slice_bitcast_fusion.7), channel_id=1, source_target_pairs={{0,192},{1,193},{2,194},{3,195},{4,196},{5,197},{6,198},{7,199},{8... | collective-permute-start | bytes 196616 | tf_op jit(solution)/shard_map/ppermute | solution.py:47
  101.1 1.5 %collective-permute-start.30 = (bf16[3,128,256]{2,1,0:T(8,128)(2,1)S(1)}, bf16[3,128,256]{2,1,0:T(8,128)(2,1)S(1)}, u32[]{:S(2)}, u32[]{:S(2)}) collective-permute-start(bf16[3,128,256]{2,1,0:T(8,128)(2,1)S(1)} %pad_maximum_fusion.2.u1), channel_id=1, source_target_pairs={{0,32},{1,33},{2,34},{3,35},{4,36},{5,37},{6,38},{7,39},{8,40},{9,... | collective-permute-start | bytes 589832 | tf_op jit(solution)/shard_map/ppermute | solution.py:47
  106.7 3.9 %collective-permute-start.37 = (bf16[4,128,256]{2,1,0:T(8,128)(2,1)S(1)}, bf16[4,128,256]{2,1,0:T(8,128)(2,1)S(1)}, u32[]{:S(2)}, u32[]{:S(2)}) collective-permute-start(bf16[4,128,256]{2,1,0:T(8,128)(2,1)S(1)} %get-tuple-element.64), channel_id=1, source_target_pairs={{0,32},{1,33},{2,34},{3,35},{4,36},{5,37},{6,38},{7,39},{8,40},{9,... | collective-permute-start | bytes 786440 | tf_op jit(solution)/shard_map/ppermute | solution.py:47
  106.9 15.5 %collective-permute-start.34 = (bf16[8,128,256]{2,1,0:T(8,128)(2,1)S(1)}, bf16[8,128,256]{2,1,0:T(8,128)(2,1)S(1)}, u32[]{:S(2)}, u32[]{:S(2)}) collective-permute-start(bf16[8,128,256]{2,1,0:T(8,128)(2,1)S(1)} %get-tuple-element.60), channel_id=1, source_target_pairs={{0,2},{1,3},{2,0},{3,1},{4,6},{5,7},{6,4},{7,5},{8,10},{9,11},{10,... | collective-permute-start | bytes 1572872 | tf_op jit(solution)/shard_map/ppermute | solution.py:47
  108.6 14.8 %collective-permute-start.35 = (bf16[8,128,256]{2,1,0:T(8,128)(2,1)S(1)}, bf16[8,128,256]{2,1,0:T(8,128)(2,1)S(1)}, u32[]{:S(2)}, u32[]{:S(2)}) collective-permute-start(bf16[8,128,256]{2,1,0:T(8,128)(2,1)S(1)} %get-tuple-element.61), channel_id=1, source_target_pairs={{0,1},{1,2},{2,3},{3,0},{4,5},{5,6},{6,7},{7,4},{8,9},{9,10},{10,1... | collective-permute-start | bytes 1572872 | tf_op jit(solution)/shard_map/ppermute | solution.py:47
  109.0 14.3 %collective-permute-start.36 = (bf16[8,128,256]{2,1,0:T(8,128)(2,1)S(1)}, bf16[8,128,256]{2,1,0:T(8,128)(2,1)S(1)}, u32[]{:S(2)}, u32[]{:S(2)}) collective-permute-start(bf16[8,128,256]{2,1,0:T(8,128)(2,1)S(1)} %get-tuple-element.62), channel_id=1, source_target_pairs={{0,3},{1,0},{2,1},{3,2},{4,7},{5,4},{6,5},{7,6},{8,11},{9,8},{10,9... | collective-permute-start | bytes 1572872 | tf_op jit(solution)/shard_map/ppermute | solution.py:47
  110.7 6.3 %collective-permute-start.38 = (bf16[128,256]{1,0:T(8,128)(2,1)S(1)}, bf16[128,256]{1,0:T(8,128)(2,1)S(1)}, u32[]{:S(2)}, u32[]{:S(2)}) collective-permute-start(bf16[128,256]{1,0:T(8,128)(2,1)S(1)} %get-tuple-element.83), channel_id=1, source_target_pairs={{0,64},{1,65},{2,66},{3,67},{4,68},{5,69},{6,70},{7,71},{8,72},{9,... | collective-permute-start | bytes 196616 | tf_op jit(solution)/shard_map/ppermute | solution.py:47
  112.5 5.0 %collective-permute-start.40 = (bf16[128,256]{1,0:T(8,128)(2,1)S(1)}, bf16[128,256]{1,0:T(8,128)(2,1)S(1)}, u32[]{:S(2)}, u32[]{:S(2)}) collective-permute-start(bf16[128,256]{1,0:T(8,128)(2,1)S(1)} %get-tuple-element.84), channel_id=1, source_target_pairs={{0,192},{1,193},{2,194},{3,195},{4,196},{5,197},{6,198},{7,199},{8... | collective-permute-start | bytes 196616 | tf_op jit(solution)/shard_map/ppermute | solution.py:47
  117.0 5.3 %collective-permute-start.39 = (bf16[128,256]{1,0:T(8,128)(2,1)S(1)}, bf16[128,256]{1,0:T(8,128)(2,1)S(1)}, u32[]{:S(2)}, u32[]{:S(2)}) collective-permute-start(bf16[128,256]{1,0:T(8,128)(2,1)S(1)} %get-tuple-element.85), channel_id=1, source_target_pairs={{0,128},{1,129},{2,130},{3,131},{4,132},{5,133},{6,134},{7,135},{8... | collective-permute-start | bytes 196616 | tf_op jit(solution)/shard_map/ppermute | solution.py:47
  123.7 6.6 %collective-permute-start.41 = (bf16[2,128,256]{2,1,0:T(8,128)(2,1)S(1)}, bf16[2,128,256]{2,1,0:T(8,128)(2,1)S(1)}, u32[]{:S(2)}, u32[]{:S(2)}) collective-permute-start(bf16[2,128,256]{2,1,0:T(8,128)(2,1)S(1)} %get-tuple-element.77), channel_id=1, source_target_pairs={{0,16},{1,17},{2,18},{3,19},{4,20},{5,21},{6,22},{7,23},{8,24},{9,... | collective-permute-start | bytes 393224 | tf_op jit(solution)/shard_map/ppermute | solution.py:47
  124.4 6.3 %collective-permute-start.43 = (bf16[2,128,256]{2,1,0:T(8,128)(2,1)S(1)}, bf16[2,128,256]{2,1,0:T(8,128)(2,1)S(1)}, u32[]{:S(2)}, u32[]{:S(2)}) collective-permute-start(bf16[2,128,256]{2,1,0:T(8,128)(2,1)S(1)} %get-tuple-element.78), channel_id=1, source_target_pairs={{0,24},{1,25},{2,26},{3,27},{4,28},{5,29},{6,30},{7,31},{8,0},{9,1... | collective-permute-start | bytes 393224 | tf_op jit(solution)/shard_map/ppermute | solution.py:47
  126.4 6.2 %collective-permute-start.42 = (bf16[2,128,256]{2,1,0:T(8,128)(2,1)S(1)}, bf16[2,128,256]{2,1,0:T(8,128)(2,1)S(1)}, u32[]{:S(2)}, u32[]{:S(2)}) collective-permute-start(bf16[2,128,256]{2,1,0:T(8,128)(2,1)S(1)} %get-tuple-element.79), channel_id=1, source_target_pairs={{0,8},{1,9},{2,10},{3,11},{4,12},{5,13},{6,14},{7,15},{8,16},{9,17... | collective-permute-start | bytes 393224 | tf_op jit(solution)/shard_map/ppermute | solution.py:47
  132.6 8.3 %collective-permute-start.44 = (bf16[128,256]{1,0:T(8,128)(2,1)S(1)}, bf16[128,256]{1,0:T(8,128)(2,1)S(1)}, u32[]{:S(2)}, u32[]{:S(2)}) collective-permute-start(bf16[128,256]{1,0:T(8,128)(2,1)S(1)} %fusion.10), channel_id=1, source_target_pairs={{0,4},{1,5},{2,6},{3,7},{4,0},{5,1},{6,2},{7,3},{8,12},{9,13},{10,... | collective-permute-start | bytes 196616 | tf_op jit(solution)/shard_map/ppermute | solution.py:47
